TPU v7x, 32 devices: a whole 2x2x4 slice. The times are simulated.
32 devices in a mesh: dp: 2 (over core), fsdp: 16 (over z, y, x).
Axes of the slice: x: 2, y: 2, z: 4, core: 2. Of those that a mesh axis runs over, the one named last changes fastest.
Arguments:
- tokens: bfloat16 [32, 864, 768], P(('dp', 'fsdp')), may hold values from -6 to 6
- actions: float32 [32, 16, 28], P(('dp', 'fsdp')), may hold values from -5 to 5
- noise: float32 [32, 16, 28], P(('dp', 'fsdp')), may hold values from -5 to 5
- timesteps: int32 [32], P(('dp', 'fsdp')), may hold values from 0 to 19
- task_mask: int32 [32, 16], P(('dp', 'fsdp')), may hold values 0 or 1
- goal_flag: int32 [32], P(('dp', 'fsdp')), may hold values from 0 to 1
- act_mask: int32 [32, 28], P(('dp', 'fsdp')), may hold values from 0 to 1, as said below
- groups: int32 [32, 864], P(('dp', 'fsdp')), may hold values from 0 to 11, never falling along the last dimension, each value on 1 to 432 neighbouring positions
- w_qkv: float32 [768, 2304], P(('dp', 'fsdp')), may hold values from -0.21875 to 0.21875
- rows_qkv: float32 [768], P(('dp', 'fsdp')), may hold values from 0.0002869898 to 0.0011479591
- cols_qkv: float32 [2304], replicated, may hold values from 9.5663265e-05 to 0.00038265306
- w_out: float32 [768, 768], P(('dp', 'fsdp')), may hold values from -0.875 to 0.875
- rows_out: float32 [768], P(('dp', 'fsdp')), may hold values from 9.5663265e-05 to 0.00038265306
- cols_out: float32 [768], replicated, may hold values from 9.5663265e-05 to 0.00038265306
- w_one: float32 [768, 3072], P(('dp', 'fsdp')), may hold values from -0.21875 to 0.21875
- rows_one: float32 [768], P(('dp', 'fsdp')), may hold values from 0.00038265306 to 0.0015306122
- cols_one: float32 [3072], replicated, may hold values from 9.5663265e-05 to 0.00038265306
- w_two: float32 [3072, 768], P(('dp', 'fsdp')), may hold values from -0.109375 to 0.109375
- rows_two: float32 [3072], P(('dp', 'fsdp')), may hold values from 9.5663265e-05 to 0.00038265306
- cols_two: float32 [768], replicated, may hold values from 0.00038265306 to 0.0015306122
- w_table: float32 [768, 28], P(('dp', 'fsdp')), may hold values from -0.21875 to 0.21875
- var_table: float32 [768, 28], P(('dp', 'fsdp')), may hold values from 1.1708785e-05 to 4.7333386e-05
- small: float32 [768, 6], P(('dp', 'fsdp')), may hold values from -2 to 3
- var_small: float32 [768, 6], P(('dp', 'fsdp')), may hold values from 4.9824615e-07 to 1.9929846e-06
Outputs:
- loss_sum: float32 [], replicated
- count: float32 [], replicated
- clip_rms: float32 [], replicated
- grad_qkv: float32 [768, 2304], P(('dp', 'fsdp'))
- new_rows_qkv: float32 [768], P(('dp', 'fsdp'))
- new_cols_qkv: float32 [2304], replicated
- new_qkv: float32 [768, 2304], P(('dp', 'fsdp'))
- grad_out: float32 [768, 768], P(('dp', 'fsdp'))
- new_rows_out: float32 [768], P(('dp', 'fsdp'))
- new_cols_out: float32 [768], replicated
- new_out: float32 [768, 768], P(('dp', 'fsdp'))
- grad_one: float32 [768, 3072], P(('dp', 'fsdp'))
- new_rows_one: float32 [768], P(('dp', 'fsdp'))
- new_cols_one: float32 [3072], replicated
- new_one: float32 [768, 3072], P(('dp', 'fsdp'))
- grad_two: float32 [3072, 768], P(('dp', 'fsdp'))
- new_rows_two: float32 [3072], P(('dp', 'fsdp'))
- new_cols_two: float32 [768], replicated
- new_two: float32 [3072, 768], P(('dp', 'fsdp'))
- grad_table: float32 [768, 28], P(('dp', 'fsdp'))
- new_var_table: float32 [768, 28], P(('dp', 'fsdp'))
- new_table: float32 [768, 28], P(('dp', 'fsdp'))
- grad_small: float32 [768, 6], P(('dp', 'fsdp'))
- new_var_small: float32 [768, 6], P(('dp', 'fsdp'))
- new_small: float32 [768, 6], P(('dp', 'fsdp'))
Inputs may be any that keep to these rules, and one draw needn't show every extreme that they name: `act_mask`: entry 0 of every item is 1.
All inputs are finite; a program needn't handle non-finite values. No bound on the sum of `task_mask` on one device may be relied on, other than what follows from the above.
Results may differ from a plain program's by a relative error of at most 0.01.
The roundings to bfloat16 on the way count: a program that leaves them out, or rounds other values in their place, can miss the bound.
Values may be sent and summed in bfloat16 or wider, within the bound.
No kernel may reach another device: no remote copies, remote signals or barrier semaphores. Data moves between devices by JAX's collectives and lax.ppermute only.
A program may use at most 192 MiB of HBM per device.

v0:
```python
import math

import jax
import jax.numpy as jnp
from jax import lax
from jax.sharding import PartitionSpec as P

D = 768
HEADS = 12
HDIM = 64
FF = 3072
GOALTOK = 64
ACTW = 28
TSTEPS = 20
STEP = 10


rate_matrix = 0.05
rate_small = 0.3
clip_level = 0.5


def layer_norm(h, gain, bias):
    mean = jnp.mean(h, -1, keepdims=True)
    centered = h - mean
    variance = jnp.mean(centered * centered, -1, keepdims=True)
    return centered * lax.rsqrt(variance + 1e-06) * gain + bias


def condition(actions, noise, tstep, width):
    frac = (tstep.astype(jnp.float32) / TSTEPS + 0.008) / 1.008
    alpha_bar = jnp.cos(frac * (math.pi / 2)) ** 2
    noisy = jnp.sqrt(alpha_bar) * actions + jnp.sqrt(1.0 - alpha_bar) * noise
    half = width // 2
    freq = jnp.exp(jnp.arange(half).astype(jnp.float32) * (-math.log(10000.0) / half))
    angle = tstep.astype(jnp.float32) * freq
    return (noisy, jnp.concatenate([jnp.sin(angle), jnp.cos(angle)]))


def visible_mask(groups, task_mask, goal_flag):
    seq = groups.shape[0]
    task = task_mask.shape[0]
    places = jnp.arange(seq)
    task_pad = jnp.pad(task_mask, (0, seq - task)) * (1 - goal_flag)
    valid = jnp.where(places < task, task_pad, jnp.where(places < task + GOALTOK, goal_flag, 1))
    seen = (groups[None, :] <= groups[:, None]) & (valid[None, :] > 0)
    return seen | (places[:, None] == places[None, :])


def dot_plain(left, right):
    return jnp.dot(left, right, preferred_element_type=jnp.float32)


def dot_right(left, right):
    return lax.dot_general(
        left, right, (((1,), (1,)), ((), ())), preferred_element_type=jnp.float32
    )


def dot_left(left, right):
    return lax.dot_general(
        left, right, (((0,), (0,)), ((), ())), preferred_element_type=jnp.float32
    )


def head_probs(query, key_part, visible):
    scores = dot_right(query, key_part) * HDIM ** (-0.5)
    scores = jnp.where(visible, scores, -1000000000.0)
    return jax.nn.softmax(scores, axis=-1)


def forward_item(weights, item):
    w_qkv, w_out, w_one, w_two, w_table, gains = weights
    tokens, actions, noise, tstep, task_mask, goal_flag, act_mask, groups = item
    seq = tokens.shape[0]
    read = noise.shape[0]
    width = w_qkv.shape[0]
    noisy, temb = condition(actions, noise, tstep, width)
    noisy_low = noisy.astype(jnp.bfloat16)
    embed = dot_right(noisy_low, w_table)
    h_zero = tokens.astype(jnp.float32).at[seq - read :].add(embed + temb)
    normed = layer_norm(h_zero, gains[:, 0], gains[:, 1]).astype(jnp.bfloat16)
    qkv = dot_plain(normed, w_qkv).astype(jnp.bfloat16)
    parts = qkv.reshape(seq, 3, HEADS, HDIM).transpose(1, 2, 0, 3)
    visible = visible_mask(groups, task_mask, goal_flag)

    def forward_one_head(trio):
        probs = head_probs(trio[0], trio[1], visible)
        return dot_plain(probs.astype(jnp.bfloat16), trio[2])

    heads = lax.map(forward_one_head, (parts[0], parts[1], parts[2]))
    attn = heads.transpose(1, 0, 2).reshape(seq, width).astype(jnp.bfloat16)
    resid = h_zero + dot_plain(attn, w_out)
    normed_two = layer_norm(resid, gains[:, 2], gains[:, 3]).astype(jnp.bfloat16)
    up = dot_plain(normed_two, w_one)
    mid = jax.nn.gelu(up).astype(jnp.bfloat16)
    out = resid + dot_plain(mid, w_two)
    last = layer_norm(out[seq - read :], gains[:, 4], gains[:, 5]).astype(jnp.bfloat16)
    diff = dot_plain(last, w_table) - noise
    loss = jnp.sum(act_mask.astype(jnp.float32)[None, :] * diff * diff)
    kept = (noisy_low, h_zero, normed, qkv, attn, resid, normed_two, up, mid, out, last, diff)
    return (loss, kept)


def backward_upper(weights, item, kept, seed):
    w_qkv, w_out, w_one, w_two, w_table, gains = weights
    tokens, actions, noise, tstep, task_mask, goal_flag, act_mask, groups = item
    noisy_low, h_zero, normed, qkv, attn, resid, normed_two, up, mid, out, last, diff = kept
    seq = tokens.shape[0]
    read = noise.shape[0]
    width = w_qkv.shape[0]
    grad_guess = (seed * 2.0 * act_mask.astype(jnp.float32)[None, :] * diff).astype(jnp.bfloat16)
    g_table = dot_left(last, grad_guess)
    _, back_three = jax.vjp(layer_norm, out[seq - read :], gains[:, 4], gains[:, 5])
    d_rows, d_gain_three, d_bias_three = back_three(dot_right(grad_guess, w_table))
    d_out = jnp.zeros((seq, width), jnp.float32).at[seq - read :].set(d_rows)
    d_z = d_out.astype(jnp.bfloat16)
    g_two = dot_left(mid, d_z)
    _, back_gelu = jax.vjp(jax.nn.gelu, up)
    d_up = back_gelu(dot_right(d_z, w_two))[0].astype(jnp.bfloat16)
    g_one = dot_left(normed_two, d_up)
    _, back_two = jax.vjp(layer_norm, resid, gains[:, 2], gains[:, 3])
    d_part, d_gain_two, d_bias_two = back_two(dot_right(d_up, w_one))
    d_resid = d_out + d_part
    d_att = d_resid.astype(jnp.bfloat16)
    g_out = dot_left(attn, d_att)
    nothing = jnp.zeros_like(d_gain_two)
    g_small = jnp.stack(
        [nothing, nothing, d_gain_two, d_bias_two, d_gain_three, d_bias_three], axis=1
    )
    return ((g_out, g_one, g_two, g_table, g_small), (d_resid, d_att))


def backward_lower(weights, item, kept, carried):
    w_qkv, w_out, w_one, w_two, w_table, gains = weights
    tokens, actions, noise, tstep, task_mask, goal_flag, act_mask, groups = item
    noisy_low, h_zero, normed, qkv, attn, resid, normed_two, up, mid, out, last, diff = kept
    d_resid, d_att = carried
    seq = tokens.shape[0]
    read = noise.shape[0]
    width = w_qkv.shape[0]
    scale = HDIM ** (-0.5)
    d_attn = dot_right(d_att, w_out).astype(jnp.bfloat16)
    parts = qkv.reshape(seq, 3, HEADS, HDIM).transpose(1, 2, 0, 3)
    d_heads = d_attn.reshape(seq, HEADS, HDIM).transpose(1, 0, 2)
    visible = visible_mask(groups, task_mask, goal_flag)

    def backward_one_head(group):
        query, key_part, value, d_head = group
        probs = head_probs(query, key_part, visible)
        d_probs = dot_right(d_head, value)
        d_scores = (probs * (d_probs - jnp.sum(d_probs * probs, -1, keepdims=True))).astype(
            jnp.bfloat16
        )
        d_query = dot_plain(d_scores, key_part) * scale
        d_key = dot_left(d_scores, query) * scale
        d_value = dot_left(probs.astype(jnp.bfloat16), d_head)
        return jnp.stack([d_query, d_key, d_value])

    d_parts = lax.map(backward_one_head, (parts[0], parts[1], parts[2], d_heads))
    d_qkv = d_parts.transpose(2, 1, 0, 3).reshape(seq, 3 * width).astype(jnp.bfloat16)
    g_qkv = dot_left(normed, d_qkv)
    _, back_one = jax.vjp(layer_norm, h_zero, gains[:, 0], gains[:, 1])
    d_first, d_gain_one, d_bias_one = back_one(dot_right(d_qkv, w_qkv))
    d_h = d_resid + d_first
    d_embed = d_h[seq - read :].astype(jnp.bfloat16)
    g_table = dot_left(d_embed, noisy_low)
    nothing = jnp.zeros_like(d_gain_one)
    g_small = jnp.stack([d_gain_one, d_bias_one, nothing, nothing, nothing, nothing], axis=1)
    return (g_qkv, g_table, g_small)


def with_gains(parts):
    return tuple(parts[:5]) + (parts[5].astype(jnp.float32),)


def on_device(
    tokens,
    actions,
    noise,
    timesteps,
    task_mask,
    goal_flag,
    act_mask,
    groups,
    w_qkv,
    rows_qkv,
    cols_qkv,
    w_out,
    rows_out,
    cols_out,
    w_one,
    rows_one,
    cols_one,
    w_two,
    rows_two,
    cols_two,
    w_table,
    var_table,
    small,
    var_small,
):
    items = (tokens, actions, noise, timesteps, task_mask, goal_flag, act_mask, groups)
    count = lax.psum(noise.shape[1] * jnp.sum(act_mask.astype(jnp.float32)), ("dp", "fsdp"))
    wire = (
        w_qkv.astype(jnp.bfloat16),
        w_out.astype(jnp.bfloat16),
        w_one.astype(jnp.bfloat16),
        w_two.astype(jnp.bfloat16),
        w_table.astype(jnp.bfloat16),
        small.astype(jnp.bfloat16),
    )
    weights = with_gains(
        (
            lax.all_gather(wire[0], ("dp", "fsdp"), axis=0, tiled=True),
            lax.all_gather(wire[1], ("dp", "fsdp"), axis=0, tiled=True),
            lax.all_gather(wire[2], ("dp", "fsdp"), axis=0, tiled=True),
            lax.all_gather(wire[3], ("dp", "fsdp"), axis=0, tiled=True),
            lax.all_gather(wire[4], ("dp", "fsdp"), axis=0, tiled=True),
            lax.all_gather(wire[5], ("dp", "fsdp"), axis=0, tiled=True),
        )
    )

    def forward_visit(acc, item):
        loss, kept = forward_item(weights, item)
        return (acc + loss, kept)

    loss_local, kept_all = lax.scan(forward_visit, jnp.zeros((), jnp.float32), items)
    weights_back = with_gains(
        (
            lax.all_gather(wire[0], ("dp", "fsdp"), axis=0, tiled=True),
            lax.all_gather(wire[1], ("dp", "fsdp"), axis=0, tiled=True),
            lax.all_gather(wire[2], ("dp", "fsdp"), axis=0, tiled=True),
            lax.all_gather(wire[3], ("dp", "fsdp"), axis=0, tiled=True),
            lax.all_gather(wire[4], ("dp", "fsdp"), axis=0, tiled=True),
            lax.all_gather(wire[5], ("dp", "fsdp"), axis=0, tiled=True),
        )
    )
    seed = 1.0 / count
    upper_zero = tuple((jnp.zeros(weights_back[i].shape, jnp.float32) for i in (1, 2, 3, 4, 5)))

    def upper_visit(acc, pair):
        found, carried = backward_upper(weights_back, pair[0], pair[1], seed)
        return (tuple((a + f for a, f in zip(acc, found))), carried)

    upper, carried_all = lax.scan(upper_visit, upper_zero, (items, kept_all))
    lower_zero = (jnp.zeros(weights_back[0].shape, jnp.float32), upper[3], upper[4])

    def lower_visit(acc, triple):
        found = backward_lower(weights_back, triple[0], triple[1], triple[2])
        return (tuple((a + f for a, f in zip(acc, found))), None)

    lower, _ = lax.scan(lower_visit, lower_zero, (items, kept_all, carried_all))
    g_qkv, g_out, g_one, g_two, g_table, g_small = (
        lax.psum_scatter(lower[0], ("dp", "fsdp"), scatter_dimension=0, tiled=True),
        lax.psum_scatter(upper[0], ("dp", "fsdp"), scatter_dimension=0, tiled=True),
        lax.psum_scatter(upper[1], ("dp", "fsdp"), scatter_dimension=0, tiled=True),
        lax.psum_scatter(upper[2], ("dp", "fsdp"), scatter_dimension=0, tiled=True),
        lax.psum_scatter(lower[1], ("dp", "fsdp"), scatter_dimension=0, tiled=True),
        lax.psum_scatter(lower[2], ("dp", "fsdp"), scatter_dimension=0, tiled=True),
    )
    beta = 1.0 - float(STEP) ** (-0.8)
    mats = (g_qkv, g_out, g_one, g_two)
    squares = tuple((g * g for g in mats))
    rows_new = tuple(
        (
            beta * r + (1.0 - beta) * jnp.sum(sq, 1)
            for r, sq in zip((rows_qkv, rows_out, rows_one, rows_two), squares)
        )
    )
    col_parts = tuple((jnp.sum(sq, 0) for sq in squares))
    row_totals = tuple((jnp.sum(r) for r in rows_new))
    var_table_new = beta * var_table + (1.0 - beta) * g_table * g_table
    var_small_new = beta * var_small + (1.0 - beta) * g_small * g_small
    unit_table = g_table * lax.rsqrt(var_table_new)
    unit_small = g_small * lax.rsqrt(var_small_new)
    vector_squares = jnp.sum(unit_table * unit_table) + jnp.sum(unit_small * unit_small)
    cols_old = (cols_qkv, cols_out, cols_one, cols_two)
    summed = lax.psum(
        (
            col_parts[0],
            col_parts[1],
            col_parts[2],
            col_parts[3],
            row_totals[0],
            row_totals[1],
            row_totals[2],
            row_totals[3],
            loss_local,
        ),
        ("dp", "fsdp"),
    )
    cols_new = tuple((beta * c + (1.0 - beta) * s for c, s in zip(cols_old, summed[0:4])))
    totals = summed[4:8]
    loss_sum = summed[8]
    units = tuple(
        (
            g * lax.rsqrt(r[:, None] * c[None, :] / t)
            for g, r, c, t in zip(mats, rows_new, cols_new, totals)
        )
    )
    local_squares = vector_squares + sum((jnp.sum(u * u) for u in units))
    squares_total = lax.psum(local_squares, ("dp", "fsdp"))
    entries = 4 * D * D + 2 * D * FF + D * ACTW + 6 * D
    clip_rms = jnp.sqrt(squares_total / entries)
    factor = 1.0 / jnp.maximum(1.0, clip_rms / clip_level)
    result = [loss_sum, count, clip_rms]
    for master, grad, rows, cols, unit in zip(
        (w_qkv, w_out, w_one, w_two), mats, rows_new, cols_new, units
    ):
        result += [grad, rows, cols, master - rate_matrix * unit * factor]
    result += [g_table, var_table_new, w_table - rate_matrix * unit_table * factor]
    result += [g_small, var_small_new, small - rate_small * unit_small * factor]
    return tuple(result)


def solution(mesh):
    placed = (
        P(("dp", "fsdp"), None, None),
        P(("dp", "fsdp"), None, None),
        P(("dp", "fsdp"), None, None),
        P(("dp", "fsdp")),
        P(("dp", "fsdp"), None),
        P(("dp", "fsdp")),
        P(("dp", "fsdp"), None),
        P(("dp", "fsdp"), None),
        P(("dp", "fsdp"), None),
        P(("dp", "fsdp")),
        P(),
        P(("dp", "fsdp"), None),
        P(("dp", "fsdp")),
        P(),
        P(("dp", "fsdp"), None),
        P(("dp", "fsdp")),
        P(),
        P(("dp", "fsdp"), None),
        P(("dp", "fsdp")),
        P(),
        P(("dp", "fsdp"), None),
        P(("dp", "fsdp"), None),
        P(("dp", "fsdp"), None),
        P(("dp", "fsdp"), None),
    )
    return jax.shard_map(
        on_device,
        mesh=mesh,
        in_specs=placed,
        out_specs=(
            P(),
            P(),
            P(),
            P(("dp", "fsdp"), None),
            P(("dp", "fsdp")),
            P(),
            P(("dp", "fsdp"), None),
            P(("dp", "fsdp"), None),
            P(("dp", "fsdp")),
            P(),
            P(("dp", "fsdp"), None),
            P(("dp", "fsdp"), None),
            P(("dp", "fsdp")),
            P(),
            P(("dp", "fsdp"), None),
            P(("dp", "fsdp"), None),
            P(("dp", "fsdp")),
            P(),
            P(("dp", "fsdp"), None),
            P(("dp", "fsdp"), None),
            P(("dp", "fsdp"), None),
            P(("dp", "fsdp"), None),
            P(("dp", "fsdp"), None),
            P(("dp", "fsdp"), None),
            P(("dp", "fsdp"), None),
        ),
        check_vma=False,
    )
```

profile of v0, /device:TPU:0, one launch (start us, length us, event | category | flops | bytes accessed | tf_op | source)
XLA Modules:
  0.0 1207.1 jit_solution(4868549140075101482)
XLA Ops:
  17.5 71.5 %all_gather.24 = bf16[768,28]{1,0:T(8,128)(2,1)S(1)} all-gather(bf16[24,28]{1,0:T(8,128)(2,1)S(1)} %convert_element_type.132), channel_id=1, replica_groups=mesh['dp'=2,'fsdp'=16] {'dp','fsdp'}, dimensions={0}, use_global_device_ids=true | all-gather | bytes 44352 | tf_op jit(solution)/shard_map/all_gather | solution.py:219
  92.8 64.0 %all-gather = bf16[32,24,6]{1,2,0:T(8,128)(2,1)S(1)} all-gather(bf16[1,24,6]{1,2,0:T(8,128)(2,1)S(1)} %convert_bitcast_fusion.2), channel_id=1, replica_groups=mesh['dp'=2,'fsdp'=16] {'dp','fsdp'}, dimensions={0}, use_global_device_ids=true | all-gather | bytes 9504 | tf_op jit(solution)/shard_map/all_gather | solution.py:220
  158.5 37.8 %psum.78 = f32[]{:T(128)} all-reduce(f32[]{:T(128)S(6)} %mul_shard_map.3), channel_id=1, replica_groups=mesh['dp'=2,'fsdp'=16] {'dp','fsdp'}, use_global_device_ids=true, to_apply=%region_13.14 | all-reduce | flops 1 | bytes 8 | tf_op jit(solution)/shard_map/psum | solution.py:204
  197.1 7.1 convolution_convert_fusion
  204.2 6.4 copy.75
  210.6 4.3 slice_bitcast_fusion
  226.6 63.8 %while.26 = (s32[]{:T(128)}, bf16[12,864,64]{1,2,0:T(8,128)(2,1)}, bf16[12,864,64]{2,1,0:T(8,128)(2,1)}, bf16[12,864,64]{2,1,0:T(8,128)(2,1)}, bf16[12,864,64]{2...) while((s32[]{:T(128)}, bf16[12,864,64]{1,2,0:T(8,128)(2,1)}, ...), condition=%wide.region_5.6_spmd.clone, body=%wide.region_2.5_spmd.clone.sunk | while | flops 200059200 | bytes 9879509 | solution.py:91
  295.6 11.5 fusion.87
  307.1 10.7 fusion.88
  320.5 12.0 fusion.55
  332.5 4.8 multiply_reduce_fusion.2
  345.2 128.6 %while.27 = (s32[]{:T(128)}, bf16[12,3,864,64]{2,3,1,0:T(8,128)(2,1)}, bf16[12,864,64]{2,1,0:T(8,128)(2,1)}, bf16[12,864,64]{2,1,0:T(8,128)(2,1)}, bf16[12,864,6...) while((s32[]{:T(128)}, ...), condition=%wide.region_22.23_spmd.clone, body=%wide.region_18.22_spmd.clone.sunk | while | flops 494647776 | bytes 27775196 | solution.py:160
  477.1 4.2 multiply_reduce_fusion.1
  484.4 4.9 fusion.64
  489.4 8.9 fusion.85
  500.0 10.3 fusion.86
  510.4 11.8 fusion.56
  523.0 58.4 %reduce-scatter.17.cloned.1.call-done = f32[24,28]{1,0:T(8,128)} async-done(((f32[768,28]{1,0:T(8,128)}), f32[24,28]{1,0:T(8,128)}) %reduce-scatter.17.cloned.1.call-update) | async-done | bytes 2704
  582.9 103.4 %reduce-scatter.11.cloned.1.call-done = f32[24,768]{1,0:T(8,128)} async-done(((f32[768,768]{1,0:T(8,128)}), f32[24,768]{1,0:T(8,128)}) %reduce-scatter.11.cloned.1.call-update) | async-done | bytes 73744 | tf_op jit(solution)/shard_map/reduce_scatter | solution.py:256
  687.9 122.8 %reduce-scatter.9.cloned.1.call-done = f32[24,2304]{1,0:T(8,128)} async-done(((f32[768,2304]{1,0:T(8,128)}), f32[24,2304]{1,0:T(8,128)}) %reduce-scatter.9.cloned.1.call-update) | async-done | bytes 221200 | tf_op jit(solution)/shard_map/reduce_scatter | solution.py:255
  812.5 140.7 %reduce-scatter.13.cloned.1.call-done = f32[24,3072]{1,0:T(8,128)} async-done(((f32[768,3072]{1,0:T(8,128)}), f32[24,3072]{1,0:T(8,128)}) %reduce-scatter.13.cloned.1.call-update) | async-done | bytes 294928 | tf_op jit(solution)/shard_map/reduce_scatter | solution.py:257
  955.0 139.3 %reduce-scatter.15.cloned.1.call-done = f32[96,768]{1,0:T(8,128)} async-done(((f32[3072,768]{1,0:T(8,128)}), f32[96,768]{1,0:T(8,128)}) %reduce-scatter.15.cloned.1.call-update) | async-done | bytes 294928 | tf_op jit(solution)/shard_map/reduce_scatter | solution.py:258
  1096.0 40.8 %all-reduce.5 = (f32[768,6]{0,1:T(8,128)S(1)}, f32[]{:T(128)}, f32[2304]{0:T(1024)S(1)}, f32[]{:T(128)}, f32[768]{0:T(1024)S(1)}, /*index=5*/f32[]{:T(128)}, f32[3072]{0:T(1024)S(1)}, f32[]{:T(128)}, f32[768]{0:T(1024)S(1)}) all-reduce(f32[768,6]{0,1:T(8,128)S(1)} %maximum_add_fusion, ...), channel_id=3, replica_groups=mesh['dp'=2,'fsdp'=16] {'dp','fsdp'}, use_global_device_ids=true, to_apply=%region_33.34.clone | all-reduce | flops 11524 | bytes 92192
  1150.9 39.5 %all-reduce.4 = (f32[]{:T(128)}, f32[]{:T(128)}) all-reduce(f32[]{:T(128)} %get-tuple-element.509, f32[]{:T(128)S(6)} %add.305), channel_id=1, replica_groups=mesh['dp'=2,'fsdp'=16] {'dp','fsdp'}, use_global_device_ids=true, to_apply=%region_11.12 | all-reduce | flops 2 | bytes 16 | tf_op jit(solution)/shard_map/psum | solution.py:279
  (371 shorter events, 267.5 us)
Async XLA Ops:
  7.2 189.9 %all-gather.6.cloned.1.call-start = ((), (), s32[]{:S(2)}) async-start(), calls=%async_computation.5 | async-start | bytes 3649536 | tf_op jit(solution)/shard_map/all_gather | solution.py:215
  8.9 281.5 %all-gather.8.cloned.1.call-start = ((), (), s32[]{:S(2)}) async-start(), calls=%async_computation.6 | async-start | bytes 1216512 | tf_op jit(solution)/shard_map/all_gather | solution.py:216
  10.4 285.1 %all-gather.10.cloned.1.call-start = ((), (), s32[]{:S(2)}) async-start(), calls=%async_computation.7 | async-start | bytes 4866048 | tf_op jit(solution)/shard_map/all_gather | solution.py:217
  12.2 294.9 %all-gather.12.cloned.1.call-start = ((), (), s32[]{:S(2)}) async-start(), calls=%async_computation.8 | async-start | bytes 4866048 | tf_op jit(solution)/shard_map/all_gather | solution.py:218
  13.9 567.6 %reduce-scatter.17.cloned.1.call-start = ((), (), s32[]{:S(2)}) async-start(), calls=%async_computation.13 | async-start | bytes 405504
  484.3 201.9 %reduce-scatter.11.cloned.1.call-start = ((), (), s32[]{:S(2)}) async-start(), calls=%async_computation.10 | async-start | bytes 2433024 | tf_op jit(solution)/shard_map/reduce_scatter | solution.py:256
  489.3 321.4 %reduce-scatter.9.cloned.1.call-start = ((), (), s32[]{:S(2)}) async-start(), calls=%async_computation.9 | async-start | bytes 7299072 | tf_op jit(solution)/shard_map/reduce_scatter | solution.py:255
  498.3 454.9 %reduce-scatter.13.cloned.1.call-start = ((), (), s32[]{:S(2)}) async-start(), calls=%async_computation.11 | async-start | bytes 9732096 | tf_op jit(solution)/shard_map/reduce_scatter | solution.py:257
  510.3 584.0 %reduce-scatter.15.cloned.1.call-start = ((), (), s32[]{:S(2)}) async-start(), calls=%async_computation.12 | async-start | bytes 9732096 | tf_op jit(solution)/shard_map/reduce_scatter | solution.py:258
  522.2 573.2 %copy-start.55 = (f32[96]{0:T(128)S(1)}, f32[96]{0:T(128)}, u32[]{:S(2)}) copy-start(f32[96]{0:T(128)} %param.50) | copy-start | bytes 1156
  522.2 614.7 %copy-start.45 = (f32[768]{0:T(1024)S(1)}, f32[768]{0:T(1024)}, u32[]{:S(2)}) copy-start(f32[768]{0:T(1024)} %param.51) | copy-start | bytes 9220
  522.2 614.7 %copy-start.37 = (f32[3072]{0:T(1024)S(1)}, f32[3072]{0:T(1024)}, u32[]{:S(2)}) copy-start(f32[3072]{0:T(1024)} %param.48) | copy-start | bytes 36868
  522.3 614.7 %copy-start.46 = (f32[768]{0:T(1024)S(1)}, f32[768]{0:T(1024)}, u32[]{:S(2)}) copy-start(f32[768]{0:T(1024)} %param.45) | copy-start | bytes 9220
  522.3 614.7 %copy-start.38 = (f32[2304]{0:T(1024)S(1)}, f32[2304]{0:T(1024)}, u32[]{:S(2)}) copy-start(f32[2304]{0:T(1024)} %param.42) | copy-start | bytes 27652
  522.3 626.6 %copy-start.47 = (f32[24,6]{0,1:T(8,128)S(1)}, f32[24,6]{0,1:T(8,128)}, u32[]{:S(2)}) copy-start(f32[24,6]{0,1:T(8,128)} %param.55) | copy-start | bytes 1732
  522.3 668.9 %copy-start.35 = (f32[24,6]{0,1:T(8,128)S(1)}, f32[24,6]{0,1:T(8,128)}, u32[]{:S(2)}) copy-start(f32[24,6]{0,1:T(8,128)} %param.54) | copy-start | bytes 1732
  522.3 669.5 %copy-start.8 = (f32[96,768]{1,0:T(8,128)S(1)}, f32[96,768]{1,0:T(8,128)}, u32[]{:S(2)}) copy-start(f32[96,768]{1,0:T(8,128)} %param.49) | copy-start | bytes 884740
  522.3 671.9 %copy-start.9 = (f32[24,3072]{1,0:T(8,128)S(1)}, f32[24,3072]{1,0:T(8,128)}, u32[]{:S(2)}) copy-start(f32[24,3072]{1,0:T(8,128)} %param.46) | copy-start | bytes 884740
  522.4 673.4 %copy-start.12 = (f32[24,768]{1,0:T(8,128)S(1)}, f32[24,768]{1,0:T(8,128)}, u32[]{:S(2)}) copy-start(f32[24,768]{1,0:T(8,128)} %param.43) | copy-start | bytes 221188
  522.4 674.7 %copy-start.10 = (f32[24,2304]{1,0:T(8,128)S(1)}, f32[24,2304]{1,0:T(8,128)}, u32[]{:S(2)}) copy-start(f32[24,2304]{1,0:T(8,128)} %param.40) | copy-start | bytes 663556
  522.4 676.2 %copy-start.15 = (f32[24,28]{1,0:T(8,128)S(1)}, f32[24,28]{1,0:T(8,128)}, u32[]{:S(2)}) copy-start(f32[24,28]{1,0:T(8,128)} %param.52) | copy-start | bytes 8068
  581.5 617.1 %copy-start.16 = (f32[24,28]{1,0:T(8,128)S(1)}, f32[24,28]{1,0:T(8,128)}, u32[]{:S(2)}) copy-start(f32[24,28]{1,0:T(8,128)} %reduce-scatter.17.cloned.1.call-done) | copy-start | bytes 8068
  582.9 616.3 %copy-start.17 = (f32[24,28]{1,0:T(8,128)}, f32[24,28]{1,0:T(8,128)S(1)}, u32[]{:S(2)}) copy-start(f32[24,28]{1,0:T(8,128)S(1)} %get-tuple-element.487) | copy-start | bytes 8068
  687.9 511.3 %copy-start.41 = (f32[24]{0:T(128)}, f32[24]{0:T(128)S(1)}, u32[]{:S(2)}) copy-start(f32[24]{0:T(128)S(1)} %get-tuple-element.483) | copy-start | bytes 292
  (47 other events, 3867.2 us)
Sparse Core Ops, SparseCore 0:
  11.5 63.4 all-gather.5
  78.4 52.7 all-gather.7
  134.7 63.0 all-gather.9
  201.1 62.3 all-gather.11
  484.4 96.9 reduce-scatter.16
  588.0 98.1 reduce-scatter.10
  692.5 118.2 reduce-scatter.8
  818.2 134.9 reduce-scatter.12
  959.7 134.5 reduce-scatter.14
where the time goes:
time: 1210 us
  waiting for transfers between devices  565 us (47%)
  matrix products  258 us (21%)
  blocking collectives  254 us (21%)
  other arithmetic  70.2 us (6%)
  local copies, waits for them, and re-layouts  35.3 us (3%)
  between operations  23.5 us (2%)
    reduce_scatter x1, waiting for transfers between devices, on_device(): lax.psum_scatter(upper[1], ('dp', 'fsdp'), scatter_dimension=0, tiled=True)  141 us
    reduce_scatter x1, waiting for transfers between devices, on_device(): lax.psum_scatter(upper[2], ('dp', 'fsdp'), scatter_dimension=0, tiled=True)  139 us
    reduce_scatter x1, waiting for transfers between devices, on_device(): lax.psum_scatter(lower[0], ('dp', 'fsdp'), scatter_dimension=0, tiled=True)  123 us
    dot_general x42, matrix products, dot_right(): lax.dot_general(left, right, (((1,), (1,)), ((), ())), preferred_element_...  107 us
    reduce_scatter x1, waiting for transfers between devices, on_device(): lax.psum_scatter(upper[0], ('dp', 'fsdp'), scatter_dimension=0, tiled=True)  103 us
    dot_general x29, matrix products, dot_plain(): return jnp.dot(left, right, preferred_element_type=jnp.float32)  76.8 us
    dot_general x30, matrix products, dot_left(): lax.dot_general(left, right, (((0,), (0,)), ((), ())), preferred_element_...  74.8 us
    all_gather x1, blocking collectives, on_device(): lax.all_gather(wire[4], ('dp', 'fsdp'), axis=0, tiled=True)  71.5 us
  transfers between devices with their start and end apart: 9, of which 5 were waited for; matrix products, arithmetic and copies ran while one was open for 13% of the time, Pallas kernels for 0%

commit v1 on v0

v1 whole, which is shorter than its diff:
```python
import functools
import math

import jax
import jax.numpy as jnp
from jax import lax
from jax.experimental import pallas as pl
from jax.experimental.pallas import tpu as pltpu
from jax.sharding import PartitionSpec as P

D = 768
HEADS = 12
HDIM = 64
FF = 3072
GOALTOK = 64
ACTW = 28
TSTEPS = 20
STEP = 10
LANES = 128
SLOTS = 16
AX = ("dp", "fsdp")

rate_matrix = 0.05
rate_small = 0.3
clip_level = 0.5
BF = jnp.bfloat16
F32 = jnp.float32
MIB = 1024 * 1024


class Moves:
    def __init__(self, mesh):
        self.dp = mesh.shape["dp"]
        self.fsdp = mesh.shape["fsdp"]
        self.count = self.dp * self.fsdp
        self.fast = self.dp == 2 and self.fsdp == 16
        self.depth = self.fsdp // 4

    def flip(self, value, mask):
        return lax.ppermute(value, "fsdp", [(i, i ^ mask) for i in range(self.fsdp)])

    def turn(self, value, step):
        return lax.ppermute(
            value, "fsdp", [(i, (i + 4 * step) % self.fsdp) for i in range(self.fsdp)]
        )

    def swap(self, value):
        return lax.ppermute(value, "dp", [(0, 1), (1, 0)])

    def place(self):
        inner = lax.axis_index("fsdp")
        return lax.axis_index("dp"), inner // 4, (inner // 2) % 2, inner % 2


def ordered(own, other, bit):
    first = jnp.where(bit == 0, own, other)
    second = jnp.where(bit == 0, other, own)
    return first, second


def pair(own, other, bit, blocks=1):
    first, second = ordered(own, other, bit)
    rows, width = own.shape
    shaped = (blocks, 1, rows // blocks, width)
    both = jnp.concatenate([first.reshape(shaped), second.reshape(shaped)], 1)
    return both.reshape(2 * rows, width)


def stack_at(parts, places):
    out = jnp.zeros((len(parts),) + parts[0].shape, parts[0].dtype)
    for part, at in zip(parts, places):
        out = lax.dynamic_update_index_in_dim(out, part, at, 0)
    return out


def gather_weights(moves, attn, one, two):
    if not moves.fast:
        return [[lax.all_gather(w, AX, axis=0, tiled=True)] for w in (attn, one, two)]
    core, z, y, x = moves.place()
    depth = moves.depth

    def rest(last, merge):
        mine = [merge(v, last(v)) for v in ring]
        return mine + [moves.swap(v) for v in mine]

    ring = [pair(attn, moves.flip(attn, 1), x)]
    for _ in range(depth - 1):
        ring.append(moves.turn(ring[-1], 1))
    attn_parts = rest(lambda v: moves.flip(v, 2), lambda v, o: pair(v, o, y))

    ring = [pair(one, moves.flip(one, 2), y)]
    for _ in range(depth - 1):
        ring.append(moves.turn(ring[-1], 1))
    one_parts = rest(lambda v: moves.flip(v, 1), lambda v, o: pair(v, o, x, 2))

    ring = [two]
    for _ in range(depth - 1):
        ring.append(moves.turn(ring[-1], -1))
    back = [pair(v, moves.flip(v, 2), y) for v in ring]
    ring = [back[0], back[3], back[2], back[1]] if depth == 4 else back
    two_parts = rest(lambda v: moves.flip(v, 1), lambda v, o: pair(v, o, x, 2))
    return [attn_parts, one_parts, two_parts]


def gather_rows(moves, part):
    if not moves.fast:
        return lax.all_gather(part, AX, axis=0, tiled=True)
    core, z, y, x = moves.place()
    depth = moves.depth
    parts = [part] + [moves.turn(part, k) for k in range(1, depth)]
    held = stack_at(parts, [(z - k) % depth for k in range(depth)])
    parts = [held] + [moves.flip(held, k) for k in range(1, 4)]
    spot = 2 * y + x
    held = stack_at(parts, [spot ^ k for k in range(4)])
    held = held.transpose(1, 0, 2, 3)
    held = stack_at([held, moves.swap(held)], [core, 1 - core])
    return held.reshape(moves.count * part.shape[0], part.shape[1])


def exchange(moves, blocks):
    return lax.all_to_all(blocks, AX, 0, 0, tiled=False)


def total(moves, value):
    if not moves.fast:
        return lax.psum(value, AX)
    value = value + moves.swap(value)
    value = (value + moves.flip(value, 1)) + (moves.flip(value, 2) + moves.flip(value, 3))
    return (value + moves.flip(value, 4)) + (moves.flip(value, 8) + moves.flip(value, 12))


def dot(left, right):
    return jnp.dot(left, right, preferred_element_type=F32)


def dot_right(left, right):
    return lax.dot_general(left, right, (((1,), (1,)), ((), ())), preferred_element_type=F32)


def dot_left(left, right):
    return lax.dot_general(left, right, (((0,), (0,)), ((), ())), preferred_element_type=F32)


def normal(h):
    mean = jnp.mean(h, -1, keepdims=True)
    centered = h - mean
    root = lax.rsqrt(jnp.mean(centered * centered, -1, keepdims=True) + 1e-06)
    return centered * root, root


def normal_back(grad, unit, root, gain):
    scaled = grad * gain
    return root * (
        scaled
        - jnp.mean(scaled, -1, keepdims=True)
        - unit * jnp.mean(scaled * unit, -1, keepdims=True)
    )


def spread(rows):
    read = rows.shape[0]
    tall = jnp.concatenate([rows.astype(F32)] * HEADS, 0)
    return jnp.where(own_head(read), tall, 0.0).astype(BF)


def own_head(read):
    row = lax.broadcasted_iota(jnp.int32, (HEADS * read, D), 0) // read
    lane = lax.broadcasted_iota(jnp.int32, (HEADS * read, D), 1) // HDIM
    return row == lane


def gathered(tall):
    read = tall.shape[0] // HEADS
    kept = jnp.where(own_head(read), tall, 0.0)
    out = kept[0:read]
    for head in range(1, HEADS):
        out = out + kept[head * read : (head + 1) * read]
    return out


def copies_in(parts, target, sems, depth):
    started = []
    if len(parts) == 1:
        started.append(pltpu.make_async_copy(parts[0], target, sems.at[0]))
    else:
        core = lax.axis_index("dp")
        z = lax.axis_index("fsdp") // 4
        rows = parts[0].shape[0]
        for k, part in enumerate(parts):
            half = core if k < depth else 1 - core
            block = half * depth + lax.rem(z - (k % depth) + depth, depth)
            start = pl.multiple_of(block * rows, rows)
            started.append(pltpu.make_async_copy(part, target.at[pl.ds(start, rows)], sems.at[k]))
    for copy in started:
        copy.start()
    return started


def norm_kernel(tok_ref, last_ref, gain_ref, a_ref, unit_ref, h_ref):
    step = pl.program_id(0)
    h_ref[...] = tok_ref[...].astype(F32)
    read = last_ref.shape[0]
    rows = h_ref.shape[0]

    @pl.when(step == pl.num_programs(0) - 1)
    def _():
        h_ref[rows - read :, :] = last_ref[...]

    unit, _ = normal(h_ref[...])
    unit_ref[...] = unit
    a_ref[...] = (unit * gain_ref[0:1, :] + gain_ref[1:2, :]).astype(BF)


def attend_kernel(depth, n, a_ref, last_ref, gain_ref, seen_ref, *refs):
    parts = refs[:n]
    q_ref, qk_ref, p_ref, pa_ref, o_ref, y_ref, a2_ref, w_ref, sems = refs[n:]
    for copy in copies_in(parts, w_ref, sems, depth):
        copy.wait()
    seq = a_ref.shape[0]
    read = last_ref.shape[0]
    a = a_ref[...]
    q = dot(a_ref[seq - read :, :], w_ref[:, 0:D]).astype(BF)
    q_ref[...] = q
    qk = (dot_right(spread(q), w_ref[:, D : 2 * D]) * HDIM ** (-0.5)).astype(BF)
    qk_ref[...] = qk
    scores = dot_right(qk, a)
    seen = jnp.concatenate([seen_ref[...]] * HEADS, 0)
    scores = jnp.where(seen > 0.5, scores, -1000000000.0)
    top = jnp.max(scores, -1, keepdims=True)
    grown = jnp.exp(scores - top)
    probs = grown / jnp.sum(grown, -1, keepdims=True)
    p_ref[...] = probs
    pa = dot(probs.astype(BF), a).astype(BF)
    pa_ref[...] = pa
    o = gathered(dot(pa, w_ref[:, 2 * D : 3 * D])).astype(BF)
    o_ref[...] = o
    y = last_ref[...] + dot(o, w_ref[:, 3 * D :])
    y_ref[...] = y
    unit, _ = normal(y)
    a2_ref[...] = (unit * gain_ref[2:3, :] + gain_ref[3:4, :]).astype(BF)


def feed_kernel(
    depth, n, y_ref, a2_ref, gain_ref, table_ref, noise_ref, weigh_ref, wo_ref, *refs
):
    one_parts, two_parts = refs[:n], refs[n : 2 * n]
    (
        m_ref, dz_ref, du_ref, f_ref, de_ref, da_ref, do_ref, dy_ref, small_ref, loss_ref,
        one, two, sems,
    ) = refs[2 * n :]
    first = copies_in(one_parts, one, sems.at[0], depth)
    second = copies_in(two_parts, two, sems.at[1], depth)
    for copy in first:
        copy.wait()
    y = y_ref[...]
    a2 = a2_ref[...]
    u = dot(a2, one[...])
    root_two = math.sqrt(2.0 / math.pi)
    curve = jnp.tanh(root_two * (u + 0.044715 * (u * u * u)))
    half = 0.5 * (1.0 + curve)
    m = (u * half).astype(BF)
    slope = half + 0.5 * u * (1.0 - curve * curve) * (root_two * (1.0 + 3.0 * 0.044715 * (u * u)))
    m_ref[...] = m
    for copy in second:
        copy.wait()
    h2 = y + dot(m, two[...])
    unit3, root3 = normal(h2)
    gain2, gain3 = gain_ref[2:3, :], gain_ref[4:5, :]
    f = (unit3 * gain3 + gain_ref[5:6, :]).astype(BF)
    f_ref[...] = f
    lane = lax.broadcasted_iota(jnp.int32, table_ref.shape, 1)
    table = jnp.where(lane < ACTW, table_ref[...].astype(F32), 0.0).astype(BF)
    e = dot(f, table) - noise_ref[...]
    mask = weigh_ref[0:1, :]
    loss_ref[...] = jnp.broadcast_to(jnp.sum(mask * e * e), loss_ref.shape)
    de = (weigh_ref[1:2, :] * e).astype(BF)
    de_ref[...] = de
    df = dot_right(de, table)
    dh2 = normal_back(df, unit3, root3, gain3)
    dz = dh2.astype(BF)
    dz_ref[...] = dz
    du = (slope * dot_right(dz, two[...])).astype(BF)
    du_ref[...] = du
    da2 = dot_right(du, one[...])
    unit2, root2 = normal(y)
    dy = dh2 + normal_back(da2, unit2, root2, gain2)
    dy_ref[...] = dy
    da = dy.astype(BF)
    da_ref[...] = da
    do_ref[...] = dot_right(da, wo_ref[...]).astype(BF)
    small_ref[...] = jnp.concatenate(
        [
            jnp.zeros((2, D), F32),
            jnp.sum(da2 * unit2, 0, keepdims=True),
            jnp.sum(da2, 0, keepdims=True),
            jnp.sum(df * unit3, 0, keepdims=True),
            jnp.sum(df, 0, keepdims=True),
            jnp.zeros((2, D), F32),
        ],
        0,
    )


def back_kernel(
    a_ref, unit_ref, p_ref, qk_ref, do_ref, dy_ref, last_ref, gain_ref, w_ref,
    dq_ref, dsa_ref, demb_ref, small_ref, da_ref,
):
    seq = a_ref.shape[0]
    read = dy_ref.shape[0]
    a = a_ref[...]
    probs = p_ref[...]
    dv = dot_right(spread(do_ref[...]), w_ref[:, 2 * D : 3 * D]).astype(BF)
    dp = dot_right(dv, a)
    ds = (probs * (dp - jnp.sum(dp * probs, -1, keepdims=True))).astype(BF)
    dsa = dot(ds, a).astype(BF)
    dsa_ref[...] = dsa
    dq = (gathered(dot(dsa, w_ref[:, D : 2 * D])) * HDIM ** (-0.5)).astype(BF)
    dq_ref[...] = dq
    da_ref[...] = dot_left(ds, qk_ref[...]) + dot_left(probs.astype(BF), dv)
    da_ref[seq - read :, :] = da_ref[seq - read :, :] + dot_right(dq, w_ref[:, 0:D])
    unit, root = normal(last_ref[...])
    dh = dy_ref[...] + normal_back(da_ref[seq - read :, :], unit, root, gain_ref[0:1, :])
    demb_ref[...] = dh.astype(BF)
    da = da_ref[...]
    small_ref[...] = jnp.concatenate(
        [
            jnp.sum(da * unit_ref[...], 0, keepdims=True),
            jnp.sum(da, 0, keepdims=True),
            jnp.zeros((6, D), F32),
        ],
        0,
    )


VMEM = pl.BlockSpec(memory_space=pltpu.VMEM)
ANY = pl.BlockSpec(memory_space=pl.ANY)


def shape(dims, dtype):
    return jax.ShapeDtypeStruct(dims, dtype)


def params():
    return pltpu.CompilerParams(vmem_limit_bytes=48 * MIB)


def run_norm(tokens, last, gains):
    seq = tokens.shape[0]
    rows = seq // 6
    return pl.pallas_call(
        norm_kernel,
        grid=(6,),
        out_shape=(shape((seq, D), BF), shape((seq, D), F32)),
        in_specs=[
            pl.BlockSpec((rows, D), lambda i: (i, 0)),
            pl.BlockSpec(last.shape, lambda i: (0, 0)),
            pl.BlockSpec(gains.shape, lambda i: (0, 0)),
        ],
        out_specs=(
            pl.BlockSpec((rows, D), lambda i: (i, 0)),
            pl.BlockSpec((rows, D), lambda i: (i, 0)),
        ),
        scratch_shapes=[pltpu.VMEM((rows, D), F32)],
        compiler_params=params(),
        name="norm_tokens",
    )(tokens, last, gains)


def run_attend(moves, normed, last, gains, seen, parts):
    seq, read, n = normed.shape[0], last.shape[0], len(parts)
    tall = HEADS * read
    return pl.pallas_call(
        functools.partial(attend_kernel, moves.depth, n),
        out_shape=(
            shape((read, D), BF),
            shape((tall, D), BF),
            shape((tall, seq), F32),
            shape((tall, D), BF),
            shape((read, D), BF),
            shape((read, D), F32),
            shape((read, D), BF),
            shape((D, 4 * D), BF),
        ),
        in_specs=[VMEM] * 4 + [ANY] * n,
        out_specs=(VMEM,) * 8,
        scratch_shapes=[pltpu.SemaphoreType.DMA((n,))],
        compiler_params=params(),
        name="attend",
    )(normed, last, gains, seen, *parts)


def run_feed(moves, y, a2, gains, packed, noise, weigh, weights, one, two):
    read, n = y.shape[0], len(one)
    return pl.pallas_call(
        functools.partial(feed_kernel, moves.depth, n),
        grid=(1,),
        out_shape=(
            shape((read, FF), BF),
            shape((read, D), BF),
            shape((read, FF), BF),
            shape((read, D), BF),
            shape((read, LANES), BF),
            shape((read, D), BF),
            shape((read, D), BF),
            shape((read, D), F32),
            shape((8, D), F32),
            shape((8, LANES), F32),
        ),
        in_specs=[VMEM] * 6 + [pl.BlockSpec((D, D), lambda i: (0, 3))] + [ANY] * (2 * n),
        out_specs=(VMEM,) * 10,
        scratch_shapes=[
            pltpu.VMEM((D, FF), BF),
            pltpu.VMEM((FF, D), BF),
            pltpu.SemaphoreType.DMA((2, n)),
        ],
        compiler_params=params(),
        name="feed",
    )(y, a2, gains, packed, noise, weigh, weights, *one, *two)


def run_back(normed, unit, probs, qk, do, dy, last, gains, weights):
    seq, read = normed.shape[0], dy.shape[0]
    return pl.pallas_call(
        back_kernel,
        grid=(1,),
        out_shape=(
            shape((read, D), BF),
            shape((HEADS * read, D), BF),
            shape((read, D), BF),
            shape((8, D), F32),
        ),
        in_specs=[VMEM] * 8 + [pl.BlockSpec((D, 3 * D), lambda i: (0, 0))],
        out_specs=(VMEM,) * 4,
        scratch_shapes=[pltpu.VMEM((seq, D), F32)],
        compiler_params=params(),
        name="back",
    )(normed, unit, probs, qk, do, dy, last, gains, weights)


def condition(actions, noise, tstep, width):
    frac = (tstep.astype(F32) / TSTEPS + 0.008) / 1.008
    alpha_bar = jnp.cos(frac * (math.pi / 2)) ** 2
    noisy = jnp.sqrt(alpha_bar) * actions + jnp.sqrt(1.0 - alpha_bar) * noise
    half = width // 2
    freq = jnp.exp(jnp.arange(half).astype(F32) * (-math.log(10000.0) / half))
    angle = tstep.astype(F32) * freq
    return (noisy, jnp.concatenate([jnp.sin(angle), jnp.cos(angle)]))


def visible_last(groups, task_mask, goal_flag, read):
    seq = groups.shape[0]
    task = task_mask.shape[0]
    places = jnp.arange(seq)
    task_pad = jnp.pad(task_mask, (0, seq - task)) * (1 - goal_flag)
    valid = jnp.where(places < task, task_pad, jnp.where(places < task + GOALTOK, goal_flag, 1))
    seen = (groups[None, :] <= groups[seq - read :, None]) & (valid[None, :] > 0)
    seen = seen | (places[seq - read :, None] == places[None, :])
    return seen.astype(F32)


def to_owners(slots, count):
    kinds, read, width = slots.shape
    own = width // count
    blocks = slots.reshape(kinds, read, count, own).transpose(2, 1, 0, 3)
    return blocks.reshape(count, read, kinds * own)


def lanes_to(value, width):
    return jnp.pad(value, ((0, 0), (0, width - value.shape[1])))


def heads_own(tall, own):
    lane = jnp.arange(D) // HDIM
    keep = lane[None, None, :] == jnp.arange(HEADS)[:, None, None]
    return jnp.sum(jnp.where(keep, tall.reshape(HEADS, own, D), 0.0), 0)


def on_device(moves, *arrays):
    (
        tokens, actions, noise, timesteps, task_mask, goal_flag, act_mask, groups,
        w_qkv, rows_qkv, cols_qkv, w_out, rows_out, cols_out,
        w_one, rows_one, cols_one, w_two, rows_two, cols_two,
        w_table, var_table, small, var_small,
    ) = arrays
    tokens, actions, noise, tstep = tokens[0], actions[0], noise[0], timesteps[0]
    read = noise.shape[0]
    seq = tokens.shape[0]
    count = moves.count
    own = w_qkv.shape[0]

    attn = jnp.concatenate([w_qkv, w_out], 1).astype(BF)
    attn_parts, one_parts, two_parts = gather_weights(
        moves, attn, w_one.astype(BF), w_two.astype(BF)
    )

    marks = jnp.sum(act_mask.astype(F32))
    first_row = (jnp.arange(own) == 0).astype(F32)[:, None]
    wire = lanes_to(jnp.concatenate([w_table, small, first_row * marks], 1), LANES).astype(BF)
    packed = exchange(moves, jnp.broadcast_to(wire[None], (count,) + wire.shape))
    packed = packed.reshape(D, LANES)
    gains = jnp.pad(packed[:, ACTW : ACTW + 6].T.astype(F32), ((0, 2), (0, 0)))
    entries_count = read * jnp.sum(packed[:, ACTW + 6].astype(F32))
    seed = 1.0 / entries_count

    noisy, temb = condition(actions, noise, tstep, D)
    noisy_low = lanes_to(noisy.astype(BF), LANES)
    embed = dot_right(noisy_low[:, :ACTW], packed[:, :ACTW])
    last = tokens[seq - read :].astype(F32) + (embed + temb)
    normed, unit = run_norm(tokens, last, gains)
    seen = visible_last(groups[0], task_mask[0], goal_flag[0], read)
    q, qk, probs, pa, o, y, a2, weights = run_attend(moves, normed, last, gains, seen, attn_parts)

    mask = act_mask[0].astype(F32)
    weigh = lanes_to(jnp.stack([mask, seed * 2.0 * mask]), LANES)
    weigh = jnp.pad(weigh, ((0, 6), (0, 0)))
    m, dz, du, f, de, da, do, dy, small_up, loss = run_feed(
        moves, y, a2, gains, packed, lanes_to(noise, LANES), weigh, weights, one_parts, two_parts
    )
    dq, dsa, demb, small_low = run_back(normed, unit, probs, qk, do, dy, last, gains, weights)
    g_vec = (small_up + small_low)[0:6]
    g_high = g_vec.astype(BF)
    g_rest = (g_vec - g_high.astype(F32)).astype(BF)
    split = jnp.concatenate([g_high, g_rest, jnp.zeros((4, D), BF)], 0)

    early = jnp.concatenate(
        [
            pa.reshape(HEADS, read, D),
            jnp.stack([o, normed[seq - read :], a2, jnp.zeros_like(a2)]),
        ],
        0,
    )
    late = jnp.concatenate(
        [
            dsa.reshape(HEADS, read, D),
            jnp.stack([f, demb, split, jnp.zeros_like(f)]),
        ],
        0,
    )
    n_rows = count * read
    got_early = exchange(moves, to_owners(early, count)).reshape(n_rows, SLOTS * own)
    got_mid = exchange(moves, m.reshape(read, count, FF // count).transpose(1, 0, 2))
    got_mid = got_mid.reshape(n_rows, FF // count)
    got_late = exchange(moves, to_owners(late, count)).reshape(n_rows, SLOTS * own)

    all_q = gather_rows(moves, q)
    all_up = gather_rows(moves, jnp.concatenate([dz, du, de, noisy_low], 1))
    all_low = gather_rows(moves, jnp.concatenate([da, do, dq], 1))
    all_dz, all_du = all_up[:, 0:D], all_up[:, D : D + FF]
    all_de, all_noisy = all_up[:, D + FF :][:, :LANES], all_up[:, D + FF + LANES :]
    all_da, all_do, all_dq = all_low[:, :D], all_low[:, D : 2 * D], all_low[:, 2 * D :]

    heads = HEADS * own

    def slot(array, k):
        return array[:, k * own : (k + 1) * own]

    g_v = heads_own(dot_left(got_early[:, :heads], all_do), own)
    g_out = dot_left(slot(got_early, HEADS), all_da)
    g_one = dot_left(slot(got_early, HEADS + 2), all_du)
    g_two = dot_left(got_mid, all_dz)
    g_q = dot_left(slot(got_early, HEADS + 1), all_dq)
    g_k = heads_own(dot_left(got_late[:, :heads], all_q), own) * HDIM ** (-0.5)
    g_qkv = jnp.concatenate([g_q, g_k, g_v], 1)
    g_table = (
        dot_left(slot(got_late, HEADS), all_de) + dot_left(slot(got_late, HEADS + 1), all_noisy)
    )[:, :ACTW]
    parts = jnp.sum(slot(got_late, HEADS + 2).reshape(count, read, own).astype(F32), 0)
    g_small = (parts[0:6] + parts[6:12]).T

    beta = 1.0 - float(STEP) ** (-0.8)
    mats = (g_qkv, g_out, g_one, g_two)
    squares = tuple((g * g for g in mats))
    rows_new = tuple(
        (
            beta * r + (1.0 - beta) * jnp.sum(sq, 1)
            for r, sq in zip((rows_qkv, rows_out, rows_one, rows_two), squares)
        )
    )
    var_table_new = beta * var_table + (1.0 - beta) * g_table * g_table
    var_small_new = beta * var_small + (1.0 - beta) * g_small * g_small
    unit_table = g_table * lax.rsqrt(var_table_new)
    unit_small = g_small * lax.rsqrt(var_small_new)
    vector_squares = jnp.sum(unit_table * unit_table) + jnp.sum(unit_small * unit_small)
    col_parts = [jnp.sum(sq, 0) for sq in squares]
    over_rows = [jnp.sum(sq / r[:, None], 0) for sq, r in zip(squares, rows_new)]
    singles = jnp.stack([jnp.sum(r) for r in rows_new] + [vector_squares, loss[0, 0]])
    sums = jnp.concatenate(col_parts + over_rows + [singles])
    length = sums.shape[0]
    sums = jnp.pad(sums, (0, -length % (8 * LANES))).reshape(-1, LANES)
    sums = total(moves, sums).reshape(-1)[:length]
    cuts = []
    at = 0
    for size in [c.shape[0] for c in col_parts] * 2:
        cuts.append(sums[at : at + size])
        at += size
    totals = [sums[at + k] for k in range(4)]
    squares_total, loss_sum = sums[at + 4], sums[at + 5]
    cols_new = tuple(
        (
            beta * c + (1.0 - beta) * s
            for c, s in zip((cols_qkv, cols_out, cols_one, cols_two), cuts[:4])
        )
    )
    for c, over, t in zip(cols_new, cuts[4:], totals):
        squares_total = squares_total + t * jnp.sum(over / c)
    units = tuple(
        (
            g * lax.rsqrt(r[:, None] * c[None, :] / t)
            for g, r, c, t in zip(mats, rows_new, cols_new, totals)
        )
    )
    entries = 4 * D * D + 2 * D * FF + D * ACTW + 6 * D
    clip_rms = jnp.sqrt(squares_total / entries)
    factor = 1.0 / jnp.maximum(1.0, clip_rms / clip_level)
    result = [loss_sum, entries_count, clip_rms]
    for master, grad, rows, cols, update in zip(
        (w_qkv, w_out, w_one, w_two), mats, rows_new, cols_new, units
    ):
        result += [grad, rows, cols, master - rate_matrix * update * factor]
    result += [g_table, var_table_new, w_table - rate_matrix * unit_table * factor]
    result += [g_small, var_small_new, small - rate_small * unit_small * factor]
    return tuple(result)


def solution(mesh):
    rows = P(AX)
    items = (rows,) * 8
    matrix = (rows, rows, P())
    plain = (rows, rows)
    return jax.shard_map(
        functools.partial(on_device, Moves(mesh)),
        mesh=mesh,
        in_specs=items + matrix * 4 + plain * 2,
        out_specs=(P(),) * 3 + (rows, rows, P(), rows) * 4 + (rows,) * 6,
        check_vma=False,
    )
```

time: 1210 us -> 363 us (0.30)
  waiting for transfers between devices: 565 us -> 99.2 us
  blocking collectives: 254 us -> 0 us
  matrix products: 258 us -> 9.62 us
  starting transfers between devices: 0.37 us -> 91.2 us
  local copies, waits for them, and re-layouts: 35.3 us -> 92.7 us
  other arithmetic: 70.2 us -> 31.7 us
  Pallas kernels: 0 us -> 22.7 us
    reduce_scatter x4 -> x0, waiting for transfers between devices: 506 us -> none  [the longest x1 141 us: on_device(): lax.psum_scatter(upper[1], ('dp', 'fsdp'), scatter_dimension=0, tiled=True)]
    all_gather x2 -> x0, blocking collectives: 135 us -> none  [the longest x1 71.5 us: on_device(): lax.all_gather(wire[4], ('dp', 'fsdp'), axis=0, tiled=True)]
    dot_general x42 -> x1, matrix products: 107 us -> 0.16 us  [dot_right(): lax.dot_general(left, right, (((1,), (1,)), ((), ())), preferred_element_...]
    ppermute x0 -> x67, waiting for transfers between devices: none -> 91.4 us  [the longest x33 70.6 us: flip(): lax.ppermute(value, 'fsdp', [(i, i ^ mask) for i in range(self.fsdp)])]
    psum x2 -> x0, blocking collectives: 77.3 us -> none  [the longest x1 39.5 us: on_device(): lax.psum((col_parts[0], col_parts[1], col_parts[2], col_parts[3], row_tot...]
    dot_general x29 -> x0, matrix products: 76.8 us -> none  [dot_plain(): return jnp.dot(left, right, preferred_element_type=jnp.float32)]
    ppermute x0 -> x67, starting transfers between devices: none -> 75.5 us  [the longest x33 45.5 us: flip(): lax.ppermute(value, 'fsdp', [(i, i ^ mask) for i in range(self.fsdp)])]
    dot_general x30 -> x8, matrix products: 74.8 us -> 9.46 us  [dot_left(): lax.dot_general(left, right, (((0,), (0,)), ((), ())), preferred_element_...]
  transfers between devices with their start and end apart: 9 -> 71, of which waited for: 5 -> 29; matrix products, arithmetic and copies ran while one was open for 13% -> 29% of each run, Pallas kernels for 0% -> 3%
where the time goes in v1:
time: 363 us; the launch traced here: 361 us
  waiting for transfers between devices  99.2 us (27%)
  local copies, waits for them, and re-layouts  92.7 us (26%)
  starting transfers between devices  91.2 us (25%)
  other arithmetic  31.7 us (9%)
  Pallas kernels  22.7 us (6%)
  between operations  13.6 us (4%)
  matrix products  9.62 us (3%)
    ppermute x33, waiting for transfers between devices, flip(): lax.ppermute(value, 'fsdp', [(i, i ^ mask) for i in range(self.fsdp)])  70.6 us
    ppermute x33, starting transfers between devices, flip(): lax.ppermute(value, 'fsdp', [(i, i ^ mask) for i in range(self.fsdp)])  45.5 us
    ppermute x18, starting transfers between devices, turn(): lax.ppermute(value, 'fsdp', [(i, (i + 4 * step) % self.fsdp) for i in ran...  27.7 us
    unnamed x157, local copies, waits for them, and re-layouts  24.1 us
    dynamic_update_slice x29, local copies, waits for them, and re-layouts, stack_at(): out = lax.dynamic_update_index_in_dim(out, part, at, 0)  22.8 us
    ppermute x18, waiting for transfers between devices, turn(): lax.ppermute(value, 'fsdp', [(i, (i + 4 * step) % self.fsdp) for i in ran...  19.6 us
    all_to_all x4, starting transfers between devices, exchange(): return lax.all_to_all(blocks, AX, 0, 0, tiled=False)  15.7 us
    pallas_call x1, Pallas kernels, run_feed(): pl.pallas_call(functools.partial(feed_kernel, moves.depth, n), grid=(1,),...  10.1 us
  transfers between devices with their start and end apart: 71, of which 29 were waited for; matrix products, arithmetic and copies ran while one was open for 29% of the time, Pallas kernels for 3%

profile of v1, /device:TPU:0, one launch (start us, length us, event | category | flops | bytes accessed | tf_op | source)
XLA Modules:
  0.0 360.7 jit_solution(6765763608234279908)
XLA Ops:
  1.8 5.1 %collective-permute-start.26 = (bf16[96,768]{1,0:T(8,128)(2,1)S(1)}, bf16[96,768]{1,0:T(8,128)(2,1)}, u32[]{:S(2)}, u32[]{:S(2)}) collective-permute-start(bf16[96,768]{1,0:T(8,128)(2,1)S(1)} %convert_element_type.86), channel_id=1, source_target_pairs={{0,12},{1,13},{2,14},{3,15},{4,0},{5,1},{6,2},{7,3},{8,4},{9,5},{1... | collective-permute-start | bytes 442376 | tf_op jit(solution)/shard_map/ppermute | solution.py:43
  29.9 7.4 %collective-permute-done.33 = bf16[96,768]{1,0:T(8,128)(2,1)S(1)} collective-permute-done((bf16[96,768]{1,0:T(8,128)(2,1)}, bf16[96,768]{1,0:T(8,128)(2,1)S(1)}, u32[]{:S(2)}, u32[]{:S(2)}) %collective-permute-start.33) | collective-permute-done | bytes 147488 | tf_op jit(solution)/shard_map/ppermute | solution.py:40
  54.3 3.6 collective-permute-done.29
  60.1 5.4 %collective-permute-done.32 = bf16[192,768]{1,0:T(8,128)(2,1)S(1)} collective-permute-done((bf16[192,768]{1,0:T(8,128)(2,1)S(1)}, bf16[192,768]{1,0:T(8,128)(2,1)S(1)}, u32[]{:S(2)}, u32[]{:S(2)}) %collective-permute-start.32) | collective-permute-done | bytes 294944 | tf_op jit(solution)/shard_map/ppermute | solution.py:40
  67.5 5.0 %collective-permute-done.3 = bf16[48,3072]{1,0:T(8,128)(2,1)S(1)} collective-permute-done((bf16[48,3072]{1,0:T(8,128)(2,1)S(1)}, bf16[48,3072]{1,0:T(8,128)(2,1)S(1)}, u32[]{:S(2)}, u32[]{:S(2)}) %collective-permute-start.3) | collective-permute-done | bytes 294944 | tf_op jit(solution)/shard_map/ppermute | solution.py:40
  75.0 5.0 %collective-permute-done.15 = bf16[48,3072]{1,0:T(8,128)(2,1)S(1)} collective-permute-done((bf16[48,3072]{1,0:T(8,128)(2,1)S(1)}, bf16[48,3072]{1,0:T(8,128)(2,1)S(1)}, u32[]{:S(2)}, u32[]{:S(2)}) %collective-permute-start.15) | collective-permute-done | bytes 294944 | tf_op jit(solution)/shard_map/ppermute | solution.py:40
  83.0 3.7 %collective-permute-done.30 = bf16[192,768]{1,0:T(8,128)(2,1)S(1)} collective-permute-done((bf16[192,768]{1,0:T(8,128)(2,1)S(1)}, bf16[192,768]{1,0:T(8,128)(2,1)S(1)}, u32[]{:S(2)}, u32[]{:S(2)}) %collective-permute-start.30) | collective-permute-done | bytes 294944 | tf_op jit(solution)/shard_map/ppermute | solution.py:40
  95.6 5.5 %collective-permute-done.6 = bf16[48,3072]{1,0:T(8,128)(2,1)S(1)} collective-permute-done((bf16[48,3072]{1,0:T(8,128)(2,1)S(1)}, bf16[48,3072]{1,0:T(8,128)(2,1)S(1)}, u32[]{:S(2)}, u32[]{:S(2)}) %collective-permute-start.6) | collective-permute-done | bytes 294944 | tf_op jit(solution)/shard_map/ppermute | solution.py:43
  104.2 5.5 %collective-permute-done.18 = bf16[48,3072]{1,0:T(8,128)(2,1)S(1)} collective-permute-done((bf16[48,3072]{1,0:T(8,128)(2,1)S(1)}, bf16[48,3072]{1,0:T(8,128)(2,1)S(1)}, u32[]{:S(2)}, u32[]{:S(2)}) %collective-permute-start.18) | collective-permute-done | bytes 294944 | tf_op jit(solution)/shard_map/ppermute | solution.py:43
  112.0 7.1 %collective-permute-done.19 = bf16[48,3072]{1,0:T(8,128)(2,1)S(1)} collective-permute-done((bf16[48,3072]{1,0:T(8,128)(2,1)S(1)}, bf16[48,3072]{1,0:T(8,128)(2,1)S(1)}, u32[]{:S(2)}, u32[]{:S(2)}) %collective-permute-start.19) | collective-permute-done | bytes 294944 | tf_op jit(solution)/shard_map/ppermute | solution.py:40
  132.4 6.1 %attend.1 = (bf16[16,768]{1,0:T(8,128)(2,1)S(1)}, bf16[192,768]{1,0:T(8,128)(2,1)S(1)}, f32[192,864]{1,0:T(8,128)}, bf16[192,768]{1,0:T(8,128)(2,1)S(1)}, bf16[1...) custom-call(bf16[864,768]{1,0:T(8,128)(2,1)} %copy-done, ...), custom_call_target="tpu_custom_call" | custom-call | tf_op jit(solution)/shard_map/attend/pallas_call | solution.py:372
  140.0 10.1 %feed.1 = (bf16[16,3072]{1,0:T(8,128)(2,1)S(1)}, bf16[16,768]{1,0:T(8,128)(2,1)S(1)}, bf16[16,3072]{1,0:T(8,128)(2,1)S(1)}, bf16[16,768]{1,0:T(8,128)(2,1)S(1)},...) custom-call(f32[16,768]{1,0:T(8,128)S(1)} %get-tuple-element.53.y_re, ...), custom_call_target="tpu_custom_call" | custom-call | tf_op jit(solution)/shard_map/feed/pallas_call | solution.py:394
  150.8 3.7 %collective-permute-start.55 = (bf16[16,4096]{1,0:T(8,128)(2,1)}, bf16[16,4096]{1,0:T(8,128)(2,1)}, u32[]{:S(2)}, u32[]{:S(2)}) collective-permute-start(bf16[16,4096]{1,0:T(8,128)(2,1)} %fusion.15), channel_id=1, source_target_pairs={{0,12},{1,13},{2,14},{3,15},{4,0},{5,1},{6,2},{7,3},{8,4},{9,5},{1... | collective-permute-start | bytes 393224 | tf_op jit(solution)/shard_map/ppermute | solution.py:43
  157.1 4.9 %back.1 = (bf16[16,768]{1,0:T(8,128)(2,1)S(1)}, bf16[192,768]{1,0:T(8,128)(2,1)S(1)}, bf16[16,768]{1,0:T(8,128)(2,1)S(1)}, f32[8,768]{1,0:T(8,128)S(1)}) custom-call(bf16[864,768]{1,0:T(8,128)(2,1)S(1)} %copy-done.1, f32[864,768]{1,0:T(8,128)S(1)} %copy-done.3, f32[192,864]{1,0:T(8,128)S(1)} %copy-done.9, bf16[192,768]{1,0:T(8,128)(2,1)S(1)} %copy-done.21, ...), custom_call_target="tpu_custom_call" | custom-call | tf_op jit(solution)/shard_map/back/pallas_call | solution.py:423
  162.3 3.7 %concatenate.134 = bf16[12,16,32,24]{3,2,1,0:T(8,128)(2,1)} reshape(bf16[192,768]{1,0:T(8,128)(2,1)S(1)} %get-tuple-element.62) | data formatting | bytes 589824 | tf_op jit(solution)/shard_map/concatenate | solution.py:532
  171.9 4.3 %copy.89 = bf16[32,16,16,24]{3,2,1,0:T(8,128)(2,1)} copy(bf16[32,16,16,24]{3,0,1,2:T(8,128)(2,1)} %bitcast.295) | data formatting | bytes 786432 | tf_op jit(solution)/shard_map/transpose | solution.py:464
  176.2 4.1 %reshape.421 = bf16[32,16,384]{2,1,0:T(8,128)(2,1)} reshape(bf16[32,16,16,24]{3,2,1,0:T(8,128)(2,1)} %copy.89) | data formatting | bytes 786432 | tf_op jit(solution)/shard_map/reshape | solution.py:465
  180.3 3.9 %all-to-all-start.2 = ((bf16[32,16,384]{2,1,0:T(8,128)(2,1)}), bf16[32,16,384]{2,1,0:T(8,128)(2,1)S(1)}, u32[]{:S(2)}, u32[]{:S(2)}) async-start(bf16[32,16,384]{2,1,0:T(8,128)(2,1)} %reshape.421), calls=%async_computation.2 | async-start | bytes 786432 | tf_op jit(solution)/shard_map/all_to_all | solution.py:121
  184.3 3.7 %concatenate.114 = bf16[12,16,32,24]{3,2,1,0:T(8,128)(2,1)} reshape(bf16[192,768]{1,0:T(8,128)(2,1)S(1)} %copy-done.23) | data formatting | bytes 589824 | tf_op jit(solution)/shard_map/concatenate | solution.py:525
  199.8 4.3 %copy.85 = bf16[32,16,16,24]{3,2,1,0:T(8,128)(2,1)} copy(bf16[32,16,16,24]{3,0,1,2:T(8,128)(2,1)} %bitcast.294) | data formatting | bytes 786432 | tf_op jit(solution)/shard_map/transpose | solution.py:464
  204.0 4.1 %reshape.379 = bf16[32,16,384]{2,1,0:T(8,128)(2,1)} reshape(bf16[32,16,16,24]{3,2,1,0:T(8,128)(2,1)} %copy.85) | data formatting | bytes 786432 | tf_op jit(solution)/shard_map/reshape | solution.py:465
  259.4 13.6 %collective-permute-done.57 = bf16[4,16,4096]{2,1,0:T(8,128)(2,1)S(1)} collective-permute-done((bf16[4,16,4096]{2,1,0:T(8,128)(2,1)}, bf16[4,16,4096]{2,1,0:T(8,128)(2,1)S(1)}, u32[]{:S(2)}, u32[]{:S(2)}) %collective-permute-start.57) | collective-permute-done | bytes 524320 | tf_op jit(solution)/shard_map/ppermute | solution.py:40
  280.3 6.6 %all-to-all-start.1 = ((bf16[32,16,384]{2,1,0:T(8,128)(2,1)}), bf16[32,16,384]{2,1,0:T(8,128)(2,1)S(1)}, u32[]{:S(2)}, u32[]{:S(2)}) async-start(bf16[32,16,384]{2,1,0:T(8,128)(2,1)} %reshape.379), calls=%async_computation.1 | async-start | bytes 786432 | tf_op jit(solution)/shard_map/all_to_all | solution.py:121
  295.5 5.4 %all-to-all-done.1 = bf16[32,16,384]{2,1,0:T(8,128)(2,1)S(1)} async-done(((bf16[32,16,384]{2,1,0:T(8,128)(2,1)}), bf16[32,16,384]{2,1,0:T(8,128)(2,1)S(1)}, u32[]{:S(2)}, u32[]{:S(2)}) %all-to-all-start.1) | async-done | bytes 393248 | tf_op jit(solution)/shard_map/all_to_all | solution.py:121
  (450 shorter events, 215.4 us)
Async XLA Ops:
  1.8 26.1 %collective-permute-start.26 = (bf16[96,768]{1,0:T(8,128)(2,1)S(1)}, bf16[96,768]{1,0:T(8,128)(2,1)}, u32[]{:S(2)}, u32[]{:S(2)}) collective-permute-start(bf16[96,768]{1,0:T(8,128)(2,1)S(1)} %convert_element_type.86), channel_id=1, source_target_pairs={{0,12},{1,13},{2,14},{3,15},{4,0},{5,1},{6,2},{7,3},{8,4},{9,5},{1... | collective-permute-start | bytes 442376 | tf_op jit(solution)/shard_map/ppermute | solution.py:43
  6.9 22.4 %collective-permute-start.24 = (bf16[96,768]{1,0:T(8,128)(2,1)S(1)}, bf16[96,768]{1,0:T(8,128)(2,1)S(1)}, u32[]{:S(2)}, u32[]{:S(2)}) collective-permute-start(bf16[96,768]{1,0:T(8,128)(2,1)S(1)} %convert_element_type.86), channel_id=1, source_target_pairs={{0,2},{1,3},{2,0},{3,1},{4,6},{5,7},{6,4},{7,5},{8,10},{9,11},{10,... | collective-permute-start | bytes 442376 | tf_op jit(solution)/shard_map/ppermute | solution.py:40
  17.6 24.9 %all-to-all-start = ((bf16[32,24,128]{2,1,0:T(8,128)(2,1)}), bf16[32,24,128]{2,1,0:T(8,128)(2,1)S(1)}, u32[]{:S(2)}, u32[]{:S(2)}) async-start(bf16[32,24,128]{2,1,0:T(8,128)(2,1)} %broadcast_in_dim.183), calls=%async_computation | async-start | bytes 393216 | tf_op jit(solution)/shard_map/all_to_all | solution.py:121
  22.9 35.5 %collective-permute-start.2 = (bf16[48,3072]{1,0:T(8,128)(2,1)S(1)}, bf16[48,3072]{1,0:T(8,128)(2,1)S(1)}, u32[]{:S(2)}, u32[]{:S(2)}) collective-permute-start(bf16[48,3072]{1,0:T(8,128)(2,1)S(1)} %bitcast.324), channel_id=1, source_target_pairs={{0,4},{1,5},{2,6},{3,7},{4,8},{5,9},{6,10},{7,11},{8,12},{9,13},{1... | collective-permute-start | bytes 884744 | tf_op jit(solution)/shard_map/ppermute | solution.py:43
  24.7 20.9 %collective-permute-start.1 = (bf16[48,3072]{1,0:T(8,128)(2,1)S(1)}, bf16[48,3072]{1,0:T(8,128)(2,1)S(1)}, u32[]{:S(2)}, u32[]{:S(2)}) collective-permute-start(bf16[48,3072]{1,0:T(8,128)(2,1)S(1)} %bitcast.325), channel_id=1, source_target_pairs={{0,2},{1,3},{2,0},{3,1},{4,6},{5,7},{6,4},{7,5},{8,10},{9,11},{10,... | collective-permute-start | bytes 884744 | tf_op jit(solution)/shard_map/ppermute | solution.py:40
  26.3 41.1 %collective-permute-start.14 = (bf16[48,3072]{1,0:T(8,128)(2,1)S(1)}, bf16[48,3072]{1,0:T(8,128)(2,1)S(1)}, u32[]{:S(2)}, u32[]{:S(2)}) collective-permute-start(bf16[48,3072]{1,0:T(8,128)(2,1)S(1)} %bitcast.322), channel_id=1, source_target_pairs={{0,4},{1,5},{2,6},{3,7},{4,8},{5,9},{6,10},{7,11},{8,12},{9,13},{1... | collective-permute-start | bytes 884744 | tf_op jit(solution)/shard_map/ppermute | solution.py:43
  27.8 19.4 %collective-permute-start.13 = (bf16[48,3072]{1,0:T(8,128)(2,1)S(1)}, bf16[48,3072]{1,0:T(8,128)(2,1)S(1)}, u32[]{:S(2)}, u32[]{:S(2)}) collective-permute-start(bf16[48,3072]{1,0:T(8,128)(2,1)S(1)} %bitcast.323), channel_id=1, source_target_pairs={{0,1},{1,0},{2,3},{3,2},{4,5},{5,4},{6,7},{7,6},{8,9},{9,8},{10,11... | collective-permute-start | bytes 884744 | tf_op jit(solution)/shard_map/ppermute | solution.py:40
  44.3 38.7 %collective-permute-start.25 = (bf16[192,768]{1,0:T(8,128)(2,1)S(1)}, bf16[192,768]{1,0:T(8,128)(2,1)S(1)}, u32[]{:S(2)}, u32[]{:S(2)}) collective-permute-start(bf16[192,768]{1,0:T(8,128)(2,1)S(1)} %bitcast.310), channel_id=1, source_target_pairs={{0,1},{1,0},{2,3},{3,2},{4,5},{5,4},{6,7},{7,6},{8,9},{9,8},{10,11... | collective-permute-start | bytes 884744 | tf_op jit(solution)/shard_map/ppermute | solution.py:40
  58.5 52.1 %collective-permute-start.8 = (bf16[96,3072]{1,0:T(8,128)(2,1)S(1)}, bf16[96,3072]{1,0:T(8,128)(2,1)S(1)}, u32[]{:S(2)}, u32[]{:S(2)}) collective-permute-start(bf16[96,3072]{1,0:T(8,128)(2,1)S(1)} %bitcast.280), channel_id=1, source_target_pairs={{0,16},{16,0},{1,17},{17,1},{2,18},{18,2},{3,19},{19,3},{4,20},{20... | collective-permute-start | bytes 1769480 | tf_op jit(solution)/shard_map/ppermute | solution.py:48
  60.1 50.7 %collective-permute-start.20 = (bf16[96,3072]{1,0:T(8,128)(2,1)S(1)}, bf16[96,3072]{1,0:T(8,128)(2,1)S(1)}, u32[]{:S(2)}, u32[]{:S(2)}) collective-permute-start(bf16[96,3072]{1,0:T(8,128)(2,1)S(1)} %bitcast.288), channel_id=1, source_target_pairs={{0,16},{16,0},{1,17},{17,1},{2,18},{18,2},{3,19},{19,3},{4,20},{20... | collective-permute-start | bytes 1769480 | tf_op jit(solution)/shard_map/ppermute | solution.py:48
  83.0 37.0 %collective-permute-start.38 = (bf16[384,768]{1,0:T(8,128)(2,1)S(1)}, bf16[384,768]{1,0:T(8,128)(2,1)S(1)}, u32[]{:S(2)}, u32[]{:S(2)}) collective-permute-start(bf16[384,768]{1,0:T(8,128)(2,1)S(1)} %bitcast.301), channel_id=1, source_target_pairs={{0,16},{16,0},{1,17},{17,1},{2,18},{18,2},{3,19},{19,3},{4,20},{20... | collective-permute-start | bytes 1769480 | tf_op jit(solution)/shard_map/ppermute | solution.py:48
  120.0 19.8 %collective-permute-start.21 = (bf16[96,3072]{1,0:T(8,128)(2,1)}, bf16[96,3072]{1,0:T(8,128)(2,1)}, u32[]{:S(2)}, u32[]{:S(2)}) collective-permute-start(bf16[96,3072]{1,0:T(8,128)(2,1)} %bitcast.35.refs_1_), channel_id=1, source_target_pairs={{0,16},{16,0},{1,17},{17,1},{2,18},{18,2},{3,19},{19,3},{4,20},{20... | collective-permute-start | bytes 1769480 | tf_op jit(solution)/shard_map/ppermute | solution.py:48
  120.6 19.3 %collective-permute-start.36 = (bf16[384,768]{1,0:T(8,128)(2,1)}, bf16[384,768]{1,0:T(8,128)(2,1)}, u32[]{:S(2)}, u32[]{:S(2)}) collective-permute-start(bf16[384,768]{1,0:T(8,128)(2,1)} %bitcast.53.refs_9_), channel_id=1, source_target_pairs={{0,16},{16,0},{1,17},{17,1},{2,18},{18,2},{3,19},{19,3},{4,20},{20... | collective-permute-start | bytes 1769480 | tf_op jit(solution)/shard_map/ppermute | solution.py:48
  121.6 18.3 %collective-permute-start.35 = (bf16[384,768]{1,0:T(8,128)(2,1)}, bf16[384,768]{1,0:T(8,128)(2,1)}, u32[]{:S(2)}, u32[]{:S(2)}) collective-permute-start(bf16[384,768]{1,0:T(8,128)(2,1)} %bitcast.47.refs_8_), channel_id=1, source_target_pairs={{0,16},{16,0},{1,17},{17,1},{2,18},{18,2},{3,19},{19,3},{4,20},{20... | collective-permute-start | bytes 1769480 | tf_op jit(solution)/shard_map/ppermute | solution.py:48
  150.7 86.8 %collective-permute-start.53 = (bf16[16,4096]{1,0:T(8,128)(2,1)}, bf16[16,4096]{1,0:T(8,128)(2,1)}, u32[]{:S(2)}, u32[]{:S(2)}) collective-permute-start(bf16[16,4096]{1,0:T(8,128)(2,1)} %fusion.15), channel_id=1, source_target_pairs={{0,4},{1,5},{2,6},{3,7},{4,8},{5,9},{6,10},{7,11},{8,12},{9,13},{1... | collective-permute-start | bytes 393224 | tf_op jit(solution)/shard_map/ppermute | solution.py:43
  150.7 89.8 %collective-permute-start.54 = (bf16[16,4096]{1,0:T(8,128)(2,1)}, bf16[16,4096]{1,0:T(8,128)(2,1)}, u32[]{:S(2)}, u32[]{:S(2)}) collective-permute-start(bf16[16,4096]{1,0:T(8,128)(2,1)} %fusion.15), channel_id=1, source_target_pairs={{0,8},{1,9},{2,10},{3,11},{4,12},{5,13},{6,14},{7,15},{8,0},{9,1},... | collective-permute-start | bytes 393224 | tf_op jit(solution)/shard_map/ppermute | solution.py:43
  150.8 91.2 %collective-permute-start.55 = (bf16[16,4096]{1,0:T(8,128)(2,1)}, bf16[16,4096]{1,0:T(8,128)(2,1)}, u32[]{:S(2)}, u32[]{:S(2)}) collective-permute-start(bf16[16,4096]{1,0:T(8,128)(2,1)} %fusion.15), channel_id=1, source_target_pairs={{0,12},{1,13},{2,14},{3,15},{4,0},{5,1},{6,2},{7,3},{8,4},{9,5},{1... | collective-permute-start | bytes 393224 | tf_op jit(solution)/shard_map/ppermute | solution.py:43
  180.3 100.0 %all-to-all-start.2 = ((bf16[32,16,384]{2,1,0:T(8,128)(2,1)}), bf16[32,16,384]{2,1,0:T(8,128)(2,1)S(1)}, u32[]{:S(2)}, u32[]{:S(2)}) async-start(bf16[32,16,384]{2,1,0:T(8,128)(2,1)} %reshape.421), calls=%async_computation.2 | async-start | bytes 786432 | tf_op jit(solution)/shard_map/all_to_all | solution.py:121
  191.1 27.3 %collective-permute-start.39 = (bf16[16,2304]{1,0:T(8,128)(2,1)S(1)}, bf16[16,2304]{1,0:T(8,128)(2,1)S(1)}, u32[]{:S(2)}, u32[]{:S(2)}) collective-permute-start(bf16[16,2304]{1,0:T(8,128)(2,1)S(1)} %constant_dynamic-update-slice_fusion.4), channel_id=1, source_target_pairs={{0,4},{1,5},{2,6},{3,7},{4,8},{5,9},{6,10},{7,11},{8,12},{9,13},{1... | collective-permute-start | bytes 221192 | tf_op jit(solution)/shard_map/ppermute | solution.py:43
  247.3 25.6 %collective-permute-start.57 = (bf16[4,16,4096]{2,1,0:T(8,128)(2,1)}, bf16[4,16,4096]{2,1,0:T(8,128)(2,1)S(1)}, u32[]{:S(2)}, u32[]{:S(2)}) collective-permute-start(bf16[4,16,4096]{2,1,0:T(8,128)(2,1)} %bitcast_dynamic-update-slice_fusion.14), channel_id=1, source_target_pairs={{0,2},{1,3},{2,0},{3,1},{4,6},{5,7},{6,4},{7,5},{8,10},{9,11},{10,... | collective-permute-start | bytes 1572872 | tf_op jit(solution)/shard_map/ppermute | solution.py:40
  249.9 23.9 %collective-permute-start.58 = (bf16[4,16,4096]{2,1,0:T(8,128)(2,1)}, bf16[4,16,4096]{2,1,0:T(8,128)(2,1)S(1)}, u32[]{:S(2)}, u32[]{:S(2)}) collective-permute-start(bf16[4,16,4096]{2,1,0:T(8,128)(2,1)} %bitcast_dynamic-update-slice_fusion.14), channel_id=1, source_target_pairs={{0,3},{1,2},{2,1},{3,0},{4,7},{5,6},{6,5},{7,4},{8,11},{9,10},{10,... | collective-permute-start | bytes 1572872 | tf_op jit(solution)/shard_map/ppermute | solution.py:40
  254.4 39.7 %collective-permute-start.45 = (bf16[4,4,16,2304]{3,2,1,0:T(8,128)(2,1)}, bf16[4,4,16,2304]{3,2,1,0:T(8,128)(2,1)}, u32[]{:S(2)}, u32[]{:S(2)}) collective-permute-start(bf16[4,4,16,2304]{3,2,1,0:T(8,128)(2,1)} %bitcast.77), channel_id=1, source_target_pairs={{0,16},{16,0},{1,17},{17,1},{2,18},{18,2},{3,19},{19,3},{4,20},{20... | collective-permute-start | bytes 3538952 | tf_op jit(solution)/shard_map/ppermute | solution.py:48
  280.3 26.1 %collective-permute-start.59 = (bf16[4,4,16,4096]{3,2,1,0:T(8,128)(2,1)}, bf16[4,4,16,4096]{3,2,1,0:T(8,128)(2,1)}, u32[]{:S(2)}, u32[]{:S(2)}) collective-permute-start(bf16[4,4,16,4096]{3,2,1,0:T(8,128)(2,1)} %bitcast.110), channel_id=1, source_target_pairs={{0,16},{16,0},{1,17},{17,1},{2,18},{18,2},{3,19},{19,3},{4,20},{20... | collective-permute-start | bytes 6291464 | tf_op jit(solution)/shard_map/ppermute | solution.py:48
  280.3 20.6 %all-to-all-start.1 = ((bf16[32,16,384]{2,1,0:T(8,128)(2,1)}), bf16[32,16,384]{2,1,0:T(8,128)(2,1)S(1)}, u32[]{:S(2)}, u32[]{:S(2)}) async-start(bf16[32,16,384]{2,1,0:T(8,128)(2,1)} %reshape.379), calls=%async_computation.1 | async-start | bytes 786432 | tf_op jit(solution)/shard_map/all_to_all | solution.py:121
  (117 other events, 1698.2 us)

commit v2 on v1

v2 whole, which is shorter than its diff:
```python
import functools
import math

import jax
import jax.numpy as jnp
from jax import lax
from jax.experimental import pallas as pl
from jax.experimental.pallas import tpu as pltpu
from jax.sharding import PartitionSpec as P

D = 768
HEADS = 12
HDIM = 64
FF = 3072
GOALTOK = 64
ACTW = 28
TSTEPS = 20
STEP = 10
LANES = 128
SLOTS = 16
AX = ("dp", "fsdp")

rate_matrix = 0.05
rate_small = 0.3
clip_level = 0.5
BF = jnp.bfloat16
F32 = jnp.float32
MIB = 1024 * 1024


class Moves:
    def __init__(self, mesh):
        self.dp = mesh.shape["dp"]
        self.fsdp = mesh.shape["fsdp"]
        self.count = self.dp * self.fsdp
        self.fast = self.dp == 2 and self.fsdp == 16
        self.depth = self.fsdp // 4

    def flip(self, value, mask):
        return lax.ppermute(value, "fsdp", [(i, i ^ mask) for i in range(self.fsdp)])

    def turn(self, value, step):
        return lax.ppermute(
            value, "fsdp", [(i, (i + 4 * step) % self.fsdp) for i in range(self.fsdp)]
        )

    def swap(self, value):
        return lax.ppermute(value, "dp", [(0, 1), (1, 0)])

    def place(self):
        inner = lax.axis_index("fsdp")
        return lax.axis_index("dp"), inner // 4, (inner // 2) % 2, inner % 2


def pair(own, other, bit, blocks=1):
    rows, width = own.shape
    shaped = (blocks, rows // blocks, width)
    own, other = own.reshape(shaped), other.reshape(shaped)
    both = jnp.where(
        bit == 0, jnp.concatenate([own, other], 1), jnp.concatenate([other, own], 1)
    )
    return both.reshape(2 * rows, width)


def after(value, waits):
    if not waits:
        return value
    return lax.optimization_barrier((value,) + tuple(waits))[0]


def gather_weights(moves, attn, one, two):
    if not moves.fast:
        return [[lax.all_gather(w, AX, axis=0, tiled=True)] for w in (attn, one, two)]
    core, z, y, x = moves.place()
    sent = {"x": [], "y": [], "z": [], "c": []}
    move = {
        "x": lambda v: moves.flip(v, 1),
        "y": lambda v: moves.flip(v, 2),
        "z": lambda v: moves.turn(v, 1),
        "c": moves.swap,
    }

    def go(link, value):
        got = move[link](value)
        sent[link].append(got)
        return got

    cz1 = go("z", two)
    ax, by, cy0 = go("x", attn), go("y", one), go("y", two)
    a0, b0, c0 = pair(attn, ax, x), pair(one, by, y), pair(two, cy0, y)
    a1, b1 = go("z", a0), go("z", b0)
    bx0, ay0, cx0 = go("x", b0), go("y", a0), go("x", c0)
    am0, bm0, cm0 = pair(a0, ay0, y), pair(b0, bx0, x, 2), pair(c0, cx0, x, 2)
    am0s, bm0s, cm0s = go("c", am0), go("c", bm0), go("c", cm0)
    a2, cz2, b2 = go("z", a1), go("z", cz1), go("z", b1)
    ay1, cy1 = go("y", a1), go("y", cz1)
    c1 = pair(cz1, cy1, y)
    bx1, cx1 = go("x", b1), go("x", c1)
    am1, bm1, cm1 = pair(a1, ay1, y), pair(b1, bx1, x, 2), pair(c1, cx1, x, 2)
    am1s, bm1s, cm1s = go("c", am1), go("c", bm1), go("c", cm1)
    a3, cz3, b3 = go("z", a2), go("z", cz2), go("z", b2)
    ay2, cy2 = go("y", a2), go("y", cz2)
    c2 = pair(cz2, cy2, y)
    bx2, cx2 = go("x", b2), go("x", c2)
    am2 = pair(a2, ay2, y)
    am2s = go("c", am2)
    ay3, cy3 = go("y", a3), go("y", cz3)
    am3 = pair(a3, ay3, y)
    am3s = go("c", am3)
    bm2, cm2 = pair(b2, bx2, x, 2), pair(c2, cx2, x, 2)
    bm2s, cm2s = go("c", bm2), go("c", cm2)
    c3 = pair(cz3, cy3, y)
    cx3, bx3 = go("x", c3), go("x", b3)
    cm3, bm3 = pair(c3, cx3, x, 2), pair(b3, bx3, x, 2)
    cm3s, bm3s = go("c", cm3), go("c", bm3)
    return [
        [am0, am1, am2, am3, am0s, am1s, am2s, am3s],
        [bm0, bm1, bm2, bm3, bm0s, bm1s, bm2s, bm3s],
        [cm0, cm1, cm2, cm3, cm0s, cm1s, cm2s, cm3s],
    ]


def joined(parts):
    rows, width = parts[0].shape

    def body(*refs):
        for k, ref in enumerate(refs[:-1]):
            refs[-1][k * rows : (k + 1) * rows, :] = ref[...]

    return pl.pallas_call(
        body,
        out_shape=shape((rows * len(parts), width), parts[0].dtype),
        in_specs=[VMEM] * len(parts),
        out_specs=VMEM,
        compiler_params=pltpu.CompilerParams(vmem_limit_bytes=4 * MIB),
        name="joined",
    )(*parts)


def gather_z_first(moves, part, waits=()):
    held = joined([part] + [moves.turn(part, k) for k in range(1, moves.depth)])
    held = after(held, waits)
    return [held] + [moves.flip(held, k) for k in range(1, 4)]


def gather_z_last(moves, part, waits=()):
    held = [after(joined([part] + [moves.flip(part, k) for k in range(1, 4)]), waits)]
    for _ in range(moves.depth - 1):
        held.append(moves.turn(held[-1], 1))
    return held


def sources(depth, z_first):
    inner = lax.axis_index("fsdp")
    z, y, x = inner // 4, lax.rem(inner // 2, 2), lax.rem(inner, 2)
    out = []
    for k in range(4 * depth):
        step, flips = (k % depth, k // depth) if z_first else (k // 4, k % 4)
        at = lax.rem(z - step + depth, depth) * 4
        at = at + (1 - y if flips & 2 else y) * 2 + (1 - x if flips & 1 else x)
        out.append(at)
    return out


def exchange(moves, blocks):
    return lax.all_to_all(blocks, "fsdp" if moves.fast else AX, 0, 0, tiled=False)


def total(moves, value):
    if not moves.fast:
        return lax.psum(value, AX)
    value = value + moves.swap(value)
    value = (value + moves.flip(value, 1)) + (moves.flip(value, 2) + moves.flip(value, 3))
    return (value + moves.flip(value, 4)) + (moves.flip(value, 8) + moves.flip(value, 12))


def dot(left, right):
    return jnp.dot(left, right, preferred_element_type=F32)


def dot_right(left, right):
    return lax.dot_general(left, right, (((1,), (1,)), ((), ())), preferred_element_type=F32)


def dot_left(left, right):
    return lax.dot_general(left, right, (((0,), (0,)), ((), ())), preferred_element_type=F32)


def normal(h):
    mean = jnp.mean(h, -1, keepdims=True)
    centered = h - mean
    root = lax.rsqrt(jnp.mean(centered * centered, -1, keepdims=True) + 1e-06)
    return centered * root, root


def normal_back(grad, unit, root, gain):
    scaled = grad * gain
    return root * (
        scaled
        - jnp.mean(scaled, -1, keepdims=True)
        - unit * jnp.mean(scaled * unit, -1, keepdims=True)
    )


def spread(rows):
    read = rows.shape[0]
    tall = jnp.concatenate([rows.astype(F32)] * HEADS, 0)
    return jnp.where(own_head(read), tall, 0.0).astype(BF)


def own_head(read):
    row = lax.broadcasted_iota(jnp.int32, (HEADS * read, D), 0) // read
    lane = lax.broadcasted_iota(jnp.int32, (HEADS * read, D), 1) // HDIM
    return row == lane


def gathered(tall):
    read = tall.shape[0] // HEADS
    kept = jnp.where(own_head(read), tall, 0.0)
    out = kept[0:read]
    for head in range(1, HEADS):
        out = out + kept[head * read : (head + 1) * read]
    return out


def assemble(out_ref, parts, depth):
    if len(parts) == 1:
        out_ref[...] = parts[0][...]
        return
    core, z = lax.axis_index("dp"), lax.axis_index("fsdp") // 4
    rows = parts[0].shape[0]
    for k, part in enumerate(parts):
        half = core if k < depth else 1 - core
        block = half * depth + lax.rem(z - k % depth + depth, depth)
        out_ref[pl.ds(pl.multiple_of(block * rows, rows), rows), :] = part[...]


def square_eye(n):
    row = lax.broadcasted_iota(jnp.int32, (n, n), 0)
    return row == lax.broadcasted_iota(jnp.int32, (n, n), 1)


def column(row):
    return jnp.sum(jnp.where(square_eye(row.shape[1]), row, 0.0), 1, keepdims=True)


def as_row(col):
    return jnp.sum(jnp.where(square_eye(col.shape[0]), col, 0.0), 0, keepdims=True)


def pack_blocks(slots, out_ref, own, width):
    inner, read, _ = out_ref.shape
    cores = D // own // inner
    width = width // cores
    tiles = D // LANES
    lane = lax.broadcasted_iota(jnp.int32, (read, LANES), 1)
    moved = [pltpu.roll(v, own * k, 1) if k else v for k, v in enumerate(slots)]
    for d in range(cores * inner):
        base = own * d
        shift = base % LANES
        held = []
        for tile in range(base // LANES, base // LANES + pl.cdiv(shift + width, LANES)):
            low = tile * LANES - base
            at = (tile % tiles) * LANES
            first = min(max(low, 0) // own, len(slots) - 1)
            last = min(min(low + LANES, width) - 1, len(slots) * own - 1) // own
            part = moved[first][:, at : at + LANES]
            for k in range(first + 1, last + 1):
                part = jnp.where(lane >= k * own - low, moved[k][:, at : at + LANES], part)
            held.append(part)
        block = jnp.concatenate(held, 1)
        if shift:
            block = pltpu.roll(block, len(held) * LANES - shift, 1)
        start = d // inner * width
        out_ref[d % inner, :, start : start + width] = block[:, :width].astype(BF)


def pack_columns(value, out_ref, own):
    inner, read, _ = out_ref.shape
    tiles = value.shape[1] // LANES
    for d in range(value.shape[1] // own):
        tile, shift = own * d // LANES, own * d % LANES
        first = value[:, tile * LANES : (tile + 1) * LANES]
        if shift:
            at = (tile + 1) % tiles * LANES
            both = jnp.concatenate([first, value[:, at : at + LANES]], 1)
            first = pltpu.roll(both, 2 * LANES - shift, 1)[:, :LANES]
        start = d // inner * LANES
        out_ref[d % inner, :, start : start + LANES] = first.astype(BF)


def head_slots(tall, read):
    return [tall[k * read : (k + 1) * read].astype(F32) for k in range(HEADS)]


def wire_kernel(
    act_ref, qkv_ref, out_ref, one_ref, two_ref, table_ref, small_ref, attn_ref, one_low, two_low
):
    own = qkv_ref.shape[0]
    attn_ref[:, 0 : 3 * D] = qkv_ref[...].astype(BF)
    attn_ref[:, 3 * D : 4 * D] = out_ref[...].astype(BF)
    marks = jnp.sum(act_ref[...].astype(F32), 1, keepdims=True)
    first = lax.broadcasted_iota(jnp.int32, (own, 1), 0) == 0
    parts = [table_ref[...]] + [column(small_ref[k : k + 1, :]) for k in range(6)]
    parts += [jnp.where(first, marks, 0.0), jnp.zeros((own, LANES - ACTW - 7), F32)]
    attn_ref[:, 4 * D :] = jnp.concatenate(parts, 1).astype(BF)
    one_low[...] = one_ref[...].astype(BF)
    two_low[...] = two_ref[...].astype(BF)


def norm_kernel(depth, n, tok_ref, noisy_ref, temb_ref, *refs):
    parts = refs[:n]
    a_ref, unit_ref, last_ref, gain_ref, count_ref, w_ref, h_ref = refs[n:]
    assemble(w_ref, parts, depth)
    seq, read = tok_ref.shape[0], noisy_ref.shape[0]
    rows = h_ref.shape[0]
    table = w_ref[:, 4 * D :]
    pick = lax.broadcasted_iota(jnp.int32, (8, LANES), 1) - ACTW
    pick = pick == lax.broadcasted_iota(jnp.int32, (8, LANES), 0)
    gains = dot_right(jnp.where(pick, 1.0, 0.0).astype(BF), table)
    gain_ref[...] = gains
    count_ref[...] = read * jnp.sum(gains[6:7, :], 1, keepdims=True)
    embed = dot_right(noisy_ref[...], table)
    last = tok_ref[seq - read :, :].astype(F32) + (embed + temb_ref[...])
    last_ref[...] = last
    for start in range(0, seq, rows):
        h_ref[...] = tok_ref[start : start + rows, :].astype(F32)
        if start + rows == seq:
            h_ref[rows - read :, :] = last
        unit, _ = normal(h_ref[...])
        unit_ref[start : start + rows, :] = unit
        a_ref[start : start + rows, :] = (unit * gains[0:1, :] + gains[1:2, :]).astype(BF)


def attend_kernel(packs, a_ref, last_ref, gain_ref, seen_ref, noisy_ref, w_ref, *refs):
    q_ref, qk_ref, p_ref, pa_ref, o_ref, y_ref, a2_ref = refs[:7]
    seq = a_ref.shape[0]
    read = last_ref.shape[0]
    a = a_ref[...]
    q = dot(a_ref[seq - read :, :], w_ref[:, 0:D]).astype(BF)
    q_ref[:, 0:D] = q
    q_ref[:, D:] = noisy_ref[...]
    qk = (dot_right(spread(q), w_ref[:, D : 2 * D]) * HDIM ** (-0.5)).astype(BF)
    qk_ref[...] = qk
    scores = dot_right(qk, a)
    seen = jnp.concatenate([seen_ref[...]] * HEADS, 0)
    scores = jnp.where(seen > 0.5, scores, -1000000000.0)
    top = jnp.max(scores, -1, keepdims=True)
    grown = jnp.exp(scores - top)
    probs = grown / jnp.sum(grown, -1, keepdims=True)
    p_ref[...] = probs
    pa = dot(probs.astype(BF), a).astype(BF)
    pa_ref[...] = pa
    o = gathered(dot(pa, w_ref[:, 2 * D : 3 * D])).astype(BF)
    o_ref[...] = o
    y = last_ref[...] + dot(o, w_ref[:, 3 * D : 4 * D])
    y_ref[...] = y
    unit, _ = normal(y)
    a2 = (unit * gain_ref[2:3, :] + gain_ref[3:4, :]).astype(BF)
    a2_ref[...] = a2
    if packs:
        slots = head_slots(pa, read)
        slots += [v.astype(F32) for v in (o, a_ref[seq - read :, :], a2)]
        pack_blocks(slots, refs[7], D // packs, refs[7].shape[2])


def feed_kernel(
    depth, n, packs, y_ref, a2_ref, gain_ref, count_ref, noise_ref, mask_ref, w_ref, *refs
):
    (
        m_ref, du_ref, two_ref, f_ref, dy_ref, do_ref, small_ref, loss_ref, one, two,
    ) = refs[2 * n :]
    assemble(one, refs[:n], depth)
    assemble(two, refs[n : 2 * n], depth)
    y = y_ref[...]
    a2 = a2_ref[...]
    u = dot(a2, one[...])
    root_two = math.sqrt(2.0 / math.pi)
    curve = jnp.tanh(root_two * (u + 0.044715 * (u * u * u)))
    half = 0.5 * (1.0 + curve)
    m = (u * half).astype(BF)
    slope = half + 0.5 * u * (1.0 - curve * curve) * (root_two * (1.0 + 3.0 * 0.044715 * (u * u)))
    if packs:
        pack_columns(m.astype(F32), m_ref, FF // packs)
    else:
        m_ref[...] = m
    h2 = y + dot(m, two[...])
    unit3, root3 = normal(h2)
    gain2, gain3 = gain_ref[2:3, :], gain_ref[4:5, :]
    f = (unit3 * gain3 + gain_ref[5:6, :]).astype(BF)
    f_ref[...] = f
    table = w_ref[:, 4 * D :].astype(F32)
    lane = lax.broadcasted_iota(jnp.int32, table.shape, 1)
    table = jnp.where(lane < ACTW, table, 0.0).astype(BF)
    e = dot(f, table) - noise_ref[...]
    mask = mask_ref[...]
    loss_ref[...] = jnp.sum(jnp.sum(mask * e * e, 1, keepdims=True), 0, keepdims=True)
    de = ((1.0 / count_ref[...]) * 2.0 * mask * e).astype(BF)
    two_ref[:, 3 * D :] = de
    df = dot_right(de, table)
    dh2 = normal_back(df, unit3, root3, gain3)
    dz = dh2.astype(BF)
    two_ref[:, 0:D] = dz
    du = (slope * dot_right(dz, two[...])).astype(BF)
    du_ref[...] = du
    da2 = dot_right(du, one[...])
    unit2, root2 = normal(y)
    dy = dh2 + normal_back(da2, unit2, root2, gain2)
    dy_ref[...] = dy
    da = dy.astype(BF)
    two_ref[:, D : 2 * D] = da
    do = dot_right(da, w_ref[:, 3 * D : 4 * D]).astype(BF)
    two_ref[:, 2 * D : 3 * D] = do
    do_ref[...] = do
    small_ref[...] = jnp.concatenate(
        [
            jnp.zeros((2, D), F32),
            jnp.sum(da2 * unit2, 0, keepdims=True),
            jnp.sum(da2, 0, keepdims=True),
            jnp.sum(df * unit3, 0, keepdims=True),
            jnp.sum(df, 0, keepdims=True),
            jnp.zeros((2, D), F32),
        ],
        0,
    )


def back_kernel(
    packs, a_ref, unit_ref, p_ref, qk_ref, do_ref, dy_ref, last_ref, gain_ref, f_ref, up_ref, w_ref,
    m_ref, q_ref, *refs,
):
    if packs:
        early_ref, *refs = refs
    dq_ref, *refs = refs
    da_ref = refs[-1]
    seq = a_ref.shape[0]
    read = dy_ref.shape[0]
    a = a_ref[...]
    probs = p_ref[...]
    dv = dot_right(spread(do_ref[...]), w_ref[:, 2 * D : 3 * D]).astype(BF)
    dp = dot_right(dv, a)
    ds = (probs * (dp - jnp.sum(dp * probs, -1, keepdims=True))).astype(BF)
    dsa = dot(ds, a).astype(BF)
    dq = (gathered(dot(dsa, w_ref[:, D : 2 * D])) * HDIM ** (-0.5)).astype(BF)
    dq_ref[:, 0:D] = dq
    dq_ref[:, D:] = q_ref[...]
    da_ref[...] = dot_left(ds, qk_ref[...]) + dot_left(probs.astype(BF), dv)
    da_ref[seq - read :, :] = da_ref[seq - read :, :] + dot_right(dq, w_ref[:, 0:D])
    unit, root = normal(last_ref[...])
    dh = dy_ref[...] + normal_back(da_ref[seq - read :, :], unit, root, gain_ref[0:1, :])
    demb = dh.astype(BF)
    da = da_ref[...]
    low = [jnp.sum(da * unit_ref[...], 0, keepdims=True), jnp.sum(da, 0, keepdims=True)]
    sums = jnp.concatenate(low + [up_ref[2:6, :]], 0)
    high = sums.astype(BF).astype(F32)
    split = jnp.concatenate([high, sums - high, jnp.zeros((read - 12, D), F32)], 0)
    if packs:
        slots = head_slots(dsa, read)
        slots += [f_ref[...].astype(F32), demb.astype(F32), split]
        width = early_ref.shape[2]
        pack_blocks(slots, refs[0], D // packs, width)
        refs[0][:, :, width : 2 * width] = early_ref[...]
        refs[0][:, :, 2 * width :] = m_ref[...]
    else:
        dsa_ref, demb_ref, split_ref = refs[:3]
        dsa_ref[...] = dsa
        demb_ref[...] = demb
        split_ref[...] = split.astype(BF)


def own_rows(out_ref, got_ref, order, read, base=0):
    core = lax.axis_index("dp")
    width = out_ref.shape[2]
    for side in range(2):
        start = base + (core if side == 0 else 1 - core) * width
        lanes = pl.ds(pl.multiple_of(start, LANES), width)
        for k, source in enumerate(order):
            rows = pl.ds(pl.multiple_of(source * read, read), read)
            out_ref[side, k * read : (k + 1) * read, :] = got_ref[rows, lanes]


def fill(out_ref, refs):
    rows = refs[0].shape[0]
    for k, ref in enumerate(refs):
        out_ref[k * rows : (k + 1) * rows, :] = ref[...]


def head_blocks(tall, own):
    lane = lax.broadcasted_iota(jnp.int32, (own, D), 1) // HDIM
    out = tall[0:own]
    for head in range(1, HEADS):
        out = jnp.where(lane == head, tall[head * own : (head + 1) * own], out)
    return out


def statistics(grad, rows_old):
    beta = 1.0 - float(STEP) ** (-0.8)
    squares = grad * grad
    rows = beta * rows_old + (1.0 - beta) * jnp.sum(squares, 1, keepdims=True)
    return rows, jnp.sum(squares, 0, keepdims=True), jnp.sum(squares / rows, 0, keepdims=True)


def upper_kernel(
    depth, own, got_ref, *refs
):
    one_refs, two_refs = refs[:4], refs[4:8]
    mine_ref, theirs_ref, early, turned, mid, one, two = refs[8:]
    read = got_ref.shape[0] // (4 * depth)
    own_two = FF // (D // own)
    width = 2 * SLOTS * own
    own_rows(early, got_ref, sources(depth, True), read, width)
    own_rows(turned, got_ref, sources(depth, False), read, width)
    own_rows(mid, got_ref, sources(depth, False), read, 2 * width)
    fill(one, one_refs)
    fill(two, two_refs)
    at = HEADS * own - 256
    for side, out_ref in enumerate((mine_ref, theirs_ref)):
        out_ref[0:own_two, :] = dot_left(mid[side], two[:, 0:D])[:own_two]
        tail = turned[side, :, 256:384]
        start = own_two
        out_ref[start : start + own, :] = dot_left(tail, two[:, D : 2 * D])[at : at + own]
        start = start + own
        tall = dot_left(turned[side], two[:, 2 * D : 3 * D])
        out_ref[start : start + own, :] = head_blocks(tall, own)
        tail = early[side, :, 256:384]
        for k in range(FF // D):
            start = start + own
            part = dot_left(tail, one[:, k * D : (k + 1) * D])
            out_ref[start : start + own, :] = part[at + 2 * own : at + 3 * own]


def upper_sum_kernel(
    mine_ref, got_ref, r_one_ref, r_two_ref, r_out_ref,
    g_one_ref, n_one_ref, g_two_ref, n_two_ref, g_out_ref, n_out_ref, g_v_ref, stat_ref,
):
    own, own_two = g_one_ref.shape[0], g_two_ref.shape[0]
    both = mine_ref[...] + got_ref[...]
    g_two = both[0:own_two]
    at = own_two
    g_out = both[at : at + own]
    g_v_ref[...] = both[at + own : at + 2 * own]
    at = at + 2 * own
    g_one = jnp.concatenate([both[at + k * own : at + (k + 1) * own] for k in range(FF // D)], 1)
    g_out_ref[...] = g_out
    g_one_ref[...] = g_one
    g_two_ref[...] = g_two
    n_out, c_out, t_out = statistics(g_out, column(r_out_ref[...]))
    n_one, c_one, t_one = statistics(g_one, column(r_one_ref[...]))
    n_two, c_two, t_two = statistics(g_two, column(r_two_ref[...]))
    n_out_ref[...] = as_row(n_out)
    n_one_ref[...] = as_row(n_one)
    n_two_ref[...] = as_row(n_two)
    stat_ref[...] = jnp.zeros_like(stat_ref)
    stat_ref[0:1, :] = c_one
    stat_ref[1:2, :] = t_one
    stat_ref[2:3, :] = jnp.concatenate([c_out, t_out, c_two, t_two], 1)
    lane = lax.broadcasted_iota(jnp.int32, (1, LANES), 1)
    singles = jnp.where(lane == 1, jnp.sum(n_out), 0.0)
    singles = jnp.where(lane == 2, jnp.sum(n_one), singles)
    stat_ref[3:4, 3 * D : 3 * D + LANES] = jnp.where(lane == 3, jnp.sum(n_two), singles)


def lower_kernel(depth, own, got_ref, *refs):
    dq_refs, two_refs = refs[:4], refs[4:8]
    mine_ref, theirs_ref, early, late, turned, low, de = refs[8:]
    read = got_ref.shape[0] // (4 * depth)
    own_rows(early, got_ref, sources(depth, True), read, 2 * SLOTS * own)
    own_rows(late, got_ref, sources(depth, True), read)
    own_rows(turned, got_ref, sources(depth, False), read)
    fill(low, dq_refs)
    dq, q = low.at[:, 0:D], low.at[:, D:]
    rows = two_refs[0].shape[0]
    for k, ref in enumerate(two_refs):
        de[k * rows : (k + 1) * rows, :] = ref[:, 3 * D :]
    at = HEADS * own - 256
    count = de.shape[0]
    row = lax.rem(lax.broadcasted_iota(jnp.int32, (count, LANES), 0), read)
    lane = lax.broadcasted_iota(jnp.int32, (count, LANES), 1)
    pick = jnp.where((row == lane) | (row == lane + 6), 1.0, 0.0)
    pick = jnp.where(lane < 6, pick, 0.0).astype(BF)
    for side, out_ref in enumerate((mine_ref, theirs_ref)):
        tail = early[side, :, 256:384]
        out_ref[:, 0:D] = dot_left(tail, dq[...])[at + own : at + 2 * own]
        tall = dot_left(late[side], q[:, 0:D])
        out_ref[:, D : 2 * D] = head_blocks(tall, own) * HDIM ** (-0.5)
        tail = late[side, :, 256:384]
        table = dot_left(turned[side, :, 256:384], de[...])[at : at + own]
        table = table + dot_left(tail, q[:, D:])[at + own : at + 2 * own]
        out_ref[:, 2 * D : 2 * D + LANES] = table
        out_ref[:, 2 * D + LANES :] = dot_left(pick, tail)[:own]


def lower_sum_kernel(
    mine_ref, got_ref, g_v_ref, stat_in_ref, loss_ref, r_qkv_ref, var_table_ref, var_small_ref,
    g_qkv_ref, n_qkv_ref, g_table_ref, n_table_ref, u_table_ref, g_small_ref, n_small_ref,
    u_small_ref, stat_ref,
):
    both = mine_ref[...] + got_ref[...]
    g_table = both[:, 2 * D : 2 * D + ACTW]
    own = g_v_ref.shape[0]
    at = 2 * D + LANES + (HEADS + 2) * own - 256
    g_small = both[0:6, at : at + own]
    g_qkv = jnp.concatenate([both[:, 0 : 2 * D], g_v_ref[...]], 1)
    g_qkv_ref[...] = g_qkv
    n_qkv, c_qkv, t_qkv = statistics(g_qkv, column(r_qkv_ref[...]))
    n_qkv_ref[...] = as_row(n_qkv)
    beta = 1.0 - float(STEP) ** (-0.8)
    plain = jnp.zeros((), F32)
    for grad, old_ref, g_ref, n_ref, u_ref in (
        (g_table, var_table_ref, g_table_ref, n_table_ref, u_table_ref),
        (g_small, var_small_ref, g_small_ref, n_small_ref, u_small_ref),
    ):
        new = beta * old_ref[...] + (1.0 - beta) * grad * grad
        unit = grad * lax.rsqrt(new)
        g_ref[...] = grad
        n_ref[...] = new
        u_ref[...] = unit
        plain = plain + jnp.sum(unit * unit)
    stat_ref[...] = stat_in_ref[...]
    stat_ref[3:4, 0 : 3 * D] = c_qkv
    stat_ref[4:5, 0 : 3 * D] = t_qkv
    lane = lax.broadcasted_iota(jnp.int32, (1, LANES), 1)
    singles = stat_in_ref[3:4, 3 * D : 3 * D + LANES]
    singles = jnp.where(lane == 0, jnp.sum(n_qkv), singles)
    singles = jnp.where(lane == 4, plain, singles)
    stat_ref[3:4, 3 * D : 3 * D + LANES] = jnp.where(lane == 5, loss_ref[...], singles)


def flat(square):
    return jnp.concatenate([square[k : k + 1, :] for k in range(square.shape[0])], 1)


def folded(row):
    return jnp.concatenate(
        [row[:, k * LANES : (k + 1) * LANES] for k in range(row.shape[1] // LANES)], 0
    )


def renew_kernel(
    entries, stat_ref, *refs,
):
    ins, outs = refs[: 20], refs[20:]
    beta = 1.0 - float(STEP) ** (-0.8)
    c_qkv, t_qkv = stat_ref[3:4, 0 : 3 * D], stat_ref[4:5, 0 : 3 * D]
    c_one, t_one = stat_ref[0:1, :], stat_ref[1:2, :]
    c_out, t_out = stat_ref[2:3, 0:D], stat_ref[2:3, D : 2 * D]
    c_two, t_two = stat_ref[2:3, 2 * D : 3 * D], stat_ref[2:3, 3 * D :]
    at = 3 * D
    squares = stat_ref[3:4, at + 4 : at + 5]
    news = []
    for k, (c, t) in enumerate(
        ((c_qkv, t_qkv), (c_out, t_out), (c_one, t_one), (c_two, t_two))
    ):
        old_ref = ins[4 * k]
        whole = stat_ref[3:4, at + k : at + k + 1]
        new = beta * flat(old_ref[...]) + (1.0 - beta) * c
        squares = squares + whole * jnp.sum(t / new, 1, keepdims=True)
        news.append((new, whole))
    clip = jnp.sqrt(squares / entries)
    factor = 1.0 / jnp.maximum(1.0, clip / clip_level)
    for k, (new, whole) in enumerate(news):
        _, rows_ref, grad_ref, master_ref = ins[4 * k : 4 * k + 4]
        unit = grad_ref[...] * lax.rsqrt(column(rows_ref[...]) * new / whole)
        outs[2 * k][...] = folded(new)
        outs[2 * k + 1][...] = master_ref[...] - rate_matrix * unit * factor
    unit_ref, master_ref = ins[16:18]
    outs[8][...] = master_ref[...] - rate_matrix * unit_ref[...] * factor
    unit_ref, master_ref = ins[18:20]
    outs[9][...] = master_ref[...] - rate_small * unit_ref[...] * factor
    outs[10][...] = stat_ref[3:4, at + 5 : at + 6]
    outs[11][...] = clip


VMEM = pl.BlockSpec(memory_space=pltpu.VMEM)


def shape(dims, dtype):
    return jax.ShapeDtypeStruct(dims, dtype)


def params(mib):
    return pltpu.CompilerParams(vmem_limit_bytes=mib * MIB)


def call(kernel, name, mib, ins, outs, scratch=(), specs=None):
    return pl.pallas_call(
        kernel,
        out_shape=tuple(shape(*out) for out in outs),
        in_specs=specs or [VMEM] * len(ins),
        out_specs=(VMEM,) * len(outs),
        scratch_shapes=[pltpu.VMEM(*one) for one in scratch],
        compiler_params=pltpu.CompilerParams(vmem_limit_bytes=mib * MIB),
        name=name,
    )(*ins)


def run_wire(act_mask, w_qkv, w_out, w_one, w_two, w_table, small):
    own = w_qkv.shape[0]
    outs = [((own, 4 * D + LANES), BF), (w_one.shape, BF), (w_two.shape, BF)]
    ins = (act_mask, w_qkv, w_out, w_one, w_two, w_table, small.T)
    return call(wire_kernel, "wire", 60, ins, outs)


def run_norm(moves, tokens, noisy, temb, parts):
    seq, read = tokens.shape[0], noisy.shape[0]
    outs = [((seq, D), BF), ((seq, D), F32), ((read, D), F32), ((8, D), F32), ((1, 1), F32)]
    outs.append(((D, parts[0].shape[1]), BF))
    kernel = functools.partial(norm_kernel, moves.depth, len(parts))
    ins = (tokens, noisy, temb, *parts)
    return call(kernel, "norm_tokens", 20, ins, outs, [((seq // 6, D), F32)])


def run_attend(moves, normed, last, gains, seen, noisy, weights):
    seq, read = normed.shape[0], last.shape[0]
    tall = HEADS * read
    outs = [
        ((read, D + LANES), BF),
        ((tall, D), BF),
        ((tall, seq), F32),
        ((tall, D), BF),
        ((read, D), BF),
        ((read, D), F32),
        ((read, D), BF),
    ]
    packs = moves.count if moves.fast else 0
    if packs:
        outs.append(((moves.fsdp, read, moves.dp * SLOTS * D // packs), BF))
    ins = (normed, last, gains, seen, noisy, weights)
    return call(functools.partial(attend_kernel, packs), "attend", 14, ins, outs)


def run_feed(moves, y, a2, gains, count, noise, mask, weights, one, two):
    read = y.shape[0]
    packs = moves.count if moves.fast else 0
    outs = [
        ((moves.fsdp, read, moves.dp * LANES) if packs else (read, FF), BF),
        ((read, FF), BF),
        ((read, 3 * D + LANES), BF),
        ((read, D), BF),
        ((read, D), F32),
        ((read, D), BF),
        ((8, D), F32),
        ((1, 1), F32),
    ]
    ins = (y, a2, gains, count, noise, mask, weights, *one, *two)
    kernel = functools.partial(feed_kernel, moves.depth, len(one), packs)
    return call(kernel, "feed", 24, ins, outs, [((D, FF), BF), ((FF, D), BF)])


def run_back(moves, normed, unit, probs, qk, do, dy, last, gains, f, sums, weights, *more):
    seq, read = normed.shape[0], dy.shape[0]
    packs = moves.count if moves.fast else 0
    outs = [((read, 2 * D + LANES), BF)]
    if packs:
        outs.append(((moves.fsdp, read, moves.dp * (2 * SLOTS * D // packs + LANES)), BF))
    else:
        outs += [((HEADS * read, D), BF), ((read, D), BF), ((read, D), BF)]
    ins = (normed, unit, probs, qk, do, dy, last, gains, f, sums, weights, *more)
    return call(functools.partial(back_kernel, packs), "back", 16, ins, outs, [((seq, D), F32)])


def run_upper(moves, got, one, two, own):
    rows = got.shape[0]
    outs = [((6 * own + FF // moves.count, D), F32)] * 2
    scratch = [
        ((2, rows, SLOTS * own), BF),
        ((2, rows, SLOTS * own), BF),
        ((2, rows, LANES), BF),
        ((rows, one[0].shape[1]), BF),
        ((rows, two[0].shape[1]), BF),
    ]
    kernel = functools.partial(upper_kernel, moves.depth, own)
    return call(kernel, "upper_grads", 16, (got, *one, *two), outs, scratch)


def run_upper_sum(mine, got, r_one, r_two, r_out):
    own, own_two = r_one.shape[0], r_two.shape[0]
    outs = [
        ((own, FF), F32),
        ((1, own), F32),
        ((own_two, D), F32),
        ((1, own_two), F32),
        ((own, D), F32),
        ((1, own), F32),
        ((own, D), F32),
        ((8, FF), F32),
    ]
    ins = (mine, got, r_one[None, :], r_two[None, :], r_out[None, :])
    return call(upper_sum_kernel, "upper_sums", 16, ins, outs)


def run_lower(moves, got, dq, two, own):
    rows = got.shape[0]
    outs = [((own, 2 * D + 2 * LANES), F32)] * 2
    scratch = [((2, rows, SLOTS * own), BF)] * 3 + [((rows, dq[0].shape[1]), BF), ((rows, LANES), BF)]
    kernel = functools.partial(lower_kernel, moves.depth, own)
    return call(kernel, "lower_grads", 12, (got, *dq, *two), outs, scratch)


def run_lower_sum(mine, got, g_v, stats, loss, r_qkv, var_table, var_small):
    own = r_qkv.shape[0]
    table, small = ((own, ACTW), F32), ((6, own), F32)
    outs = [((own, 3 * D), F32), ((1, own), F32)] + [table] * 3 + [small] * 3
    outs.append((stats.shape, F32))
    ins = (mine, got, g_v, stats, loss, r_qkv[None, :], var_table, var_small)
    return call(lower_sum_kernel, "lower_sums", 16, ins, outs)


def run_renew(stats, mats, plain):
    ins, outs = [stats], []
    for cols, rows, grad, master in mats:
        ins += [cols.reshape(-1, LANES), rows, grad, master]
        outs += [((cols.shape[0] // LANES, LANES), F32), (master.shape, F32)]
    for update, master in plain:
        ins += [update, master]
        outs.append((master.shape, F32))
    outs += [((1, 1), F32)] * 2
    entries = float(4 * D * D + 2 * D * FF + D * ACTW + 6 * D)
    return call(functools.partial(renew_kernel, entries), "renew", 60, ins, outs)


def condition(actions, noise, tstep, width):
    frac = (tstep.astype(F32) / TSTEPS + 0.008) / 1.008
    alpha_bar = jnp.cos(frac * (math.pi / 2)) ** 2
    noisy = jnp.sqrt(alpha_bar) * actions + jnp.sqrt(1.0 - alpha_bar) * noise
    half = width // 2
    freq = jnp.exp(jnp.arange(half).astype(F32) * (-math.log(10000.0) / half))
    angle = tstep.astype(F32) * freq
    return (noisy, jnp.concatenate([jnp.sin(angle), jnp.cos(angle)]))


def visible_last(groups, task_mask, goal_flag, read):
    seq = groups.shape[0]
    task = task_mask.shape[0]
    places = jnp.arange(seq)
    task_pad = jnp.pad(task_mask, (0, seq - task)) * (1 - goal_flag)
    valid = jnp.where(places < task, task_pad, jnp.where(places < task + GOALTOK, goal_flag, 1))
    seen = (groups[None, :] <= groups[seq - read :, None]) & (valid[None, :] > 0)
    seen = seen | (places[seq - read :, None] == places[None, :])
    return seen.astype(F32)


def to_owners(slots, count):
    kinds, read, width = slots.shape
    own = width // count
    blocks = slots.reshape(kinds, read, count, own).transpose(2, 1, 0, 3)
    return blocks.reshape(count, read, kinds * own)


def lanes_to(value, width):
    return jnp.pad(value, ((0, 0), (0, width - value.shape[1])))


def heads_own(tall, own):
    lane = jnp.arange(D) // HDIM
    keep = lane[None, None, :] == jnp.arange(HEADS)[:, None, None]
    return jnp.sum(jnp.where(keep, tall.reshape(HEADS, own, D), 0.0), 0)


def on_device(moves, *arrays):
    (
        tokens, actions, noise, timesteps, task_mask, goal_flag, act_mask, groups,
        w_qkv, rows_qkv, cols_qkv, w_out, rows_out, cols_out,
        w_one, rows_one, cols_one, w_two, rows_two, cols_two,
        w_table, var_table, small, var_small,
    ) = arrays
    tokens, actions, noise, tstep = tokens[0], actions[0], noise[0], timesteps[0]
    read = noise.shape[0]
    seq = tokens.shape[0]
    count = moves.count
    own = w_qkv.shape[0]

    attn, one, two = gather_weights(
        moves, *run_wire(act_mask, w_qkv, w_out, w_one, w_two, w_table, small)
    )
    noisy, temb = condition(actions, noise, tstep, D)
    noisy_low = lanes_to(noisy.astype(BF), LANES)
    normed, unit, last, gains, entries_count, attn = run_norm(
        moves, tokens, noisy_low, temb[None, :], attn
    )
    seen = visible_last(groups[0], task_mask[0], goal_flag[0], read)
    q, qk, probs, pa, o, y, a2, *early = run_attend(
        moves, normed, last, gains, seen, noisy_low, attn
    )
    def got(blocks):
        return exchange(moves, blocks).reshape(moves.fsdp * read, blocks.shape[2])

    mask = lanes_to(act_mask.astype(F32), LANES)
    m, du, grads, f, dy, do, small_up, loss = run_feed(
        moves, y, a2, gains, entries_count, lanes_to(noise, LANES), mask, attn, one, two
    )
    dq, *late = run_back(
        moves, normed, unit, probs, qk, do, dy, last, gains, f, small_up, attn, m, q, *early
    )
    entries_count = entries_count.reshape(())
    if not moves.fast:
        factors = (pa, o, normed[seq - read :], a2, m, du, grads, f, dq) + tuple(late)
        return plain_update(moves, factors, loss, entries_count, arrays[8:])
    all_grads = gather_z_last(moves, grads, (dq,))
    all_du = gather_z_first(moves, du, (dq,))
    got_late = got(late[0])
    all_dq = gather_z_first(moves, dq)
    mine, theirs = run_upper(moves, got_late, all_du, all_grads, own)
    g_one, n_one, g_two, n_two, g_out, n_out, g_v, stats = run_upper_sum(
        mine, moves.swap(theirs), rows_one, rows_two, rows_out
    )
    mine, theirs = run_lower(moves, got_late, all_dq, all_grads, own)
    (
        g_qkv, n_qkv, g_table, v_table, u_table, g_small, v_small, u_small, stats,
    ) = run_lower_sum(
        mine, moves.swap(theirs), g_v, stats, loss, rows_qkv, var_table, var_small.T
    )
    stats = total(moves, stats)
    news = run_renew(
        stats,
        (
            (cols_qkv, n_qkv, g_qkv, w_qkv),
            (cols_out, n_out, g_out, w_out),
            (cols_one, n_one, g_one, w_one),
            (cols_two, n_two, g_two, w_two),
        ),
        ((u_table, w_table), (u_small, small.T)),
    )
    result = [news[10].reshape(()), entries_count, news[11].reshape(())]
    for k, (grad, rows) in enumerate(
        ((g_qkv, n_qkv), (g_out, n_out), (g_one, n_one), (g_two, n_two))
    ):
        result += [grad, rows.reshape(-1), news[2 * k].reshape(-1), news[2 * k + 1]]
    return tuple(result + [g_table, v_table, news[8], g_small.T, v_small.T, news[9].T])


def plain_update(moves, factors, loss, entries_count, arrays):
    (
        w_qkv, rows_qkv, cols_qkv, w_out, rows_out, cols_out,
        w_one, rows_one, cols_one, w_two, rows_two, cols_two,
        w_table, var_table, small, var_small,
    ) = arrays
    pa, o, normed, a2, m, du, two, f, dq, dsa, demb, split = factors
    dq, q, noisy_low = dq[:, :D], dq[:, D : 2 * D], dq[:, 2 * D :]
    read, count, own = q.shape[0], moves.count, w_qkv.shape[0]
    early = jnp.concatenate(
        [pa.reshape(HEADS, read, D), jnp.stack([o, normed, a2, jnp.zeros_like(a2)])], 0
    )
    late = jnp.concatenate(
        [dsa.reshape(HEADS, read, D), jnp.stack([f, demb, split, jnp.zeros_like(f)])], 0
    )
    n_rows = count * read
    got_early = exchange(moves, to_owners(early, count)).reshape(n_rows, SLOTS * own)
    got_mid = exchange(moves, m.reshape(read, count, FF // count).transpose(1, 0, 2))
    got_mid = got_mid.reshape(n_rows, FF // count)
    got_late = exchange(moves, to_owners(late, count)).reshape(n_rows, SLOTS * own)
    all_q, all_du, all_two, all_dq = (
        lax.all_gather(part, AX, axis=0, tiled=True)
        for part in (q, jnp.concatenate([du, noisy_low], 1), two, dq)
    )
    all_du, all_noisy = all_du[:, :FF], all_du[:, FF:]
    all_dz, all_da, all_do, all_de = (
        all_two[:, :D], all_two[:, D : 2 * D], all_two[:, 2 * D : 3 * D], all_two[:, 3 * D :]
    )

    heads = HEADS * own

    def slot(array, k):
        return array[:, k * own : (k + 1) * own]

    g_v = heads_own(dot_left(got_early[:, :heads], all_do), own)
    g_out = dot_left(slot(got_early, HEADS), all_da)
    g_one = dot_left(slot(got_early, HEADS + 2), all_du)
    g_two = dot_left(got_mid, all_dz)
    g_q = dot_left(slot(got_early, HEADS + 1), all_dq)
    g_k = heads_own(dot_left(got_late[:, :heads], all_q), own) * HDIM ** (-0.5)
    g_qkv = jnp.concatenate([g_q, g_k, g_v], 1)
    g_table = (
        dot_left(slot(got_late, HEADS), all_de) + dot_left(slot(got_late, HEADS + 1), all_noisy)
    )[:, :ACTW]
    parts = jnp.sum(slot(got_late, HEADS + 2).reshape(count, read, own).astype(F32), 0)
    g_small = (parts[0:6] + parts[6:12]).T

    beta = 1.0 - float(STEP) ** (-0.8)
    mats = (g_qkv, g_out, g_one, g_two)
    squares = tuple((g * g for g in mats))
    rows_new = tuple(
        (
            beta * r + (1.0 - beta) * jnp.sum(sq, 1)
            for r, sq in zip((rows_qkv, rows_out, rows_one, rows_two), squares)
        )
    )
    var_table_new = beta * var_table + (1.0 - beta) * g_table * g_table
    var_small_new = beta * var_small + (1.0 - beta) * g_small * g_small
    unit_table = g_table * lax.rsqrt(var_table_new)
    unit_small = g_small * lax.rsqrt(var_small_new)
    vector_squares = jnp.sum(unit_table * unit_table) + jnp.sum(unit_small * unit_small)
    col_parts = [jnp.sum(sq, 0) for sq in squares]
    over_rows = [jnp.sum(sq / r[:, None], 0) for sq, r in zip(squares, rows_new)]
    singles = jnp.stack([jnp.sum(r) for r in rows_new] + [vector_squares, loss[0, 0]])
    sums = jnp.concatenate(col_parts + over_rows + [singles])
    length = sums.shape[0]
    sums = jnp.pad(sums, (0, -length % (8 * LANES))).reshape(-1, LANES)
    sums = total(moves, sums).reshape(-1)[:length]
    cuts = []
    at = 0
    for size in [c.shape[0] for c in col_parts] * 2:
        cuts.append(sums[at : at + size])
        at += size
    totals = [sums[at + k] for k in range(4)]
    squares_total, loss_sum = sums[at + 4], sums[at + 5]
    cols_new = tuple(
        (
            beta * c + (1.0 - beta) * s
            for c, s in zip((cols_qkv, cols_out, cols_one, cols_two), cuts[:4])
        )
    )
    for c, over, t in zip(cols_new, cuts[4:], totals):
        squares_total = squares_total + t * jnp.sum(over / c)
    units = tuple(
        (
            g * lax.rsqrt(r[:, None] * c[None, :] / t)
            for g, r, c, t in zip(mats, rows_new, cols_new, totals)
        )
    )
    entries = 4 * D * D + 2 * D * FF + D * ACTW + 6 * D
    clip_rms = jnp.sqrt(squares_total / entries)
    factor = 1.0 / jnp.maximum(1.0, clip_rms / clip_level)
    result = [loss_sum, entries_count, clip_rms]
    for master, grad, rows, cols, update in zip(
        (w_qkv, w_out, w_one, w_two), mats, rows_new, cols_new, units
    ):
        result += [grad, rows, cols, master - rate_matrix * update * factor]
    result += [g_table, var_table_new, w_table - rate_matrix * unit_table * factor]
    result += [g_small, var_small_new, small - rate_small * unit_small * factor]
    return tuple(result)


def solution(mesh):
    rows = P(AX)
    items = (rows,) * 8
    matrix = (rows, rows, P())
    plain = (rows, rows)
    return jax.shard_map(
        functools.partial(on_device, Moves(mesh)),
        mesh=mesh,
        in_specs=items + matrix * 4 + plain * 2,
        out_specs=(P(),) * 3 + (rows, rows, P(), rows) * 4 + (rows,) * 6,
        check_vma=False,
    )
```

time: 363 us -> 249 us (0.69)
  local copies, waits for them, and re-layouts: 92.7 us -> 13.5 us
  waiting for transfers between devices: 99.2 us -> 127 us
  starting transfers between devices: 91.2 us -> 66.3 us
  other arithmetic: 31.7 us -> 9.94 us
  between operations: 13.6 us -> 2.91 us
  matrix products: 9.62 us -> 0 us
  Pallas kernels: 22.7 us -> 28.4 us
    ppermute x18, waiting for transfers between devices: 19.6 us -> 45.8 us  [turn(): lax.ppermute(value, 'fsdp', [(i, (i + 4 * step) % self.fsdp) for i in ran...]
    dynamic_update_slice x29 -> x0, local copies, waits for them, and re-layouts: 22.8 us -> none  [stack_at(): out = lax.dynamic_update_index_in_dim(out, part, at, 0)]
    concatenate x13 -> x0, local copies, waits for them, and re-layouts: 14.8 us -> none  [the longest x5 6.49 us: on_device(): jnp.concatenate([pa.reshape(HEADS, read, D), jnp.stack([o, normed[seq - r...]
    all_to_all x4 -> x1, starting transfers between devices: 15.7 us -> 3.63 us  [exchange(): lax.all_to_all(blocks, 'fsdp' if moves.fast else AX, 0, 0, tiled=False)]
    unnamed x157 -> x72, local copies, waits for them, and re-layouts: 24.1 us -> 13.3 us
    dot_general x9 -> x0, matrix products: 9.62 us -> none  [the longest x8 9.46 us: dot_left(): lax.dot_general(left, right, (((0,), (0,)), ((), ())), preferred_element_...]
    reduce_sum x18 -> x0, other arithmetic: 9.3 us -> none  [the longest x4 2.41 us: on_device(): jnp.sum(r)]
    ppermute x33, waiting for transfers between devices: 70.6 us -> 79.9 us  [flip(): lax.ppermute(value, 'fsdp', [(i, i ^ mask) for i in range(self.fsdp)])]
  transfers between devices with their start and end apart: 71 -> 67, of which waited for: 29 -> 35; matrix products, arithmetic and copies ran while one was open for 29% -> 4% of each run, Pallas kernels for 3% -> 3%
where the time goes in v2:
time: 249 us; the launch traced here: 248 us
  waiting for transfers between devices  127 us (51%)
  starting transfers between devices  66.3 us (27%)
  Pallas kernels  28.4 us (11%)
  local copies, waits for them, and re-layouts  13.5 us (5%)
  other arithmetic  9.94 us (4%)
  between operations  2.91 us (1%)
    ppermute x33, waiting for transfers between devices, flip(): lax.ppermute(value, 'fsdp', [(i, i ^ mask) for i in range(self.fsdp)])  79.9 us
    ppermute x18, waiting for transfers between devices, turn(): lax.ppermute(value, 'fsdp', [(i, (i + 4 * step) % self.fsdp) for i in ran...  45.8 us
    ppermute x33, starting transfers between devices, flip(): lax.ppermute(value, 'fsdp', [(i, i ^ mask) for i in range(self.fsdp)])  37.9 us
    pallas_call x10, Pallas kernels, call(): pl.pallas_call(kernel, out_shape=tuple((shape(*out) for out in outs)), in...  28.4 us
    ppermute x18, starting transfers between devices, turn(): lax.ppermute(value, 'fsdp', [(i, (i + 4 * step) % self.fsdp) for i in ran...  21.8 us
    unnamed x72, local copies, waits for them, and re-layouts  13.3 us
    select_n x23, other arithmetic, pair(): jnp.where(bit == 0, jnp.concatenate([own, other], 1), jnp.concatenate([ot...  8.35 us
  transfers between devices with their start and end apart: 67, of which 35 were waited for; matrix products, arithmetic and copies ran while one was open for 4% of the time, Pallas kernels for 3%

profile of v2, /device:TPU:0, one launch (start us, length us, event | category | flops | bytes accessed | tf_op | source)
XLA Modules:
  0.0 248.4 jit_solution(5352937890983880384)
XLA Ops:
  10.9 3.2 %collective-permute-done.12 = bf16[24,3072]{1,0:T(8,128)(2,1)S(1)} collective-permute-done((bf16[24,3072]{1,0:T(8,128)(2,1)}, bf16[24,3072]{1,0:T(8,128)(2,1)S(1)}, u32[]{:S(2)}, u32[]{:S(2)}) %collective-permute-start.12) | collective-permute-done | bytes 147488 | tf_op jit(solution)/shard_map/ppermute | solution.py:40
  22.4 3.9 %collective-permute-done.27 = bf16[96,768]{1,0:T(8,128)(2,1)S(1)} collective-permute-done((bf16[96,768]{1,0:T(8,128)(2,1)S(1)}, bf16[96,768]{1,0:T(8,128)(2,1)S(1)}, u32[]{:S(2)}, u32[]{:S(2)}) %collective-permute-start.27) | collective-permute-done | bytes 147488 | tf_op jit(solution)/shard_map/ppermute | solution.py:40
  30.2 5.1 %collective-permute-done.30 = bf16[96,768]{1,0:T(8,128)(2,1)S(1)} collective-permute-done((bf16[96,768]{1,0:T(8,128)(2,1)S(1)}, bf16[96,768]{1,0:T(8,128)(2,1)S(1)}, u32[]{:S(2)}, u32[]{:S(2)}) %collective-permute-start.30) | collective-permute-done | bytes 147488 | tf_op jit(solution)/shard_map/ppermute | solution.py:40
  38.1 4.1 %collective-permute-done.32 = bf16[96,768]{1,0:T(8,128)(2,1)S(1)} collective-permute-done((bf16[96,768]{1,0:T(8,128)(2,1)S(1)}, bf16[96,768]{1,0:T(8,128)(2,1)S(1)}, u32[]{:S(2)}, u32[]{:S(2)}) %collective-permute-start.32) | collective-permute-done | bytes 147488 | tf_op jit(solution)/shard_map/ppermute | solution.py:43
  44.4 4.0 %collective-permute-done.33 = bf16[96,768]{1,0:T(8,128)(2,1)S(1)} collective-permute-done((bf16[96,768]{1,0:T(8,128)(2,1)S(1)}, bf16[96,768]{1,0:T(8,128)(2,1)S(1)}, u32[]{:S(2)}, u32[]{:S(2)}) %collective-permute-start.33) | collective-permute-done | bytes 147488 | tf_op jit(solution)/shard_map/ppermute | solution.py:40
  54.3 4.6 %collective-permute-done.15 = bf16[48,3072]{1,0:T(8,128)(2,1)S(1)} collective-permute-done((bf16[48,3072]{1,0:T(8,128)(2,1)S(1)}, bf16[48,3072]{1,0:T(8,128)(2,1)S(1)}, u32[]{:S(2)}, u32[]{:S(2)}) %collective-permute-start.15) | collective-permute-done | bytes 294944 | tf_op jit(solution)/shard_map/ppermute | solution.py:40
  60.9 5.4 %collective-permute-done.4 = bf16[48,3200]{1,0:T(8,128)(2,1)S(1)} collective-permute-done((bf16[48,3200]{1,0:T(8,128)(2,1)S(1)}, bf16[48,3200]{1,0:T(8,128)(2,1)S(1)}, u32[]{:S(2)}, u32[]{:S(2)}) %collective-permute-start.4) | collective-permute-done | bytes 307232 | tf_op jit(solution)/shard_map/ppermute | solution.py:43
  69.2 4.8 %collective-permute-done.5 = bf16[48,3200]{1,0:T(8,128)(2,1)S(1)} collective-permute-done((bf16[48,3200]{1,0:T(8,128)(2,1)S(1)}, bf16[48,3200]{1,0:T(8,128)(2,1)S(1)}, u32[]{:S(2)}, u32[]{:S(2)}) %collective-permute-start.5) | collective-permute-done | bytes 307232 | tf_op jit(solution)/shard_map/ppermute | solution.py:40
  74.0 3.3 %collective-permute-done.6 = bf16[48,3200]{1,0:T(8,128)(2,1)S(1)} collective-permute-done((bf16[48,3200]{1,0:T(8,128)(2,1)S(1)}, bf16[48,3200]{1,0:T(8,128)(2,1)S(1)}, u32[]{:S(2)}, u32[]{:S(2)}) %collective-permute-start.6) | collective-permute-done | bytes 307232 | tf_op jit(solution)/shard_map/ppermute | solution.py:43
  78.0 5.0 %collective-permute-done.18 = bf16[48,3072]{1,0:T(8,128)(2,1)S(1)} collective-permute-done((bf16[48,3072]{1,0:T(8,128)(2,1)S(1)}, bf16[48,3072]{1,0:T(8,128)(2,1)S(1)}, u32[]{:S(2)}, u32[]{:S(2)}) %collective-permute-start.18) | collective-permute-done | bytes 294944 | tf_op jit(solution)/shard_map/ppermute | solution.py:43
  85.1 7.3 %collective-permute-done.17 = bf16[48,3072]{1,0:T(8,128)(2,1)S(1)} collective-permute-done((bf16[48,3072]{1,0:T(8,128)(2,1)S(1)}, bf16[48,3072]{1,0:T(8,128)(2,1)S(1)}, u32[]{:S(2)}, u32[]{:S(2)}) %collective-permute-start.17) | collective-permute-done | bytes 294944 | tf_op jit(solution)/shard_map/ppermute | solution.py:40
  111.6 3.4 %attend.1 = (bf16[16,896]{1,0:T(8,128)(2,1)S(1)}, bf16[192,768]{1,0:T(8,128)(2,1)S(1)}, f32[192,864]{1,0:T(8,128)S(1)}, bf16[192,768]{1,0:T(8,128)(2,1)}, bf16[1...) custom-call(bf16[864,768]{1,0:T(8,128)(2,1)S(1)} %get-tuple-element.8, ...), custom_call_target="tpu_custom_call" | custom-call | tf_op jit(solution)/shard_map/attend/pallas_call | solution.py:686
  115.1 9.4 %feed.1 = (bf16[16,16,256]{2,1,0:T(8,128)(2,1)S(1)}, bf16[16,3072]{1,0:T(8,128)(2,1)S(1)}, bf16[16,2432]{1,0:T(8,128)(2,1)S(1)}, bf16[16,768]{1,0:T(8,128)(2,1)S...) custom-call(f32[16,768]{1,0:T(8,128)S(1)} %get-tuple-element.93.y_ref, ...), custom_call_target="tpu_custom_call" | custom-call | tf_op jit(solution)/shard_map/feed/pallas_call | solution.py:686
  124.5 4.2 %back.1 = (bf16[16,1664]{1,0:T(8,128)(2,1)S(1)}, bf16[16,16,1792]{2,1,0:T(8,128)(2,1)}) custom-call(bf16[864,768]{1,0:T(8,128)(2,1)S(1)} %get-tuple-element.86.a_ref, f32[864,768]{1,0:T(8,128)S(1)} %get-tuple-element.87.unit_ref, f32[192,864]{1,0:T(8,128)S(1)} %get-tuple-element.91.p_ref, bf16[192,768]{1,0:T(8,128)(2,1)S(1)} %get-tuple-element.92.qk_ref, ...), custom_call_target="tpu_custom_call" | custom-call | tf_op jit(solution)/shard_map/back/pallas_call | solution.py:686
  128.8 3.6 %all-to-all-start = ((bf16[16,16,1792]{2,1,0:T(8,128)(2,1)}), bf16[16,16,1792]{2,1,0:T(8,128)(2,1)S(1)}, u32[]{:S(2)}, u32[]{:S(2)}) async-start(bf16[16,16,1792]{2,1,0:T(8,128)(2,1)} %get-tuple-element.105), calls=%async_computation | async-start | bytes 1835008 | tf_op jit(solution)/shard_map/all_to_all | solution.py:166
  136.0 4.0 %collective-permute-done.45.refs_1_ = bf16[16,2432]{1,0:T(8,128)(2,1)S(1)} collective-permute-done((bf16[16,2432]{1,0:T(8,128)(2,1)S(1)}, bf16[16,2432]{1,0:T(8,128)(2,1)S(1)}, u32[]{:S(2)}, u32[]{:S(2)}) %collective-permute-start.45) | collective-permute-done | bytes 77856 | tf_op jit(solution)/shard_map/ppermute | solution.py:40
  140.0 5.4 %collective-permute-done.46.refs_2_ = bf16[16,2432]{1,0:T(8,128)(2,1)S(1)} collective-permute-done((bf16[16,2432]{1,0:T(8,128)(2,1)S(1)}, bf16[16,2432]{1,0:T(8,128)(2,1)S(1)}, u32[]{:S(2)}, u32[]{:S(2)}) %collective-permute-start.46) | collective-permute-done | bytes 77856 | tf_op jit(solution)/shard_map/ppermute | solution.py:40
  145.8 12.7 %collective-permute-done.48.refs_5_ = bf16[64,2432]{1,0:T(8,128)(2,1)S(1)} collective-permute-done((bf16[64,2432]{1,0:T(8,128)(2,1)S(1)}, bf16[64,2432]{1,0:T(8,128)(2,1)S(1)}, u32[]{:S(2)}, u32[]{:S(2)}) %collective-permute-start.48) | collective-permute-done | bytes 311328 | tf_op jit(solution)/shard_map/ppermute | solution.py:43
  165.8 7.0 %collective-permute-done.52.refs_1_ = bf16[16,3072]{1,0:T(8,128)(2,1)S(1)} collective-permute-done((bf16[16,3072]{1,0:T(8,128)(2,1)S(1)}, bf16[16,3072]{1,0:T(8,128)(2,1)S(1)}, u32[]{:S(2)}, u32[]{:S(2)}) %collective-permute-start.52) | collective-permute-done | bytes 98336 | tf_op jit(solution)/shard_map/ppermute | solution.py:43
  181.6 5.8 %collective-permute-done.55.refs_1_ = bf16[64,3072]{1,0:T(8,128)(2,1)S(1)} collective-permute-done((bf16[64,3072]{1,0:T(8,128)(2,1)S(1)}, bf16[64,3072]{1,0:T(8,128)(2,1)S(1)}, u32[]{:S(2)}, u32[]{:S(2)}) %collective-permute-start.55) | collective-permute-done | bytes 393248 | tf_op jit(solution)/shard_map/ppermute | solution.py:40
  187.4 8.7 %collective-permute-done.56.refs_2_ = bf16[64,3072]{1,0:T(8,128)(2,1)S(1)} collective-permute-done((bf16[64,3072]{1,0:T(8,128)(2,1)S(1)}, bf16[64,3072]{1,0:T(8,128)(2,1)S(1)}, u32[]{:S(2)}, u32[]{:S(2)}) %collective-permute-start.56) | collective-permute-done | bytes 393248 | tf_op jit(solution)/shard_map/ppermute | solution.py:40
  211.8 4.7 %collective-permute-done.42.refs_1_ = bf16[64,1664]{1,0:T(8,128)(2,1)S(1)} collective-permute-done((bf16[64,1664]{1,0:T(8,128)(2,1)S(1)}, bf16[64,1664]{1,0:T(8,128)(2,1)S(1)}, u32[]{:S(2)}, u32[]{:S(2)}) %collective-permute-start.42) | collective-permute-done | bytes 213024 | tf_op jit(solution)/shard_map/ppermute | solution.py:40
  234.8 3.4 %collective-permute-start.65 = (f32[8,3072]{1,0:T(8,128)S(1)}, f32[8,3072]{1,0:T(8,128)S(1)}, u32[]{:S(2)}, u32[]{:S(2)}) collective-permute-start(f32[8,3072]{1,0:T(8,128)S(1)} %add_add_fusion.1), channel_id=1, source_target_pairs={{0,12},{1,13},{2,14},{3,15},{4,8},{5,9},{6,10},{7,11},{8,4},{9,5},... | collective-permute-start | bytes 294920 | tf_op jit(solution)/shard_map/ppermute | solution.py:40
  238.2 5.9 %collective-permute-done.64 = f32[8,3072]{1,0:T(8,128)S(1)} collective-permute-done((f32[8,3072]{1,0:T(8,128)S(1)}, f32[8,3072]{1,0:T(8,128)S(1)}, u32[]{:S(2)}, u32[]{:S(2)}) %collective-permute-start.64) | collective-permute-done | bytes 98336 | tf_op jit(solution)/shard_map/ppermute | solution.py:40
  (235 shorter events, 116.6 us)
Async XLA Ops:
  2.7 14.7 %collective-permute-start.24 = (bf16[96,768]{1,0:T(8,128)(2,1)}, bf16[96,768]{1,0:T(8,128)(2,1)S(1)}, u32[]{:S(2)}, u32[]{:S(2)}) collective-permute-start(bf16[96,768]{1,0:T(8,128)(2,1)} %get-tuple-element.97), channel_id=1, source_target_pairs={{0,2},{1,3},{2,0},{3,1},{4,6},{5,7},{6,4},{7,5},{8,10},{9,11},{10,... | collective-permute-start | bytes 442376 | tf_op jit(solution)/shard_map/ppermute | solution.py:40
  5.7 14.3 %collective-permute-start.26 = (bf16[96,768]{1,0:T(8,128)(2,1)}, bf16[96,768]{1,0:T(8,128)(2,1)S(1)}, u32[]{:S(2)}, u32[]{:S(2)}) collective-permute-start(bf16[96,768]{1,0:T(8,128)(2,1)} %get-tuple-element.97), channel_id=1, source_target_pairs={{0,4},{1,5},{2,6},{3,7},{4,8},{5,9},{6,10},{7,11},{8,12},{9,13},{1... | collective-permute-start | bytes 442376 | tf_op jit(solution)/shard_map/ppermute | solution.py:43
  7.3 13.4 %collective-permute-start = (bf16[24,3200]{1,0:T(8,128)(2,1)}, bf16[24,3200]{1,0:T(8,128)(2,1)S(1)}, u32[]{:S(2)}, u32[]{:S(2)}) collective-permute-start(bf16[24,3200]{1,0:T(8,128)(2,1)} %get-tuple-element.85), channel_id=1, source_target_pairs={{0,1},{1,0},{2,3},{3,2},{4,5},{5,4},{6,7},{7,6},{8,9},{9,8},{10,11... | collective-permute-start | bytes 460808 | tf_op jit(solution)/shard_map/ppermute | solution.py:40
  15.2 13.2 %collective-permute-start.13 = (bf16[48,3072]{1,0:T(8,128)(2,1)S(1)}, bf16[48,3072]{1,0:T(8,128)(2,1)S(1)}, u32[]{:S(2)}, u32[]{:S(2)}) collective-permute-start(bf16[48,3072]{1,0:T(8,128)(2,1)S(1)} %maximum_select_fusion.14), channel_id=1, source_target_pairs={{0,1},{1,0},{2,3},{3,2},{4,5},{5,4},{6,7},{7,6},{8,9},{9,8},{10,11... | collective-permute-start | bytes 884744 | tf_op jit(solution)/shard_map/ppermute | solution.py:40
  15.8 27.6 %collective-permute-start.14 = (bf16[48,3072]{1,0:T(8,128)(2,1)S(1)}, bf16[48,3072]{1,0:T(8,128)(2,1)S(1)}, u32[]{:S(2)}, u32[]{:S(2)}) collective-permute-start(bf16[48,3072]{1,0:T(8,128)(2,1)S(1)} %maximum_select_fusion.14), channel_id=1, source_target_pairs={{0,4},{1,5},{2,6},{3,7},{4,8},{5,9},{6,10},{7,11},{8,12},{9,13},{1... | collective-permute-start | bytes 884744 | tf_op jit(solution)/shard_map/ppermute | solution.py:43
  18.4 18.3 %collective-permute-start.25 = (bf16[192,768]{1,0:T(8,128)(2,1)S(1)}, bf16[192,768]{1,0:T(8,128)(2,1)S(1)}, u32[]{:S(2)}, u32[]{:S(2)}) collective-permute-start(bf16[192,768]{1,0:T(8,128)(2,1)S(1)} %maximum_select_fusion.16), channel_id=1, source_target_pairs={{0,1},{1,0},{2,3},{3,2},{4,5},{5,4},{6,7},{7,6},{8,9},{9,8},{10,11... | collective-permute-start | bytes 884744 | tf_op jit(solution)/shard_map/ppermute | solution.py:40
  26.3 15.9 %collective-permute-start.1 = (bf16[48,3200]{1,0:T(8,128)(2,1)S(1)}, bf16[48,3200]{1,0:T(8,128)(2,1)S(1)}, u32[]{:S(2)}, u32[]{:S(2)}) collective-permute-start(bf16[48,3200]{1,0:T(8,128)(2,1)S(1)} %maximum_select_fusion.12), channel_id=1, source_target_pairs={{0,2},{1,3},{2,0},{3,1},{4,6},{5,7},{6,4},{7,5},{8,10},{9,11},{10,... | collective-permute-start | bytes 921608 | tf_op jit(solution)/shard_map/ppermute | solution.py:40
  28.4 21.1 %collective-permute-start.2 = (bf16[48,3200]{1,0:T(8,128)(2,1)S(1)}, bf16[48,3200]{1,0:T(8,128)(2,1)S(1)}, u32[]{:S(2)}, u32[]{:S(2)}) collective-permute-start(bf16[48,3200]{1,0:T(8,128)(2,1)S(1)} %maximum_select_fusion.12), channel_id=1, source_target_pairs={{0,4},{1,5},{2,6},{3,7},{4,8},{5,9},{6,10},{7,11},{8,12},{9,13},{1... | collective-permute-start | bytes 921608 | tf_op jit(solution)/shard_map/ppermute | solution.py:43
  42.2 50.3 %collective-permute-start.20 = (bf16[96,3072]{1,0:T(8,128)(2,1)S(1)}, bf16[96,3072]{1,0:T(8,128)(2,1)S(1)}, u32[]{:S(2)}, u32[]{:S(2)}) collective-permute-start(bf16[96,3072]{1,0:T(8,128)(2,1)S(1)} %bitcast.75), channel_id=1, source_target_pairs={{0,16},{16,0},{1,17},{17,1},{2,18},{18,2},{3,19},{19,3},{4,20},{20... | collective-permute-start | bytes 1769480 | tf_op jit(solution)/shard_map/ppermute | solution.py:48
  49.5 19.2 %collective-permute-start.16 = (bf16[48,3072]{1,0:T(8,128)(2,1)S(1)}, bf16[48,3072]{1,0:T(8,128)(2,1)S(1)}, u32[]{:S(2)}, u32[]{:S(2)}) collective-permute-start(bf16[48,3072]{1,0:T(8,128)(2,1)S(1)} %collective-permute-done.14), channel_id=1, source_target_pairs={{0,4},{1,5},{2,6},{3,7},{4,8},{5,9},{6,10},{7,11},{8,12},{9,13},{1... | collective-permute-start | bytes 884744 | tf_op jit(solution)/shard_map/ppermute | solution.py:43
  49.6 17.9 %collective-permute-start.3 = (bf16[48,3200]{1,0:T(8,128)(2,1)S(1)}, bf16[48,3200]{1,0:T(8,128)(2,1)S(1)}, u32[]{:S(2)}, u32[]{:S(2)}) collective-permute-start(bf16[48,3200]{1,0:T(8,128)(2,1)S(1)} %collective-permute-done.2), channel_id=1, source_target_pairs={{0,2},{1,3},{2,0},{3,1},{4,6},{5,7},{6,4},{7,5},{8,10},{9,11},{10,... | collective-permute-start | bytes 921608 | tf_op jit(solution)/shard_map/ppermute | solution.py:40
  67.6 26.2 %collective-permute-start.35 = (bf16[384,768]{1,0:T(8,128)(2,1)S(1)}, bf16[384,768]{1,0:T(8,128)(2,1)S(1)}, u32[]{:S(2)}, u32[]{:S(2)}) collective-permute-start(bf16[384,768]{1,0:T(8,128)(2,1)S(1)} %bitcast.77), channel_id=1, source_target_pairs={{0,16},{16,0},{1,17},{17,1},{2,18},{18,2},{3,19},{19,3},{4,20},{20... | collective-permute-start | bytes 1769480 | tf_op jit(solution)/shard_map/ppermute | solution.py:48
  68.7 28.8 %collective-permute-start.8 = (bf16[96,3200]{1,0:T(8,128)(2,1)S(1)}, bf16[96,3200]{1,0:T(8,128)(2,1)S(1)}, u32[]{:S(2)}, u32[]{:S(2)}) collective-permute-start(bf16[96,3200]{1,0:T(8,128)(2,1)S(1)} %maximum_select_fusion.refs_0_), channel_id=1, source_target_pairs={{0,16},{16,0},{1,17},{17,1},{2,18},{18,2},{3,19},{19,3},{4,20},{20... | collective-permute-start | bytes 1843208 | tf_op jit(solution)/shard_map/ppermute | solution.py:48
  98.3 16.7 %collective-permute-start.21 = (bf16[96,3072]{1,0:T(8,128)(2,1)}, bf16[96,3072]{1,0:T(8,128)(2,1)}, u32[]{:S(2)}, u32[]{:S(2)}) collective-permute-start(bf16[96,3072]{1,0:T(8,128)(2,1)} %bitcast.15.refs_1_), channel_id=1, source_target_pairs={{0,16},{16,0},{1,17},{17,1},{2,18},{18,2},{3,19},{19,3},{4,20},{20... | collective-permute-start | bytes 1769480 | tf_op jit(solution)/shard_map/ppermute | solution.py:48
  99.7 15.4 %collective-permute-start.37 = (bf16[384,768]{1,0:T(8,128)(2,1)}, bf16[384,768]{1,0:T(8,128)(2,1)}, u32[]{:S(2)}, u32[]{:S(2)}) collective-permute-start(bf16[384,768]{1,0:T(8,128)(2,1)} %bitcast.36.refs_10_), channel_id=1, source_target_pairs={{0,16},{16,0},{1,17},{17,1},{2,18},{18,2},{3,19},{19,3},{4,20},{20... | collective-permute-start | bytes 1769480 | tf_op jit(solution)/shard_map/ppermute | solution.py:48
  100.5 14.5 %collective-permute-start.38 = (bf16[384,768]{1,0:T(8,128)(2,1)}, bf16[384,768]{1,0:T(8,128)(2,1)}, u32[]{:S(2)}, u32[]{:S(2)}) collective-permute-start(bf16[384,768]{1,0:T(8,128)(2,1)} %bitcast.41.refs_11_), channel_id=1, source_target_pairs={{0,16},{16,0},{1,17},{17,1},{2,18},{18,2},{3,19},{19,3},{4,20},{20... | collective-permute-start | bytes 1769480 | tf_op jit(solution)/shard_map/ppermute | solution.py:48
  101.8 13.2 %collective-permute-start.22 = (bf16[96,3072]{1,0:T(8,128)(2,1)}, bf16[96,3072]{1,0:T(8,128)(2,1)}, u32[]{:S(2)}, u32[]{:S(2)}) collective-permute-start(bf16[96,3072]{1,0:T(8,128)(2,1)} %bitcast.18.refs_2_), channel_id=1, source_target_pairs={{0,16},{16,0},{1,17},{17,1},{2,18},{18,2},{3,19},{19,3},{4,20},{20... | collective-permute-start | bytes 1769480 | tf_op jit(solution)/shard_map/ppermute | solution.py:48
  128.8 68.1 %all-to-all-start = ((bf16[16,16,1792]{2,1,0:T(8,128)(2,1)}), bf16[16,16,1792]{2,1,0:T(8,128)(2,1)S(1)}, u32[]{:S(2)}, u32[]{:S(2)}) async-start(bf16[16,16,1792]{2,1,0:T(8,128)(2,1)} %get-tuple-element.105), calls=%async_computation | async-start | bytes 1835008 | tf_op jit(solution)/shard_map/all_to_all | solution.py:166
  145.4 13.1 %collective-permute-start.48 = (bf16[64,2432]{1,0:T(8,128)(2,1)S(1)}, bf16[64,2432]{1,0:T(8,128)(2,1)S(1)}, u32[]{:S(2)}, u32[]{:S(2)}) collective-permute-start(bf16[64,2432]{1,0:T(8,128)(2,1)S(1)} %joined.4.refs_4_), channel_id=1, source_target_pairs={{0,4},{1,5},{2,6},{3,7},{4,8},{5,9},{6,10},{7,11},{8,12},{9,13},{1... | collective-permute-start | bytes 933896 | tf_op jit(solution)/shard_map/ppermute | solution.py:43
  158.5 20.4 %collective-permute-start.49 = (bf16[64,2432]{1,0:T(8,128)(2,1)S(1)}, bf16[64,2432]{1,0:T(8,128)(2,1)S(1)}, u32[]{:S(2)}, u32[]{:S(2)}) collective-permute-start(bf16[64,2432]{1,0:T(8,128)(2,1)S(1)} %collective-permute-done.48.refs_5_), channel_id=1, source_target_pairs={{0,4},{1,5},{2,6},{3,7},{4,8},{5,9},{6,10},{7,11},{8,12},{9,13},{1... | collective-permute-start | bytes 933896 | tf_op jit(solution)/shard_map/ppermute | solution.py:43
  177.0 19.1 %collective-permute-start.56 = (bf16[64,3072]{1,0:T(8,128)(2,1)S(1)}, bf16[64,3072]{1,0:T(8,128)(2,1)S(1)}, u32[]{:S(2)}, u32[]{:S(2)}) collective-permute-start(bf16[64,3072]{1,0:T(8,128)(2,1)S(1)} %joined.5.refs_0_), channel_id=1, source_target_pairs={{0,2},{1,3},{2,0},{3,1},{4,6},{5,7},{6,4},{7,5},{8,10},{9,11},{10,... | collective-permute-start | bytes 1179656 | tf_op jit(solution)/shard_map/ppermute | solution.py:40
  178.5 17.6 %collective-permute-start.57 = (bf16[64,3072]{1,0:T(8,128)(2,1)S(1)}, bf16[64,3072]{1,0:T(8,128)(2,1)S(1)}, u32[]{:S(2)}, u32[]{:S(2)}) collective-permute-start(bf16[64,3072]{1,0:T(8,128)(2,1)S(1)} %joined.5.refs_0_), channel_id=1, source_target_pairs={{0,3},{1,2},{2,1},{3,0},{4,7},{5,6},{6,5},{7,4},{8,11},{9,10},{10,... | collective-permute-start | bytes 1179656 | tf_op jit(solution)/shard_map/ppermute | solution.py:40
  179.0 17.9 %collective-permute-start.50 = (bf16[64,2432]{1,0:T(8,128)(2,1)S(1)}, bf16[64,2432]{1,0:T(8,128)(2,1)S(1)}, u32[]{:S(2)}, u32[]{:S(2)}) collective-permute-start(bf16[64,2432]{1,0:T(8,128)(2,1)S(1)} %collective-permute-done.49.refs_6_), channel_id=1, source_target_pairs={{0,4},{1,5},{2,6},{3,7},{4,8},{5,9},{6,10},{7,11},{8,12},{9,13},{1... | collective-permute-start | bytes 933896 | tf_op jit(solution)/shard_map/ppermute | solution.py:43
  199.1 22.3 %collective-permute-start.58 = (f32[240,768]{1,0:T(8,128)S(1)}, f32[240,768]{1,0:T(8,128)S(1)}, u32[]{:S(2)}, u32[]{:S(2)}) collective-permute-start(f32[240,768]{1,0:T(8,128)S(1)} %get-tuple-element.114), channel_id=1, source_target_pairs={{0,16},{16,0},{1,17},{17,1},{2,18},{18,2},{3,19},{19,3},{4,20},{20... | collective-permute-start | bytes 2211848 | tf_op jit(solution)/shard_map/ppermute | solution.py:48
  (79 other events, 582.8 us)

commit v3 on v2

v3 whole, which is shorter than its diff:
```python
import functools
import math

import jax
import jax.numpy as jnp
from jax import lax
from jax.experimental import pallas as pl
from jax.experimental.pallas import tpu as pltpu
from jax.sharding import PartitionSpec as P

D = 768
HEADS = 12
HDIM = 64
FF = 3072
GOALTOK = 64
ACTW = 28
TSTEPS = 20
STEP = 10
LANES = 128
SLOTS = 16
AX = ("dp", "fsdp")

rate_matrix = 0.05
rate_small = 0.3
clip_level = 0.5
BF = jnp.bfloat16
F32 = jnp.float32
MIB = 1024 * 1024


class Moves:
    def __init__(self, mesh):
        self.dp = mesh.shape["dp"]
        self.fsdp = mesh.shape["fsdp"]
        self.count = self.dp * self.fsdp
        self.fast = self.dp == 2 and self.fsdp == 16
        self.depth = self.fsdp // 4

    def flip(self, value, mask):
        return lax.ppermute(value, "fsdp", [(i, i ^ mask) for i in range(self.fsdp)])

    def turn(self, value, step):
        return lax.ppermute(
            value, "fsdp", [(i, (i + 4 * step) % self.fsdp) for i in range(self.fsdp)]
        )

    def swap(self, value):
        return lax.ppermute(value, "dp", [(0, 1), (1, 0)])

    def place(self):
        inner = lax.axis_index("fsdp")
        return lax.axis_index("dp"), inner // 4, (inner // 2) % 2, inner % 2


def pair(own, other, bit, blocks=1):
    rows, width = own.shape
    shaped = (blocks, rows // blocks, width)
    own, other = own.reshape(shaped), other.reshape(shaped)
    both = jnp.where(
        bit == 0, jnp.concatenate([own, other], 1), jnp.concatenate([other, own], 1)
    )
    return both.reshape(2 * rows, width)


def after(value, waits):
    if not waits:
        return value
    return lax.optimization_barrier((value,) + tuple(waits))[0]


def gather_weights(moves, attn, one, two):
    if not moves.fast:
        return [[lax.all_gather(w, AX, axis=0, tiled=True)] for w in (attn, one, two)]
    core, z, y, x = moves.place()
    move = {
        "x": lambda v: moves.flip(v, 1),
        "y": lambda v: moves.flip(v, 2),
        "z": lambda v: moves.turn(v, 1),
    }

    def go(link, value):
        return move[link](value)

    cz1 = go("z", two)
    ax, by, cy0 = go("x", attn), go("y", one), go("y", two)
    a0, b0, c0 = pair(attn, ax, x), pair(one, by, y), pair(two, cy0, y)
    a1, b1 = go("z", a0), go("z", b0)
    bx0, ay0, cx0 = go("x", b0), go("y", a0), go("x", c0)
    am0, bm0, cm0 = pair(a0, ay0, y), pair(b0, bx0, x, 2), pair(c0, cx0, x, 2)
    a2, cz2, b2 = go("z", a1), go("z", cz1), go("z", b1)
    ay1, cy1 = go("y", a1), go("y", cz1)
    c1 = pair(cz1, cy1, y)
    bx1, cx1 = go("x", b1), go("x", c1)
    am1, bm1, cm1 = pair(a1, ay1, y), pair(b1, bx1, x, 2), pair(c1, cx1, x, 2)
    a3, cz3, b3 = go("z", a2), go("z", cz2), go("z", b2)
    ay2, cy2 = go("y", a2), go("y", cz2)
    c2 = pair(cz2, cy2, y)
    bx2, cx2 = go("x", b2), go("x", c2)
    am2 = pair(a2, ay2, y)
    ay3, cy3 = go("y", a3), go("y", cz3)
    am3 = pair(a3, ay3, y)
    bm2, cm2 = pair(b2, bx2, x, 2), pair(c2, cx2, x, 2)
    c3 = pair(cz3, cy3, y)
    cx3, bx3 = go("x", c3), go("x", b3)
    cm3, bm3 = pair(c3, cx3, x, 2), pair(b3, bx3, x, 2)
    am0s, am1s, am2s, am3s = (moves.swap(after(v, (ay3,))) for v in (am0, am1, am2, am3))
    bm0s, bm1s, bm2s, bm3s = (moves.swap(after(v, (ay3,))) for v in (bm0, bm1, bm2, bm3))
    cm0s, cm1s, cm2s, cm3s = (moves.swap(after(v, (ay3,))) for v in (cm0, cm1, cm2, cm3))
    return [
        [am0, am1, am2, am3, am0s, am1s, am2s, am3s],
        [bm0, bm1, bm2, bm3, bm0s, bm1s, bm2s, bm3s],
        [cm0, cm1, cm2, cm3, cm0s, cm1s, cm2s, cm3s],
    ]


def joined(parts):
    rows, width = parts[0].shape

    def body(*refs):
        for k, ref in enumerate(refs[:-1]):
            refs[-1][k * rows : (k + 1) * rows, :] = ref[...]

    return pl.pallas_call(
        body,
        out_shape=shape((rows * len(parts), width), parts[0].dtype),
        in_specs=[VMEM] * len(parts),
        out_specs=VMEM,
        compiler_params=pltpu.CompilerParams(vmem_limit_bytes=4 * MIB),
        name="joined",
    )(*parts)


def gather_last(moves, first, late, du, low):
    held = joined([du] + [moves.turn(du, k) for k in range(1, moves.depth)])
    ring = [joined([low, moves.flip(low, 2)])]
    over_x = moves.flip(held, 1)
    got = sent_along(moves, [after(v, first[1:]) for v in late])
    ring.append(moves.turn(ring[0], 1))
    first = to_places(moves, first)
    sides = [moves.flip(ring[0], 1)]
    wide = joined([held, over_x])
    over_y = moves.flip(wide, 2)
    ring.append(moves.turn(after(ring[1], sides[:1] + got[1:] + first[1:]), 1))
    sides.append(moves.flip(ring[1], 1))
    late = to_places(moves, got)
    ring.append(moves.turn(after(ring[2], sides[1:]), 1))
    sides += [moves.flip(v, 1) for v in ring[2:]]
    return first, late, [wide, over_y], [v for pair in zip(ring, sides) for v in pair]


def order(depth, wide):
    out = []
    for at in range(4 * depth):
        if wide:
            out.append((at % depth, at // depth))
        else:
            out.append((at // 4, at // 2 % 2 + at % 2 * 2))
    return out


def exchange(moves, blocks):
    return lax.all_to_all(blocks, AX, 0, 0, tiled=False)


def sent_along(moves, parts):
    return [parts[0]] + [moves.turn(parts[k], k) for k in range(1, moves.depth)]


def to_places(moves, got):
    sent = regrouped(got)
    return [sent[0]] + [moves.flip(sent[p], p) for p in range(1, 4)]


def regrouped(got):
    def regroup(*refs):
        ins, outs = refs[: len(got)], refs[len(got) :]
        for p, place in enumerate(plane_places()):
            for k, ref in enumerate(ins):
                outs[p][k] = ref[place]

    _, read, width = got[0].shape
    outs = [((len(got), read, width), got[0].dtype)] * 4
    return call(regroup, "regroup", 10, got, outs)


def plane_places():
    place = lax.rem(lax.axis_index("fsdp"), 4)
    y, x = place // 2, lax.rem(place, 2)
    return [(1 - y if p & 2 else y) * 2 + (1 - x if p & 1 else x) for p in range(4)]


def total(moves, value):
    value = value + moves.swap(value)
    value = (value + moves.flip(value, 1)) + (moves.flip(value, 2) + moves.flip(value, 3))
    return (value + moves.flip(value, 4)) + (moves.flip(value, 8) + moves.flip(value, 12))


def dot(left, right):
    return jnp.dot(left, right, preferred_element_type=F32)


def dot_right(left, right):
    return lax.dot_general(left, right, (((1,), (1,)), ((), ())), preferred_element_type=F32)


def dot_left(left, right):
    return lax.dot_general(left, right, (((0,), (0,)), ((), ())), preferred_element_type=F32)


def normal(h):
    mean = jnp.mean(h, -1, keepdims=True)
    centered = h - mean
    root = lax.rsqrt(jnp.mean(centered * centered, -1, keepdims=True) + 1e-06)
    return centered * root, root


def normal_back(grad, unit, root, gain):
    scaled = grad * gain
    return root * (
        scaled
        - jnp.mean(scaled, -1, keepdims=True)
        - unit * jnp.mean(scaled * unit, -1, keepdims=True)
    )


def spread(rows):
    read = rows.shape[0]
    tall = jnp.concatenate([rows.astype(F32)] * HEADS, 0)
    return jnp.where(own_head(read), tall, 0.0).astype(BF)


def own_head(read):
    row = lax.broadcasted_iota(jnp.int32, (HEADS * read, D), 0) // read
    lane = lax.broadcasted_iota(jnp.int32, (HEADS * read, D), 1) // HDIM
    return row == lane


def gathered(tall):
    read = tall.shape[0] // HEADS
    kept = jnp.where(own_head(read), tall, 0.0)
    out = kept[0:read]
    for head in range(1, HEADS):
        out = out + kept[head * read : (head + 1) * read]
    return out


def assemble(out_ref, parts, depth):
    if len(parts) == 1:
        out_ref[...] = parts[0][...]
        return
    core, z = lax.axis_index("dp"), lax.axis_index("fsdp") // 4
    rows = parts[0].shape[0]
    for k, part in enumerate(parts):
        half = core if k < depth else 1 - core
        block = half * depth + lax.rem(z - k % depth + depth, depth)
        out_ref[pl.ds(pl.multiple_of(block * rows, rows), rows), :] = part[...]


def square_eye(n):
    row = lax.broadcasted_iota(jnp.int32, (n, n), 0)
    return row == lax.broadcasted_iota(jnp.int32, (n, n), 1)


def column(row):
    return jnp.sum(jnp.where(square_eye(row.shape[1]), row, 0.0), 1, keepdims=True)


def as_row(col):
    return jnp.sum(jnp.where(square_eye(col.shape[0]), col, 0.0), 0, keepdims=True)


def block_place(inner):
    z, depth = lax.axis_index("fsdp") // 4, lax.axis_size("fsdp") // 4
    return lax.rem(inner // 4 - z + depth, depth) * 4 + inner % 4


def pack_blocks(slots, out_ref, own, width):
    inner, read, _ = out_ref.shape
    cores = D // own // inner
    tiles = D // LANES
    lane = lax.broadcasted_iota(jnp.int32, (read, LANES), 1)
    moved = [pltpu.roll(v, own * k, 1) if k else v for k, v in enumerate(slots)]
    for d in range(cores * inner):
        base = own * d
        shift = base % LANES
        held = []
        for tile in range(base // LANES, base // LANES + pl.cdiv(shift + width, LANES)):
            low = tile * LANES - base
            at = (tile % tiles) * LANES
            first = min(max(low, 0) // own, len(slots) - 1)
            last = min(min(low + LANES, width) - 1, len(slots) * own - 1) // own
            part = moved[first][:, at : at + LANES]
            for k in range(first + 1, last + 1):
                part = jnp.where(lane >= k * own - low, moved[k][:, at : at + LANES], part)
            held.append(part)
        block = jnp.concatenate(held, 1)
        if shift:
            block = pltpu.roll(block, len(held) * LANES - shift, 1)
        start = d // inner * width
        out_ref[block_place(d % inner), :, start : start + width] = block[:, :width].astype(BF)


def pack_columns(value, out_ref, own):
    inner, read, _ = out_ref.shape
    tiles = value.shape[1] // LANES
    for d in range(value.shape[1] // own):
        tile, shift = own * d // LANES, own * d % LANES
        first = value[:, tile * LANES : (tile + 1) * LANES]
        if shift:
            at = (tile + 1) % tiles * LANES
            both = jnp.concatenate([first, value[:, at : at + LANES]], 1)
            first = pltpu.roll(both, 2 * LANES - shift, 1)[:, :LANES]
        start = d // inner * LANES
        out_ref[block_place(d % inner), :, start : start + LANES] = first.astype(BF)


def split_blocks(refs, held):
    for k, ref in enumerate(refs):
        ref[...] = held[4 * k : 4 * k + 4]


def head_slots(tall, read):
    return [tall[k * read : (k + 1) * read].astype(F32) for k in range(HEADS)]


def wire_kernel(
    qkv_ref, out_ref, one_ref, two_ref, table_ref, small_ref, step_ref, action_ref, noise_ref,
    act_ref, task_ref, goal_ref, group_ref,
    attn_ref, one_low, two_low, noisy_ref, noise_out, temb_ref, mask_ref, valid_ref,
):
    own = qkv_ref.shape[0]
    one_low[...] = one_ref[...].astype(BF)
    two_low[...] = two_ref[...].astype(BF)
    attn_ref[:, 0 : 3 * D] = qkv_ref[...].astype(BF)
    attn_ref[:, 3 * D : 4 * D] = out_ref[...].astype(BF)
    mask = act_ref[...].astype(F32)
    marks = jnp.sum(mask, 1, keepdims=True)
    first = lax.broadcasted_iota(jnp.int32, (own, 1), 0) == 0
    parts = [table_ref[...]] + [column(small_ref[k : k + 1, :]) for k in range(6)]
    parts += [jnp.where(first, marks, 0.0), jnp.zeros((own, LANES - ACTW - 7), F32)]
    attn_ref[:, 4 * D :] = join(parts).astype(BF)
    pad = LANES - ACTW
    mask_ref[...] = join([mask, jnp.zeros((1, pad), F32)])
    tstep = step_ref[...].astype(F32)
    frac = (tstep / TSTEPS + 0.008) / 1.008
    turn = jnp.cos(frac * (math.pi / 2))
    alpha_bar = turn * turn
    noise = noise_ref[...]
    noisy = jnp.sqrt(alpha_bar) * action_ref[...] + jnp.sqrt(1.0 - alpha_bar) * noise
    zeros = jnp.zeros((noise.shape[0], pad), F32)
    noisy_ref[...] = join([noisy, zeros]).astype(BF)
    noise_out[...] = join([noise, zeros])
    half = D // 2
    place = lax.broadcasted_iota(jnp.int32, (1, half), 1).astype(F32)
    angle = tstep * jnp.exp(place * (-math.log(10000.0) / half))
    temb_ref[...] = join([jnp.sin(angle), jnp.cos(angle)])
    task, seq = task_ref.shape[1], group_ref.shape[1]
    goal = goal_ref[...].astype(F32)
    tasks = task_ref[...].astype(F32) * (1.0 - goal)
    goals = jnp.zeros((1, GOALTOK), F32) + goal
    valid_ref[...] = join([tasks, goals, jnp.ones((1, seq - task - GOALTOK), F32)])


def norm_kernel(depth, n, tok_ref, noisy_ref, temb_ref, *refs):
    parts = refs[:n]
    a_ref, unit_ref, last_ref, gain_ref, count_ref, w_ref, h_ref = refs[n:]
    assemble(w_ref, parts, depth)
    seq, read = tok_ref.shape[0], noisy_ref.shape[0]
    rows = h_ref.shape[0]
    table = w_ref[:, 4 * D :]
    pick = lax.broadcasted_iota(jnp.int32, (8, LANES), 1) - ACTW
    pick = pick == lax.broadcasted_iota(jnp.int32, (8, LANES), 0)
    gains = dot_right(jnp.where(pick, 1.0, 0.0).astype(BF), table)
    gain_ref[...] = gains
    count_ref[...] = read * jnp.sum(gains[6:7, :], 1, keepdims=True)
    embed = dot_right(noisy_ref[...], table)
    last = tok_ref[seq - read :, :].astype(F32) + (embed + temb_ref[...])
    last_ref[...] = last
    for start in range(0, seq, rows):
        h_ref[...] = tok_ref[start : start + rows, :].astype(F32)
        if start + rows == seq:
            h_ref[rows - read :, :] = last
        unit, _ = normal(h_ref[...])
        unit_ref[start : start + rows, :] = unit
        a_ref[start : start + rows, :] = (unit * gains[0:1, :] + gains[1:2, :]).astype(BF)


def attend_kernel(packs, a_ref, last_ref, gain_ref, group_ref, valid_ref, noisy_ref, w_ref, *refs):
    q_ref, qk_ref, p_ref, pa_ref, o_ref, y_ref, a2_ref = refs[:7]
    seq = a_ref.shape[0]
    read = last_ref.shape[0]
    a = a_ref[...]
    q = dot(a_ref[seq - read :, :], w_ref[:, 0:D]).astype(BF)
    q_ref[:, 0:D] = q
    q_ref[:, D:] = noisy_ref[...]
    qk = (dot_right(spread(q), w_ref[:, D : 2 * D]) * HDIM ** (-0.5)).astype(BF)
    qk_ref[...] = qk
    scores = dot_right(qk, a)
    groups = group_ref[...].astype(F32)
    shown = (groups <= column(groups[:, seq - read :])) & (valid_ref[...] > 0)
    place = lax.broadcasted_iota(jnp.int32, (read, seq), 1)
    same = place == lax.broadcasted_iota(jnp.int32, (read, seq), 0) + (seq - read)
    seen = jnp.where(shown | same, 1.0, 0.0)
    seen = jnp.concatenate([seen] * HEADS, 0)
    scores = jnp.where(seen > 0.5, scores, -1000000000.0)
    top = jnp.max(scores, -1, keepdims=True)
    grown = jnp.exp(scores - top)
    probs = grown / jnp.sum(grown, -1, keepdims=True)
    p_ref[...] = probs
    pa = dot(probs.astype(BF), a).astype(BF)
    pa_ref[...] = pa
    o = gathered(dot(pa, w_ref[:, 2 * D : 3 * D])).astype(BF)
    o_ref[...] = o
    y = last_ref[...] + dot(o, w_ref[:, 3 * D : 4 * D])
    y_ref[...] = y
    unit, _ = normal(y)
    a2 = (unit * gain_ref[2:3, :] + gain_ref[3:4, :]).astype(BF)
    a2_ref[...] = a2
    if packs:
        slots = head_slots(pa, read)
        slots += [v.astype(F32) for v in (o, a_ref[seq - read :, :], a2)]
        held = refs[-1]
        pack_blocks(slots, held, D // packs, held.shape[2] // (packs // held.shape[0]))
        split_blocks(refs[7:-1], held)


def feed_kernel(
    depth, n, packs, y_ref, a2_ref, gain_ref, count_ref, noise_ref, mask_ref, w_ref, *refs
):
    m_ref, du_ref, up_ref, f_ref, dh_ref, small_ref, loss_ref, one, two = refs[2 * n :]
    assemble(one, refs[:n], depth)
    assemble(two, refs[n : 2 * n], depth)
    y = y_ref[...]
    a2 = a2_ref[...]
    u = dot(a2, one[...])
    root_two = math.sqrt(2.0 / math.pi)
    curve = jnp.tanh(root_two * (u + 0.044715 * (u * u * u)))
    half = 0.5 * (1.0 + curve)
    m = (u * half).astype(BF)
    slope = half + 0.5 * u * (1.0 - curve * curve) * (root_two * (1.0 + 3.0 * 0.044715 * (u * u)))
    if packs:
        pack_columns(m.astype(F32), m_ref, FF // packs)
    else:
        m_ref[...] = m
    h2 = y + dot(m, two[...])
    unit3, root3 = normal(h2)
    gain3 = gain_ref[4:5, :]
    f = (unit3 * gain3 + gain_ref[5:6, :]).astype(BF)
    f_ref[...] = f
    table = w_ref[:, 4 * D :].astype(F32)
    lane = lax.broadcasted_iota(jnp.int32, table.shape, 1)
    table = jnp.where(lane < ACTW, table, 0.0).astype(BF)
    e = dot(f, table) - noise_ref[...]
    mask = mask_ref[...]
    loss_ref[...] = jnp.sum(jnp.sum(mask * e * e, 1, keepdims=True), 0, keepdims=True)
    de = ((1.0 / count_ref[...]) * 2.0 * mask * e).astype(BF)
    up_ref[:, D:] = de
    df = dot_right(de, table)
    dh2 = normal_back(df, unit3, root3, gain3)
    dh_ref[...] = dh2
    dz = dh2.astype(BF)
    up_ref[:, 0:D] = dz
    du_ref[...] = (slope * dot_right(dz, two[...])).astype(BF)
    small_ref[0:1, :] = jnp.sum(df * unit3, 0, keepdims=True)
    small_ref[1:2, :] = jnp.sum(df, 0, keepdims=True)


def back_kernel(
    packs, a_ref, unit_ref, p_ref, qk_ref, y_ref, dh_ref, du_ref, one_ref, last_ref, gain_ref,
    f_ref, up_ref, small_ref, w_ref, q_ref, *refs,
):
    if packs:
        m_ref, *refs = refs
    low_ref, *refs = refs
    da_ref = refs[-1]
    seq, read = a_ref.shape[0], y_ref.shape[0]
    da2 = dot_right(du_ref[...], one_ref[...])
    unit2, root2 = normal(y_ref[...])
    dy = dh_ref[...] + normal_back(da2, unit2, root2, gain_ref[2:3, :])
    dy_low = dy.astype(BF)
    do = dot_right(dy_low, w_ref[:, 3 * D : 4 * D]).astype(BF)
    a = a_ref[...]
    probs = p_ref[...]
    dv = dot_right(spread(do), w_ref[:, 2 * D : 3 * D]).astype(BF)
    dp = dot_right(dv, a)
    ds = (probs * (dp - jnp.sum(dp * probs, -1, keepdims=True))).astype(BF)
    dsa = dot(ds, a).astype(BF)
    dq = (gathered(dot(dsa, w_ref[:, D : 2 * D])) * HDIM ** (-0.5)).astype(BF)
    low_ref[:, 0:D] = dy_low
    low_ref[:, D : 2 * D] = do
    low_ref[:, 2 * D : 3 * D] = dq
    low_ref[:, 3 * D : 4 * D] = q_ref[:, 0:D]
    low_ref[:, 4 * D : 5 * D + LANES] = up_ref[...]
    low_ref[:, 5 * D + LANES :] = q_ref[:, D:]
    da_ref[...] = dot_left(ds, qk_ref[...]) + dot_left(probs.astype(BF), dv)
    da_ref[seq - read :, :] = da_ref[seq - read :, :] + dot_right(dq, w_ref[:, 0:D])
    unit, root = normal(last_ref[...])
    dh = dy + normal_back(da_ref[seq - read :, :], unit, root, gain_ref[0:1, :])
    demb = dh.astype(BF)
    da = da_ref[...]
    sums = jnp.concatenate(
        [
            jnp.sum(da * unit_ref[...], 0, keepdims=True),
            jnp.sum(da, 0, keepdims=True),
            jnp.sum(da2 * unit2, 0, keepdims=True),
            jnp.sum(da2, 0, keepdims=True),
            small_ref[0:2, :],
        ],
        0,
    )
    high = sums.astype(BF).astype(F32)
    split = jnp.concatenate([high, sums - high, jnp.zeros((read - 12, D), F32)], 0)
    if packs:
        slots = head_slots(dsa, read)
        slots += [f_ref[...].astype(F32), demb.astype(F32), split]
        held = refs[-2]
        width = held.shape[2] - m_ref.shape[2]
        pack_blocks(slots, held, D // packs, width // (packs // held.shape[0]))
        held[:, :, width:] = m_ref[...]
        split_blocks(refs[:-2], held)
    else:
        dsa_ref, demb_ref, split_ref = refs[:3]
        dsa_ref[...] = dsa
        demb_ref[...] = demb
        split_ref[...] = split.astype(BF)


def own_rows(out_ref, got_refs, places, base=0):
    core = lax.axis_index("dp")
    read, width = got_refs[0].shape[1], out_ref.shape[2]
    for side in range(2):
        start = base + (core if side == 0 else 1 - core) * width
        lanes = pl.ds(pl.multiple_of(start, LANES), width)
        for at, (k, p) in enumerate(places):
            out_ref[side, at * read : (at + 1) * read, :] = got_refs[p][k, :, lanes]


def fill(out_ref, refs):
    rows = refs[0].shape[0]
    for k, ref in enumerate(refs):
        out_ref[k * rows : (k + 1) * rows, :] = ref[...]


def join(columns):
    return jnp.concatenate(columns, 1)


def head_blocks(tall, own):
    lane = lax.broadcasted_iota(jnp.int32, (own, D), 1) // HDIM
    out = tall[0:own]
    for head in range(1, HEADS):
        out = jnp.where(lane == head, tall[head * own : (head + 1) * own], out)
    return out


def statistics(grad, rows_old):
    beta = 1.0 - float(STEP) ** (-0.8)
    squares = grad * grad
    rows = beta * rows_old + (1.0 - beta) * jnp.sum(squares, 1, keepdims=True)
    return rows, jnp.sum(squares, 0, keepdims=True), jnp.sum(squares / rows, 0, keepdims=True)


def grads_kernel(depth, own, n, *refs):
    early_refs, late_refs, one_refs, low_refs = refs[:4], refs[4:8], refs[8:10], refs[10 : 10 + n]
    mine_ref, theirs_ref, late, early, mid, wide, one, low = refs[10 + n :]
    read = early_refs[0].shape[1]
    own_two = FF // (D // own)
    ring = order(depth, False)
    own_rows(late, late_refs, ring)
    own_rows(mid, late_refs, ring, 2 * SLOTS * own)
    own_rows(early, early_refs, ring)
    own_rows(wide, early_refs, order(depth, True))
    fill(one, one_refs)
    fill(low, low_refs)
    da, do, dq, q = (low[:, k * D : (k + 1) * D] for k in range(4))
    dz, de = low[:, 4 * D : 5 * D], low[:, 5 * D : 5 * D + LANES]
    noisy = low[:, 5 * D + LANES :]
    at = HEADS * own - 256
    count = low.shape[0]
    row = lax.rem(lax.broadcasted_iota(jnp.int32, (count, LANES), 0), read)
    lane = lax.broadcasted_iota(jnp.int32, (count, LANES), 1)
    pick = jnp.where((row == lane) | (row == lane + 6), 1.0, 0.0)
    pick = jnp.where(lane < 6, pick, 0.0).astype(BF)
    for side, out_ref in enumerate((mine_ref, theirs_ref)):
        out_ref[0:own_two, :] = dot_left(mid[side], dz)[:own_two]
        tail = early[side, :, 256:384]
        last = late[side, :, 256:384]
        table = dot_left(last, de)[at : at + own] + dot_left(last, noisy)[at + own : at + 2 * own]
        blocks = [
            dot_left(tail, da)[at : at + own],
            dot_left(tail, dq)[at + own : at + 2 * own],
            head_blocks(dot_left(late[side], q), own) * HDIM ** (-0.5),
            head_blocks(dot_left(early[side], do), own),
            jnp.concatenate(
                [table, dot_left(pick, last)[:own], jnp.zeros((own, D - 2 * LANES), F32)], 1
            ),
        ]
        tail = wide[side, :, 256:384]
        blocks += [
            dot_left(tail, one[:, k * D : (k + 1) * D])[at + 2 * own : at + 3 * own]
            for k in range(FF // D)
        ]
        for k, block in enumerate(blocks):
            start = own_two + k * own
            out_ref[start : start + own, :] = block


def sums_kernel(
    mine_ref, got_ref, loss_ref, r_qkv_ref, r_out_ref, r_one_ref, r_two_ref, var_table_ref,
    var_small_ref,
    g_qkv_ref, n_qkv_ref, g_out_ref, n_out_ref, g_one_ref, n_one_ref, g_two_ref, n_two_ref,
    g_table_ref, n_table_ref, u_table_ref, g_small_ref, n_small_ref, u_small_ref, stat_ref,
):
    own, own_two = g_out_ref.shape[0], g_two_ref.shape[0]
    both = mine_ref[...] + got_ref[...]
    g_out, g_q, g_k, g_v, plain, *ones = (
        both[own_two + k * own : own_two + (k + 1) * own] for k in range(5 + FF // D)
    )
    mats = (
        (join([g_q, g_k, g_v]), r_qkv_ref, g_qkv_ref, n_qkv_ref),
        (g_out, r_out_ref, g_out_ref, n_out_ref),
        (join(ones), r_one_ref, g_one_ref, n_one_ref),
        (both[0:own_two], r_two_ref, g_two_ref, n_two_ref),
    )
    cols, overs, wholes = [], [], []
    for grad, old_ref, g_ref, n_ref in mats:
        g_ref[...] = grad
        rows, col, over = statistics(grad, column(old_ref[...]))
        n_ref[...] = as_row(rows)
        cols.append(col)
        overs.append(over)
        wholes.append(jnp.sum(rows))
    at = LANES + (HEADS + 2) * own - 256
    beta = 1.0 - float(STEP) ** (-0.8)
    squares = jnp.zeros((), F32)
    for grad, old_ref, g_ref, n_ref, u_ref in (
        (plain[:, 0:ACTW], var_table_ref, g_table_ref, n_table_ref, u_table_ref),
        (plain[0:6, at : at + own], var_small_ref, g_small_ref, n_small_ref, u_small_ref),
    ):
        new = beta * old_ref[...] + (1.0 - beta) * grad * grad
        unit = grad * lax.rsqrt(new)
        g_ref[...] = grad
        n_ref[...] = new
        u_ref[...] = unit
        squares = squares + jnp.sum(unit * unit)
    height, width = stat_ref.shape
    lane = lax.broadcasted_iota(jnp.int32, (1, height * width - 18 * D), 1)
    singles = jnp.where(lane == 5, loss_ref[...], 0.0)
    for k, value in enumerate(wholes + [squares]):
        singles = jnp.where(lane == k, value, singles)
    row = join(cols + overs + [singles])
    for k in range(height):
        stat_ref[k : k + 1, :] = row[:, k * width : (k + 1) * width]


def flat(square):
    return jnp.concatenate([square[k : k + 1, :] for k in range(square.shape[0])], 1)


def folded(row):
    return jnp.concatenate(
        [row[:, k * LANES : (k + 1) * LANES] for k in range(row.shape[1] // LANES)], 0
    )


def renew_kernel(entries, stat_ref, *refs):
    ins, outs = refs[:20], refs[20:]
    beta = 1.0 - float(STEP) ** (-0.8)
    row = flat(stat_ref[...])
    cuts, at = [], 0
    for width in (3 * D, D, FF, D, 3 * D, D, FF, D):
        cuts.append(row[:, at : at + width])
        at += width
    squares = row[:, at + 4 : at + 5]
    loss = row[:, at + 5 : at + 6]
    news = []
    for k in range(4):
        old_ref = ins[4 * k]
        whole = row[:, at + k : at + k + 1]
        new = beta * flat(old_ref[...]) + (1.0 - beta) * cuts[k]
        squares = squares + whole * jnp.sum(cuts[4 + k] / new, 1, keepdims=True)
        news.append((new, whole))
    clip = jnp.sqrt(squares / entries)
    factor = 1.0 / jnp.maximum(1.0, clip / clip_level)
    for k, (new, whole) in enumerate(news):
        _, rows_ref, grad_ref, master_ref = ins[4 * k : 4 * k + 4]
        unit = grad_ref[...] * lax.rsqrt(column(rows_ref[...]) * new / whole)
        outs[2 * k][...] = folded(new)
        outs[2 * k + 1][...] = master_ref[...] - rate_matrix * unit * factor
    unit_ref, master_ref = ins[16:18]
    outs[8][...] = master_ref[...] - rate_matrix * unit_ref[...] * factor
    unit_ref, master_ref = ins[18:20]
    outs[9][...] = master_ref[...] - rate_small * unit_ref[...] * factor
    outs[10][...] = loss
    outs[11][...] = clip


VMEM = pl.BlockSpec(memory_space=pltpu.VMEM)


def shape(dims, dtype):
    return jax.ShapeDtypeStruct(dims, dtype)


def params(mib):
    return pltpu.CompilerParams(vmem_limit_bytes=mib * MIB)


def call(kernel, name, mib, ins, outs, scratch=(), moved=1):
    return pl.pallas_call(
        kernel,
        cost_estimate=pl.CostEstimate(
            flops=0, bytes_accessed=moved * MIB, transcendentals=0
        ),
        out_shape=tuple(shape(*out) for out in outs),
        in_specs=[VMEM] * len(ins),
        out_specs=(VMEM,) * len(outs),
        scratch_shapes=[pltpu.VMEM(*one) for one in scratch],
        compiler_params=pltpu.CompilerParams(vmem_limit_bytes=mib * MIB),
        name=name,
    )(*ins)


def run_wire(ins):
    w_qkv, w_out, w_one, w_two = ins[:4]
    own, read = w_qkv.shape[0], ins[7].shape[0]
    outs = [((own, 4 * D + LANES), BF), (w_one.shape, BF), (w_two.shape, BF)]
    outs += [((read, LANES), BF), ((read, LANES), F32), ((1, D), F32), ((1, LANES), F32)]
    outs.append((ins[12].shape, F32))
    return call(wire_kernel, "wire", 60, ins, outs, moved=6)


def run_norm(moves, tokens, noisy, temb, parts):
    seq, read = tokens.shape[0], noisy.shape[0]
    outs = [((seq, D), BF), ((seq, D), F32), ((read, D), F32), ((8, D), F32), ((1, 1), F32)]
    outs.append(((D, parts[0].shape[1]), BF))
    kernel = functools.partial(norm_kernel, moves.depth, len(parts))
    ins = (tokens, noisy, temb, *parts)
    return call(kernel, "norm_tokens", 20, ins, outs, [((seq // 6, D), F32)], moved=6)


def run_attend(moves, normed, last, *ins):
    seq, read = normed.shape[0], last.shape[0]
    tall = HEADS * read
    outs = [
        ((read, D + LANES), BF),
        ((tall, D), BF),
        ((tall, seq), F32),
        ((tall, D), BF),
        ((read, D), BF),
        ((read, D), F32),
        ((read, D), BF),
    ]
    packs, scratch = 0, []
    if moves.fast:
        packs = moves.count
        width = moves.dp * SLOTS * D // packs
        outs += [((4, read, width), BF)] * moves.depth
        scratch.append(((moves.fsdp, read, width), BF))
    kernel = functools.partial(attend_kernel, packs)
    return call(kernel, "attend", 14, (normed, last, *ins), outs, scratch, moved=11)


def run_feed(moves, y, a2, gains, count, noise, mask, weights, one, two):
    read = y.shape[0]
    packs = moves.count if moves.fast else 0
    outs = [
        ((moves.fsdp, read, moves.dp * LANES) if packs else (read, FF), BF),
        ((read, FF), BF),
        ((read, D + LANES), BF),
        ((read, D), BF),
        ((read, D), F32),
        ((2, D), F32),
        ((1, 1), F32),
        ((D, FF), BF),
    ]
    ins = (y, a2, gains, count, noise, mask, weights, *one, *two)
    kernel = functools.partial(feed_kernel, moves.depth, len(one), packs)
    return call(kernel, "feed", 24, ins, outs, [((FF, D), BF)], moved=17)


def run_back(moves, read, *ins):
    seq = ins[0].shape[0]
    outs = [((read, 5 * D + 2 * LANES), BF)]
    packs, scratch = 0, []
    if moves.fast:
        packs = moves.count
        width = moves.dp * (SLOTS * D // packs + LANES)
        outs += [((4, read, width), BF)] * moves.depth
        scratch.append(((moves.fsdp, read, width), BF))
    else:
        outs += [((HEADS * read, D), BF), ((read, D), BF), ((read, D), BF)]
    scratch.append(((seq, D), F32))
    return call(functools.partial(back_kernel, packs), "back", 20, ins, outs, scratch, moved=19)


def run_grads(moves, early, late, one, low, own):
    rows = moves.fsdp * early[0].shape[1]
    outs = [((9 * own + FF // moves.count, D), F32)] * 2
    scratch = [((2, rows, SLOTS * own), BF)] * 2 + [((2, rows, LANES), BF)]
    scratch += [((2, rows, SLOTS * own), BF)]
    scratch += [((rows, one[0].shape[1]), BF), ((rows, low[0].shape[1]), BF)]
    kernel = functools.partial(grads_kernel, moves.depth, own, len(low))
    return call(kernel, "grads", 20, (*early, *late, *one, *low), outs, scratch, moved=6)


def run_sums(mine, got, loss, rows_old, var_table, var_small):
    own, own_two = rows_old[0].shape[0], rows_old[3].shape[0]
    outs = []
    for height, width in ((own, 3 * D), (own, D), (own, FF), (own_two, D)):
        outs += [((height, width), F32), ((1, height), F32)]
    outs += [((own, ACTW), F32)] * 3 + [((6, own), F32)] * 3 + [((16, 7 * LANES), F32)]
    ins = (mine, got, loss, *(r[None, :] for r in rows_old), var_table, var_small)
    return call(sums_kernel, "sums", 16, ins, outs, moved=7)


def run_renew(stats, mats, plain):
    ins, outs = [stats], []
    for cols, rows, grad, master in mats:
        ins += [cols.reshape(-1, LANES), rows, grad, master]
        outs += [((cols.shape[0] // LANES, LANES), F32), (master.shape, F32)]
    for update, master in plain:
        ins += [update, master]
        outs.append((master.shape, F32))
    outs += [((1, 1), F32)] * 2
    entries = float(4 * D * D + 2 * D * FF + D * ACTW + 6 * D)
    return call(functools.partial(renew_kernel, entries), "renew", 60, ins, outs, moved=10)


def to_owners(slots, count):
    kinds, read, width = slots.shape
    own = width // count
    blocks = slots.reshape(kinds, read, count, own).transpose(2, 1, 0, 3)
    return blocks.reshape(count, read, kinds * own)


def lanes_to(value, width):
    return jnp.pad(value, ((0, 0), (0, width - value.shape[1])))


def heads_own(tall, own):
    lane = jnp.arange(D) // HDIM
    keep = lane[None, None, :] == jnp.arange(HEADS)[:, None, None]
    return jnp.sum(jnp.where(keep, tall.reshape(HEADS, own, D), 0.0), 0)


def on_device(moves, *arrays):
    (
        tokens, actions, noise, timesteps, task_mask, goal_flag, act_mask, groups,
        w_qkv, rows_qkv, cols_qkv, w_out, rows_out, cols_out,
        w_one, rows_one, cols_one, w_two, rows_two, cols_two,
        w_table, var_table, small, var_small,
    ) = arrays
    tokens, read, own = tokens[0], noise.shape[1], w_qkv.shape[0]
    seq = tokens.shape[0]
    attn, one, two, noisy, noise, temb, mask, valid = run_wire(
        (
            w_qkv, w_out, w_one, w_two, w_table, small.T, timesteps[:, None], actions[0], noise[0],
            act_mask, task_mask, goal_flag[:, None], groups,
        )
    )
    attn, one, two = gather_weights(moves, attn, one, two)
    normed, unit, last, gains, entries_count, attn = run_norm(moves, tokens, noisy, temb, attn)
    q, qk, probs, pa, o, y, a2, *early = run_attend(
        moves, normed, last, gains, groups, valid, noisy, attn
    )
    m, du, up, f, dh, small_up, loss, one_full = run_feed(
        moves, y, a2, gains, entries_count, noise, mask, attn, one, two
    )
    extra = ()
    if moves.fast:
        first = sent_along(moves, early)
        extra = (m,)
    low, *late = run_back(
        moves, read, normed, unit, probs, qk, y, dh, du, one_full, last, gains, f, up, small_up,
        attn, q, *extra,
    )
    entries_count = entries_count.reshape(())
    if not moves.fast:
        factors = (pa, o, normed[seq - read :], a2, m, du, f, low) + tuple(late)
        return plain_update(moves, factors, loss, entries_count, arrays[8:])
    got_early, got_late, all_du, all_low = gather_last(moves, first, late, du, low)
    mine, theirs = run_grads(moves, got_early, got_late, all_du, all_low, own)
    (
        g_qkv, n_qkv, g_out, n_out, g_one, n_one, g_two, n_two,
        g_table, v_table, u_table, g_small, v_small, u_small, stats,
    ) = run_sums(
        mine, moves.swap(theirs), loss, (rows_qkv, rows_out, rows_one, rows_two), var_table,
        var_small.T,
    )
    news = run_renew(
        total(moves, stats),
        (
            (cols_qkv, n_qkv, g_qkv, w_qkv),
            (cols_out, n_out, g_out, w_out),
            (cols_one, n_one, g_one, w_one),
            (cols_two, n_two, g_two, w_two),
        ),
        ((u_table, w_table), (u_small, small.T)),
    )
    result = [news[10].reshape(()), entries_count, news[11].reshape(())]
    for k, (grad, rows) in enumerate(
        ((g_qkv, n_qkv), (g_out, n_out), (g_one, n_one), (g_two, n_two))
    ):
        result += [grad, rows.reshape(-1), news[2 * k].reshape(-1), news[2 * k + 1]]
    return tuple(result + [g_table, v_table, news[8], g_small.T, v_small.T, news[9].T])


def plain_update(moves, factors, loss, entries_count, arrays):
    (
        w_qkv, rows_qkv, cols_qkv, w_out, rows_out, cols_out,
        w_one, rows_one, cols_one, w_two, rows_two, cols_two,
        w_table, var_table, small, var_small,
    ) = arrays
    pa, o, normed, a2, m, du, f, low, dsa, demb, split = factors
    read, count, own = low.shape[0], moves.count, w_qkv.shape[0]
    early = jnp.concatenate(
        [pa.reshape(HEADS, read, D), jnp.stack([o, normed, a2, jnp.zeros_like(a2)])], 0
    )
    late = jnp.concatenate(
        [dsa.reshape(HEADS, read, D), jnp.stack([f, demb, split, jnp.zeros_like(f)])], 0
    )
    n_rows = count * read
    got_early = exchange(moves, to_owners(early, count)).reshape(n_rows, SLOTS * own)
    got_mid = exchange(moves, m.reshape(read, count, FF // count).transpose(1, 0, 2))
    got_mid = got_mid.reshape(n_rows, FF // count)
    got_late = exchange(moves, to_owners(late, count)).reshape(n_rows, SLOTS * own)
    all_du = lax.all_gather(du, AX, axis=0, tiled=True)
    all_low = lax.all_gather(low, AX, axis=0, tiled=True)
    all_da, all_do, all_dq, all_q, all_dz = (all_low[:, k * D : (k + 1) * D] for k in range(5))
    all_de, all_noisy = all_low[:, 5 * D : 5 * D + LANES], all_low[:, 5 * D + LANES :]

    heads = HEADS * own

    def slot(array, k):
        return array[:, k * own : (k + 1) * own]

    g_v = heads_own(dot_left(got_early[:, :heads], all_do), own)
    g_out = dot_left(slot(got_early, HEADS), all_da)
    g_one = dot_left(slot(got_early, HEADS + 2), all_du)
    g_two = dot_left(got_mid, all_dz)
    g_q = dot_left(slot(got_early, HEADS + 1), all_dq)
    g_k = heads_own(dot_left(got_late[:, :heads], all_q), own) * HDIM ** (-0.5)
    g_qkv = jnp.concatenate([g_q, g_k, g_v], 1)
    g_table = (
        dot_left(slot(got_late, HEADS), all_de) + dot_left(slot(got_late, HEADS + 1), all_noisy)
    )[:, :ACTW]
    parts = jnp.sum(slot(got_late, HEADS + 2).reshape(count, read, own).astype(F32), 0)
    g_small = (parts[0:6] + parts[6:12]).T

    beta = 1.0 - float(STEP) ** (-0.8)
    mats = (g_qkv, g_out, g_one, g_two)
    squares = tuple((g * g for g in mats))
    rows_new = tuple(
        (
            beta * r + (1.0 - beta) * jnp.sum(sq, 1)
            for r, sq in zip((rows_qkv, rows_out, rows_one, rows_two), squares)
        )
    )
    var_table_new = beta * var_table + (1.0 - beta) * g_table * g_table
    var_small_new = beta * var_small + (1.0 - beta) * g_small * g_small
    unit_table = g_table * lax.rsqrt(var_table_new)
    unit_small = g_small * lax.rsqrt(var_small_new)
    vector_squares = jnp.sum(unit_table * unit_table) + jnp.sum(unit_small * unit_small)
    col_parts = [jnp.sum(sq, 0) for sq in squares]
    over_rows = [jnp.sum(sq / r[:, None], 0) for sq, r in zip(squares, rows_new)]
    singles = jnp.stack([jnp.sum(r) for r in rows_new] + [vector_squares, loss[0, 0]])
    sums = jnp.concatenate(col_parts + over_rows + [singles])
    length = sums.shape[0]
    sums = jnp.pad(sums, (0, -length % (8 * LANES))).reshape(-1, LANES)
    sums = lax.psum(sums, AX).reshape(-1)[:length]
    cuts = []
    at = 0
    for size in [c.shape[0] for c in col_parts] * 2:
        cuts.append(sums[at : at + size])
        at += size
    totals = [sums[at + k] for k in range(4)]
    squares_total, loss_sum = sums[at + 4], sums[at + 5]
    cols_new = tuple(
        (
            beta * c + (1.0 - beta) * s
            for c, s in zip((cols_qkv, cols_out, cols_one, cols_two), cuts[:4])
        )
    )
    for c, over, t in zip(cols_new, cuts[4:], totals):
        squares_total = squares_total + t * jnp.sum(over / c)
    units = tuple(
        (
            g * lax.rsqrt(r[:, None] * c[None, :] / t)
            for g, r, c, t in zip(mats, rows_new, cols_new, totals)
        )
    )
    entries = 4 * D * D + 2 * D * FF + D * ACTW + 6 * D
    clip_rms = jnp.sqrt(squares_total / entries)
    factor = 1.0 / jnp.maximum(1.0, clip_rms / clip_level)
    result = [loss_sum, entries_count, clip_rms]
    for master, grad, rows, cols, update in zip(
        (w_qkv, w_out, w_one, w_two), mats, rows_new, cols_new, units
    ):
        result += [grad, rows, cols, master - rate_matrix * update * factor]
    result += [g_table, var_table_new, w_table - rate_matrix * unit_table * factor]
    result += [g_small, var_small_new, small - rate_small * unit_small * factor]
    return tuple(result)


def solution(mesh):
    rows = P(AX)
    items = (rows,) * 8
    matrix = (rows, rows, P())
    plain = (rows, rows)
    return jax.shard_map(
        functools.partial(on_device, Moves(mesh)),
        mesh=mesh,
        in_specs=items + matrix * 4 + plain * 2,
        out_specs=(P(),) * 3 + (rows, rows, P(), rows) * 4 + (rows,) * 6,
        check_vma=False,
    )
```

time: 249 us -> 193 us (0.78)
  waiting for transfers between devices: 127 us -> 88.9 us
  local copies, waits for them, and re-layouts: 13.5 us -> 0.09 us
  starting transfers between devices: 66.3 us -> 72.3 us
  other arithmetic: 9.94 us -> 4.83 us
  Pallas kernels: 28.4 us -> 24.4 us
    ppermute x33 -> x37, waiting for transfers between devices: 79.9 us -> 48.4 us  [flip(): lax.ppermute(value, 'fsdp', [(i, i ^ mask) for i in range(self.fsdp)])]
    ppermute x18 -> x21, waiting for transfers between devices: 45.8 us -> 32.3 us  [turn(): lax.ppermute(value, 'fsdp', [(i, (i + 4 * step) % self.fsdp) for i in ran...]
    unnamed x72 -> x36, local copies, waits for them, and re-layouts: 13.3 us -> 0.09 us
    ppermute x33 -> x37, starting transfers between devices: 37.9 us -> 46.3 us  [flip(): lax.ppermute(value, 'fsdp', [(i, i ^ mask) for i in range(self.fsdp)])]
    ppermute x15 -> x14, waiting for transfers between devices: 1.52 us -> 8.2 us  [swap(): return lax.ppermute(value, 'dp', [(0, 1), (1, 0)])]
    select_n x23, other arithmetic: 8.35 us -> 4.17 us  [pair(): jnp.where(bit == 0, jnp.concatenate([own, other], 1), jnp.concatenate([ot...]
    pallas_call x10, Pallas kernels: 28.4 us -> 24.3 us  [call(): pl.pallas_call(kernel, cost_estimate=pl.CostEstimate(flops=0, bytes_acces...]
    all_to_all x1 -> x0, starting transfers between devices: 3.63 us -> none  [exchange(): lax.all_to_all(blocks, 'fsdp' if moves.fast else AX, 0, 0, tiled=False)]
  transfers between devices with their start and end apart: 67 -> 72, of which waited for: 35 -> 37; matrix products, arithmetic and copies ran while one was open for 4% -> 2% of each run, Pallas kernels for 3% -> 6%
where the time goes in v3:
time: 193 us
  waiting for transfers between devices  88.9 us (46%)
  starting transfers between devices  72.3 us (37%)
  Pallas kernels  24.4 us (13%)
  other arithmetic  4.83 us (3%)
  between operations  2.65 us (1%)
    ppermute x37, waiting for transfers between devices, flip(): lax.ppermute(value, 'fsdp', [(i, i ^ mask) for i in range(self.fsdp)])  48.4 us
    ppermute x37, starting transfers between devices, flip(): lax.ppermute(value, 'fsdp', [(i, i ^ mask) for i in range(self.fsdp)])  46.3 us
    ppermute x21, waiting for transfers between devices, turn(): lax.ppermute(value, 'fsdp', [(i, (i + 4 * step) % self.fsdp) for i in ran...  32.3 us
    pallas_call x10, Pallas kernels, call(): pl.pallas_call(kernel, cost_estimate=pl.CostEstimate(flops=0, bytes_acces...  24.3 us
    ppermute x21, starting transfers between devices, turn(): lax.ppermute(value, 'fsdp', [(i, (i + 4 * step) % self.fsdp) for i in ran...  23.6 us
    ppermute x14, waiting for transfers between devices, swap(): return lax.ppermute(value, 'dp', [(0, 1), (1, 0)])  8.2 us
    select_n x23, other arithmetic, pair(): jnp.where(bit == 0, jnp.concatenate([own, other], 1), jnp.concatenate([ot...  4.17 us
  transfers between devices with their start and end apart: 72, of which 37 were waited for; matrix products, arithmetic and copies ran while one was open for 2% of the time, Pallas kernels for 6%

profile of v3, /device:TPU:0, one launch (start us, length us, event | category | flops | bytes accessed | tf_op | source)
XLA Modules:
  0.0 193.1 jit_solution(3904217474358821853)
XLA Ops:
  2.0 2.2 %wire.1 = (bf16[24,3200]{1,0:T(8,128)(2,1)}, bf16[24,3072]{1,0:T(8,128)(2,1)}, bf16[96,768]{1,0:T(8,128)(2,1)}, bf16[16,128]{1,0:T(8,128)(2,1)}, f32[16,128]{1,0...) custom-call(f32[24,2304]{1,0:T(8,128)} %refs_3_.1, f32[24,768]{1,0:T(8,128)} %refs_7_.1, ...), custom_call_target="tpu_custom_call" | custom-call | bytes 6291456 | tf_op jit(solution)/shard_map/wire/pallas_call | solution.py:710
  4.2 3.0 %collective-permute-start.18 = (bf16[24,3072]{1,0:T(8,128)(2,1)}, bf16[24,3072]{1,0:T(8,128)(2,1)S(1)}, u32[]{:S(2)}, u32[]{:S(2)}) collective-permute-start(bf16[24,3072]{1,0:T(8,128)(2,1)} %get-tuple-element.144), channel_id=1, source_target_pairs={{0,2},{1,3},{2,0},{3,1},{4,6},{5,7},{6,4},{7,5},{8,10},{9,11},{10,... | collective-permute-start | bytes 442376 | tf_op jit(solution)/shard_map/ppermute | solution.py:40
  21.9 3.1 %collective-permute-done.33 = bf16[96,768]{1,0:T(8,128)(2,1)S(1)} collective-permute-done((bf16[96,768]{1,0:T(8,128)(2,1)S(1)}, bf16[96,768]{1,0:T(8,128)(2,1)S(1)}, u32[]{:S(2)}, u32[]{:S(2)}) %collective-permute-start.33) | collective-permute-done | bytes 147488 | tf_op jit(solution)/shard_map/ppermute | solution.py:40
  29.4 6.8 %collective-permute-done.36 = bf16[96,768]{1,0:T(8,128)(2,1)S(1)} collective-permute-done((bf16[96,768]{1,0:T(8,128)(2,1)S(1)}, bf16[96,768]{1,0:T(8,128)(2,1)S(1)}, u32[]{:S(2)}, u32[]{:S(2)}) %collective-permute-start.36) | collective-permute-done | bytes 147488 | tf_op jit(solution)/shard_map/ppermute | solution.py:40
  38.6 4.5 %collective-permute-done.38 = bf16[96,768]{1,0:T(8,128)(2,1)S(1)} collective-permute-done((bf16[96,768]{1,0:T(8,128)(2,1)S(1)}, bf16[96,768]{1,0:T(8,128)(2,1)S(1)}, u32[]{:S(2)}, u32[]{:S(2)}) %collective-permute-start.38) | collective-permute-done | bytes 147488 | tf_op jit(solution)/shard_map/ppermute | solution.py:43
  47.6 2.2 %collective-permute-done.39 = bf16[96,768]{1,0:T(8,128)(2,1)S(1)} collective-permute-done((bf16[96,768]{1,0:T(8,128)(2,1)S(1)}, bf16[96,768]{1,0:T(8,128)(2,1)S(1)}, u32[]{:S(2)}, u32[]{:S(2)}) %collective-permute-start.39) | collective-permute-done | bytes 147488 | tf_op jit(solution)/shard_map/ppermute | solution.py:40
  54.7 2.4 %collective-permute-done.22 = bf16[48,3072]{1,0:T(8,128)(2,1)S(1)} collective-permute-done((bf16[48,3072]{1,0:T(8,128)(2,1)S(1)}, bf16[48,3072]{1,0:T(8,128)(2,1)S(1)}, u32[]{:S(2)}, u32[]{:S(2)}) %collective-permute-start.22) | collective-permute-done | bytes 294944 | tf_op jit(solution)/shard_map/ppermute | solution.py:43
  57.3 2.5 %collective-permute-done.21 = bf16[48,3072]{1,0:T(8,128)(2,1)S(1)} collective-permute-done((bf16[48,3072]{1,0:T(8,128)(2,1)S(1)}, bf16[48,3072]{1,0:T(8,128)(2,1)S(1)}, u32[]{:S(2)}, u32[]{:S(2)}) %collective-permute-start.21) | collective-permute-done | bytes 294944 | tf_op jit(solution)/shard_map/ppermute | solution.py:40
  61.0 2.6 %collective-permute-done.4 = bf16[48,3200]{1,0:T(8,128)(2,1)S(1)} collective-permute-done((bf16[48,3200]{1,0:T(8,128)(2,1)S(1)}, bf16[48,3200]{1,0:T(8,128)(2,1)S(1)}, u32[]{:S(2)}, u32[]{:S(2)}) %collective-permute-start.4) | collective-permute-done | bytes 307232 | tf_op jit(solution)/shard_map/ppermute | solution.py:43
  65.1 7.1 %collective-permute-done.6 = bf16[48,3200]{1,0:T(8,128)(2,1)S(1)} collective-permute-done((bf16[48,3200]{1,0:T(8,128)(2,1)S(1)}, bf16[48,3200]{1,0:T(8,128)(2,1)S(1)}, u32[]{:S(2)}, u32[]{:S(2)}) %collective-permute-start.6) | collective-permute-done | bytes 307232 | tf_op jit(solution)/shard_map/ppermute | solution.py:43
  74.4 4.7 %collective-permute-done.7 = bf16[48,3200]{1,0:T(8,128)(2,1)S(1)} collective-permute-done((bf16[48,3200]{1,0:T(8,128)(2,1)S(1)}, bf16[48,3200]{1,0:T(8,128)(2,1)S(1)}, u32[]{:S(2)}, u32[]{:S(2)}) %collective-permute-start.7) | collective-permute-done | bytes 307232 | tf_op jit(solution)/shard_map/ppermute | solution.py:40
  88.3 3.4 %attend.1 = (bf16[16,896]{1,0:T(8,128)(2,1)S(1)}, bf16[192,768]{1,0:T(8,128)(2,1)S(1)}, f32[192,864]{1,0:T(8,128)S(1)}, bf16[192,768]{1,0:T(8,128)(2,1)}, bf16[1...) custom-call(bf16[864,768]{1,0:T(8,128)(2,1)S(1)} %get-tuple-element., ...), custom_call_target="tpu_custom_call" | custom-call | bytes 11534336 | tf_op jit(solution)/shard_map/attend/pallas_call | solution.py:710
  91.7 4.8 %feed.1 = (bf16[16,16,256]{2,1,0:T(8,128)(2,1)S(1)}, bf16[16,3072]{1,0:T(8,128)(2,1)S(1)}, bf16[16,896]{1,0:T(8,128)(2,1)S(1)}, bf16[16,768]{1,0:T(8,128)(2,1)S(...) custom-call(f32[16,768]{1,0:T(8,128)S(1)} %get-tuple-element.139.y_ref, ...), custom_call_target="tpu_custom_call" | custom-call | bytes 17825792 | tf_op jit(solution)/shard_map/feed/pallas_call | solution.py:710
  104.4 5.6 %back.1 = (bf16[16,4096]{1,0:T(8,128)(2,1)S(1)}, bf16[4,16,1024]{2,1,0:T(8,128)(2,1)S(1)}, bf16[4,16,1024]{2,1,0:T(8,128)(2,1)S(1)}, bf16[4,16,1024]{2,1,0:T(8,128)(2,1)S(1)}, bf16[4,16,1024]{2,1,0:T(8,128)(2,1)S(1)}) custom-call(bf16[864,768]{1,0:T(8,128)(2,1)S(1)} %get-tuple-element.123.a_ref, f32[864,768]{1,0:T(8,128)S(1)} %get-tuple-element.136.unit_ref, ...), custom_call_target="tpu_custom_call" | custom-call | bytes 19922944 | tf_op jit(solution)/shard_map/back/pallas_call | solution.py:710
  118.0 6.4 %collective-permute-done.15.refs_1_ = bf16[4,16,768]{2,1,0:T(8,128)(2,1)S(1)} collective-permute-done((bf16[4,16,768]{2,1,0:T(8,128)(2,1)S(1)}, bf16[4,16,768]{2,1,0:T(8,128)(2,1)S(1)}, u32[]{:S(2)}, u32[]{:S(2)}) %collective-permute-start.15) | collective-permute-done | bytes 98336 | tf_op jit(solution)/shard_map/ppermute | solution.py:40
  126.6 5.6 %collective-permute-done.17.refs_3_ = bf16[4,16,768]{2,1,0:T(8,128)(2,1)S(1)} collective-permute-done((bf16[4,16,768]{2,1,0:T(8,128)(2,1)S(1)}, bf16[4,16,768]{2,1,0:T(8,128)(2,1)S(1)}, u32[]{:S(2)}, u32[]{:S(2)}) %collective-permute-start.17) | collective-permute-done | bytes 98336 | tf_op jit(solution)/shard_map/ppermute | solution.py:40
  132.2 2.7 %collective-permute-start.47 = (bf16[4,16,1024]{2,1,0:T(8,128)(2,1)S(1)}, bf16[4,16,1024]{2,1,0:T(8,128)(2,1)S(1)}, u32[]{:S(2)}, u32[]{:S(2)}) collective-permute-start(bf16[4,16,1024]{2,1,0:T(8,128)(2,1)S(1)} %get-tuple-element.169), channel_id=1, source_target_pairs={{0,12},{1,13},{2,14},{3,15},{4,0},{5,1},{6,2},{7,3},{8,4},{9,5},{1... | collective-permute-start | bytes 393224 | tf_op jit(solution)/shard_map/ppermute | solution.py:43
  134.9 4.3 %collective-permute-done.46.refs_2_ = bf16[4,16,1024]{2,1,0:T(8,128)(2,1)S(1)} collective-permute-done((bf16[4,16,1024]{2,1,0:T(8,128)(2,1)S(1)}, bf16[4,16,1024]{2,1,0:T(8,128)(2,1)S(1)}, u32[]{:S(2)}, u32[]{:S(2)}) %collective-permute-start.46) | collective-permute-done | bytes 131104 | tf_op jit(solution)/shard_map/ppermute | solution.py:43
  145.7 4.0 %collective-permute-done.60.refs_14_ = bf16[32,4096]{1,0:T(8,128)(2,1)S(1)} collective-permute-done((bf16[32,4096]{1,0:T(8,128)(2,1)S(1)}, bf16[32,4096]{1,0:T(8,128)(2,1)S(1)}, u32[]{:S(2)}, u32[]{:S(2)}) %collective-permute-start.60) | collective-permute-done | bytes 262176 | tf_op jit(solution)/shard_map/ppermute | solution.py:43
  153.7 4.2 %collective-permute-done.62.refs_16_ = bf16[32,4096]{1,0:T(8,128)(2,1)S(1)} collective-permute-done((bf16[32,4096]{1,0:T(8,128)(2,1)S(1)}, bf16[32,4096]{1,0:T(8,128)(2,1)S(1)}, u32[]{:S(2)}, u32[]{:S(2)}) %collective-permute-start.62) | collective-permute-done | bytes 262176 | tf_op jit(solution)/shard_map/ppermute | solution.py:43
  163.5 3.6 %collective-permute-done.50.refs_7_ = bf16[4,16,1024]{2,1,0:T(8,128)(2,1)S(1)} collective-permute-done((bf16[4,16,1024]{2,1,0:T(8,128)(2,1)S(1)}, bf16[4,16,1024]{2,1,0:T(8,128)(2,1)S(1)}, u32[]{:S(2)}, u32[]{:S(2)}) %collective-permute-start.50) | collective-permute-done | bytes 131104 | tf_op jit(solution)/shard_map/ppermute | solution.py:40
  169.0 2.5 %collective-permute-done.64.got_ref = f32[312,768]{1,0:T(8,128)S(1)} collective-permute-done((f32[312,768]{1,0:T(8,128)S(1)}, f32[312,768]{1,0:T(8,128)S(1)}, u32[]{:S(2)}, u32[]{:S(2)}) %collective-permute-start.64) | collective-permute-done | bytes 958496 | tf_op jit(solution)/shard_map/ppermute | solution.py:48
  183.6 2.5 %collective-permute-start.69 = (f32[16,896]{1,0:T(8,128)S(1)}, f32[16,896]{1,0:T(8,128)S(1)}, u32[]{:S(2)}, u32[]{:S(2)}) collective-permute-start(f32[16,896]{1,0:T(8,128)S(1)} %add_add_fusion.1), channel_id=1, source_target_pairs={{0,4},{1,5},{2,6},{3,7},{4,0},{5,1},{6,2},{7,3},{8,12},{9,13},{10,... | collective-permute-start | bytes 172040 | tf_op jit(solution)/shard_map/ppermute | solution.py:40
  190.1 2.9 %renew.1 = (f32[18,128]{1,0:T(8,128)}, f32[24,2304]{1,0:T(8,128)}, f32[6,128]{1,0:T(8,128)}, f32[24,768]{1,0:T(8,128)}, f32[24,128]{1,0:T(8,128)}, /*index=5*/f3...) custom-call(f32[16,896]{1,0:T(8,128)} %add_add_fusion.stat_ref, ...), custom_call_target="tpu_custom_call" | custom-call | bytes 10485760 | tf_op jit(solution)/shard_map/renew/pallas_call | solution.py:710
  (195 shorter events, 96.7 us)
Async XLA Ops:
  12.8 31.8 %collective-permute-start.20 = (bf16[48,3072]{1,0:T(8,128)(2,1)S(1)}, bf16[48,3072]{1,0:T(8,128)(2,1)S(1)}, u32[]{:S(2)}, u32[]{:S(2)}) collective-permute-start(bf16[48,3072]{1,0:T(8,128)(2,1)S(1)} %maximum_select_fusion.14), channel_id=1, source_target_pairs={{0,4},{1,5},{2,6},{3,7},{4,8},{5,9},{6,10},{7,11},{8,12},{9,13},{1... | collective-permute-start | bytes 884744 | tf_op jit(solution)/shard_map/ppermute | solution.py:43
  14.7 14.0 %collective-permute-start.19 = (bf16[48,3072]{1,0:T(8,128)(2,1)S(1)}, bf16[48,3072]{1,0:T(8,128)(2,1)S(1)}, u32[]{:S(2)}, u32[]{:S(2)}) collective-permute-start(bf16[48,3072]{1,0:T(8,128)(2,1)S(1)} %maximum_select_fusion.14), channel_id=1, source_target_pairs={{0,1},{1,0},{2,3},{3,2},{4,5},{5,4},{6,7},{7,6},{8,9},{9,8},{10,11... | collective-permute-start | bytes 884744 | tf_op jit(solution)/shard_map/ppermute | solution.py:40
  17.3 20.0 %collective-permute-start.31 = (bf16[192,768]{1,0:T(8,128)(2,1)S(1)}, bf16[192,768]{1,0:T(8,128)(2,1)S(1)}, u32[]{:S(2)}, u32[]{:S(2)}) collective-permute-start(bf16[192,768]{1,0:T(8,128)(2,1)S(1)} %maximum_select_fusion.16), channel_id=1, source_target_pairs={{0,1},{1,0},{2,3},{3,2},{4,5},{5,4},{6,7},{7,6},{8,9},{9,8},{10,11... | collective-permute-start | bytes 884744 | tf_op jit(solution)/shard_map/ppermute | solution.py:40
  24.9 21.8 %collective-permute-start.2 = (bf16[48,3200]{1,0:T(8,128)(2,1)S(1)}, bf16[48,3200]{1,0:T(8,128)(2,1)S(1)}, u32[]{:S(2)}, u32[]{:S(2)}) collective-permute-start(bf16[48,3200]{1,0:T(8,128)(2,1)S(1)} %maximum_select_fusion.12), channel_id=1, source_target_pairs={{0,4},{1,5},{2,6},{3,7},{4,8},{5,9},{6,10},{7,11},{8,12},{9,13},{1... | collective-permute-start | bytes 921608 | tf_op jit(solution)/shard_map/ppermute | solution.py:43
  27.1 19.5 %collective-permute-start.1 = (bf16[48,3200]{1,0:T(8,128)(2,1)S(1)}, bf16[48,3200]{1,0:T(8,128)(2,1)S(1)}, u32[]{:S(2)}, u32[]{:S(2)}) collective-permute-start(bf16[48,3200]{1,0:T(8,128)(2,1)S(1)} %maximum_select_fusion.12), channel_id=1, source_target_pairs={{0,2},{1,3},{2,0},{3,1},{4,6},{5,7},{6,4},{7,5},{8,10},{9,11},{10,... | collective-permute-start | bytes 921608 | tf_op jit(solution)/shard_map/ppermute | solution.py:40
  37.3 12.8 %collective-permute-start.34 = (bf16[192,768]{1,0:T(8,128)(2,1)S(1)}, bf16[192,768]{1,0:T(8,128)(2,1)S(1)}, u32[]{:S(2)}, u32[]{:S(2)}) collective-permute-start(bf16[192,768]{1,0:T(8,128)(2,1)S(1)} %maximum_select_fusion.18), channel_id=1, source_target_pairs={{0,1},{1,0},{2,3},{3,2},{4,5},{5,4},{6,7},{7,6},{8,9},{9,8},{10,11... | collective-permute-start | bytes 884744 | tf_op jit(solution)/shard_map/ppermute | solution.py:40
  46.8 13.1 %collective-permute-start.21 = (bf16[48,3072]{1,0:T(8,128)(2,1)S(1)}, bf16[48,3072]{1,0:T(8,128)(2,1)S(1)}, u32[]{:S(2)}, u32[]{:S(2)}) collective-permute-start(bf16[48,3072]{1,0:T(8,128)(2,1)S(1)} %collective-permute-done.20), channel_id=1, source_target_pairs={{0,1},{1,0},{2,3},{3,2},{4,5},{5,4},{6,7},{7,6},{8,9},{9,8},{10,11... | collective-permute-start | bytes 884744 | tf_op jit(solution)/shard_map/ppermute | solution.py:40
  49.8 13.8 %collective-permute-start.4 = (bf16[48,3200]{1,0:T(8,128)(2,1)S(1)}, bf16[48,3200]{1,0:T(8,128)(2,1)S(1)}, u32[]{:S(2)}, u32[]{:S(2)}) collective-permute-start(bf16[48,3200]{1,0:T(8,128)(2,1)S(1)} %collective-permute-done.2), channel_id=1, source_target_pairs={{0,4},{1,5},{2,6},{3,7},{4,8},{5,9},{6,10},{7,11},{8,12},{9,13},{1... | collective-permute-start | bytes 921608 | tf_op jit(solution)/shard_map/ppermute | solution.py:43
  50.1 13.6 %collective-permute-start.3 = (bf16[48,3200]{1,0:T(8,128)(2,1)S(1)}, bf16[48,3200]{1,0:T(8,128)(2,1)S(1)}, u32[]{:S(2)}, u32[]{:S(2)}) collective-permute-start(bf16[48,3200]{1,0:T(8,128)(2,1)S(1)} %collective-permute-done.2), channel_id=1, source_target_pairs={{0,2},{1,3},{2,0},{3,1},{4,6},{5,7},{6,4},{7,5},{8,10},{9,11},{10,... | collective-permute-start | bytes 921608 | tf_op jit(solution)/shard_map/ppermute | solution.py:40
  53.5 20.2 %collective-permute-start.40 = (bf16[192,768]{1,0:T(8,128)(2,1)S(1)}, bf16[192,768]{1,0:T(8,128)(2,1)S(1)}, u32[]{:S(2)}, u32[]{:S(2)}) collective-permute-start(bf16[192,768]{1,0:T(8,128)(2,1)S(1)} %maximum_select_fusion.22), channel_id=1, source_target_pairs={{0,1},{1,0},{2,3},{3,2},{4,5},{5,4},{6,7},{7,6},{8,9},{9,8},{10,11... | collective-permute-start | bytes 884744 | tf_op jit(solution)/shard_map/ppermute | solution.py:40
  57.1 16.8 %collective-permute-start.24 = (bf16[48,3072]{1,0:T(8,128)(2,1)S(1)}, bf16[48,3072]{1,0:T(8,128)(2,1)S(1)}, u32[]{:S(2)}, u32[]{:S(2)}) collective-permute-start(bf16[48,3072]{1,0:T(8,128)(2,1)S(1)} %collective-permute-done.22), channel_id=1, source_target_pairs={{0,4},{1,5},{2,6},{3,7},{4,8},{5,9},{6,10},{7,11},{8,12},{9,13},{1... | collective-permute-start | bytes 884744 | tf_op jit(solution)/shard_map/ppermute | solution.py:43
  59.8 20.1 %collective-permute-start.23 = (bf16[48,3072]{1,0:T(8,128)(2,1)S(1)}, bf16[48,3072]{1,0:T(8,128)(2,1)S(1)}, u32[]{:S(2)}, u32[]{:S(2)}) collective-permute-start(bf16[48,3072]{1,0:T(8,128)(2,1)S(1)} %collective-permute-done.22), channel_id=1, source_target_pairs={{0,1},{1,0},{2,3},{3,2},{4,5},{5,4},{6,7},{7,6},{8,9},{9,8},{10,11... | collective-permute-start | bytes 884744 | tf_op jit(solution)/shard_map/ppermute | solution.py:40
  63.7 15.9 %collective-permute-start.5 = (bf16[48,3200]{1,0:T(8,128)(2,1)S(1)}, bf16[48,3200]{1,0:T(8,128)(2,1)S(1)}, u32[]{:S(2)}, u32[]{:S(2)}) collective-permute-start(bf16[48,3200]{1,0:T(8,128)(2,1)S(1)} %collective-permute-done.4), channel_id=1, source_target_pairs={{0,2},{1,3},{2,0},{3,1},{4,6},{5,7},{6,4},{7,5},{8,10},{9,11},{10,... | collective-permute-start | bytes 921608 | tf_op jit(solution)/shard_map/ppermute | solution.py:40
  96.5 15.1 %collective-permute-start.52 = (bf16[16,3072]{1,0:T(8,128)(2,1)S(1)}, bf16[16,3072]{1,0:T(8,128)(2,1)S(1)}, u32[]{:S(2)}, u32[]{:S(2)}) collective-permute-start(bf16[16,3072]{1,0:T(8,128)(2,1)S(1)} %get-tuple-element.155.du_ref.refs_0_), channel_id=1, source_target_pairs={{0,8},{1,9},{2,10},{3,11},{4,12},{5,13},{6,14},{7,15},{8,0},{9,1},... | collective-permute-start | bytes 294920 | tf_op jit(solution)/shard_map/ppermute | solution.py:43
  96.5 16.4 %collective-permute-start.51 = (bf16[16,3072]{1,0:T(8,128)(2,1)S(1)}, bf16[16,3072]{1,0:T(8,128)(2,1)S(1)}, u32[]{:S(2)}, u32[]{:S(2)}) collective-permute-start(bf16[16,3072]{1,0:T(8,128)(2,1)S(1)} %get-tuple-element.155.du_ref.refs_0_), channel_id=1, source_target_pairs={{0,4},{1,5},{2,6},{3,7},{4,8},{5,9},{6,10},{7,11},{8,12},{9,13},{1... | collective-permute-start | bytes 294920 | tf_op jit(solution)/shard_map/ppermute | solution.py:43
  98.5 14.9 %collective-permute-start.12 = (bf16[4,16,768]{2,1,0:T(8,128)(2,1)S(1)}, bf16[4,16,768]{2,1,0:T(8,128)(2,1)S(1)}, u32[]{:S(2)}, u32[]{:S(2)}) collective-permute-start(bf16[4,16,768]{2,1,0:T(8,128)(2,1)S(1)} %get-tuple-element.129), channel_id=1, source_target_pairs={{0,4},{1,5},{2,6},{3,7},{4,8},{5,9},{6,10},{7,11},{8,12},{9,13},{1... | collective-permute-start | bytes 294920 | tf_op jit(solution)/shard_map/ppermute | solution.py:43
  100.0 13.6 %collective-permute-start.13 = (bf16[4,16,768]{2,1,0:T(8,128)(2,1)S(1)}, bf16[4,16,768]{2,1,0:T(8,128)(2,1)S(1)}, u32[]{:S(2)}, u32[]{:S(2)}) collective-permute-start(bf16[4,16,768]{2,1,0:T(8,128)(2,1)S(1)} %get-tuple-element.130), channel_id=1, source_target_pairs={{0,8},{1,9},{2,10},{3,11},{4,12},{5,13},{6,14},{7,15},{8,0},{9,1},... | collective-permute-start | bytes 294920 | tf_op jit(solution)/shard_map/ppermute | solution.py:43
  102.8 10.9 %collective-permute-start.14 = (bf16[4,16,768]{2,1,0:T(8,128)(2,1)S(1)}, bf16[4,16,768]{2,1,0:T(8,128)(2,1)S(1)}, u32[]{:S(2)}, u32[]{:S(2)}) collective-permute-start(bf16[4,16,768]{2,1,0:T(8,128)(2,1)S(1)} %get-tuple-element.131), channel_id=1, source_target_pairs={{0,12},{1,13},{2,14},{3,15},{4,0},{5,1},{6,2},{7,3},{8,4},{9,5},{1... | collective-permute-start | bytes 294920 | tf_op jit(solution)/shard_map/ppermute | solution.py:43
  112.9 30.1 %collective-permute-start.54 = (bf16[64,3072]{1,0:T(8,128)(2,1)S(1)}, bf16[64,3072]{1,0:T(8,128)(2,1)S(1)}, u32[]{:S(2)}, u32[]{:S(2)}) collective-permute-start(bf16[64,3072]{1,0:T(8,128)(2,1)S(1)} %joined.3.refs_0_), channel_id=1, source_target_pairs={{0,1},{1,0},{2,3},{3,2},{4,5},{5,4},{6,7},{7,6},{8,9},{9,8},{10,11... | collective-permute-start | bytes 1179656 | tf_op jit(solution)/shard_map/ppermute | solution.py:40
  115.9 16.4 %collective-permute-start.45 = (bf16[4,16,1024]{2,1,0:T(8,128)(2,1)S(1)}, bf16[4,16,1024]{2,1,0:T(8,128)(2,1)S(1)}, u32[]{:S(2)}, u32[]{:S(2)}) collective-permute-start(bf16[4,16,1024]{2,1,0:T(8,128)(2,1)S(1)} %get-tuple-element.165), channel_id=1, source_target_pairs={{0,4},{1,5},{2,6},{3,7},{4,8},{5,9},{6,10},{7,11},{8,12},{9,13},{1... | collective-permute-start | bytes 393224 | tf_op jit(solution)/shard_map/ppermute | solution.py:43
  117.7 21.6 %collective-permute-start.58 = (bf16[32,4096]{1,0:T(8,128)(2,1)S(1)}, bf16[32,4096]{1,0:T(8,128)(2,1)S(1)}, u32[]{:S(2)}, u32[]{:S(2)}) collective-permute-start(bf16[32,4096]{1,0:T(8,128)(2,1)S(1)} %joined.5.refs_10_), channel_id=1, source_target_pairs={{0,4},{1,5},{2,6},{3,7},{4,8},{5,9},{6,10},{7,11},{8,12},{9,13},{1... | collective-permute-start | bytes 786440 | tf_op jit(solution)/shard_map/ppermute | solution.py:43
  124.4 14.9 %collective-permute-start.57 = (bf16[32,4096]{1,0:T(8,128)(2,1)S(1)}, bf16[32,4096]{1,0:T(8,128)(2,1)S(1)}, u32[]{:S(2)}, u32[]{:S(2)}) collective-permute-start(bf16[32,4096]{1,0:T(8,128)(2,1)S(1)} %joined.5.refs_10_), channel_id=1, source_target_pairs={{0,1},{1,0},{2,3},{3,2},{4,5},{5,4},{6,7},{7,6},{8,9},{9,8},{10,11... | collective-permute-start | bytes 786440 | tf_op jit(solution)/shard_map/ppermute | solution.py:40
  143.0 24.1 %collective-permute-start.55 = (bf16[128,3072]{1,0:T(8,128)(2,1)S(1)}, bf16[128,3072]{1,0:T(8,128)(2,1)S(1)}, u32[]{:S(2)}, u32[]{:S(2)}) collective-permute-start(bf16[128,3072]{1,0:T(8,128)(2,1)S(1)} %joined.4.refs_8_), channel_id=1, source_target_pairs={{0,2},{1,3},{2,0},{3,1},{4,6},{5,7},{6,4},{7,5},{8,10},{9,11},{10,... | collective-permute-start | bytes 2359304 | tf_op jit(solution)/shard_map/ppermute | solution.py:40
  151.7 15.5 %collective-permute-start.61 = (bf16[32,4096]{1,0:T(8,128)(2,1)S(1)}, bf16[32,4096]{1,0:T(8,128)(2,1)S(1)}, u32[]{:S(2)}, u32[]{:S(2)}) collective-permute-start(bf16[32,4096]{1,0:T(8,128)(2,1)S(1)} %collective-permute-done.60.refs_14_), channel_id=1, source_target_pairs={{0,1},{1,0},{2,3},{3,2},{4,5},{5,4},{6,7},{7,6},{8,9},{9,8},{10,11... | collective-permute-start | bytes 786440 | tf_op jit(solution)/shard_map/ppermute | solution.py:40
  (66 other events, 411.4 us)

commit v4 on v3

--- a/solution.py
+++ b/solution.py
@@ -133,7 +133,7 @@
 def gather_last(moves, first, late, du, low):
     held = joined([du] + [moves.turn(du, k) for k in range(1, moves.depth)])
     ring = [joined([low, moves.flip(low, 2)])]
-    over_x = moves.flip(held, 1)
+    over_x = moves.flip(after(held, [low]), 1)
     got = sent_along(moves, [after(v, first[1:]) for v in late])
     ring.append(moves.turn(ring[0], 1))
     first = to_places(moves, first)

time: 193 us -> 193 us (level)
  no operation moved by 1% of the time
where the time goes in v4:
time: 193 us
  waiting for transfers between devices  88.9 us (46%)
  starting transfers between devices  72.3 us (37%)
  Pallas kernels  24.4 us (13%)
  other arithmetic  4.83 us (3%)
  between operations  2.65 us (1%)
    ppermute x37, waiting for transfers between devices, flip(): lax.ppermute(value, 'fsdp', [(i, i ^ mask) for i in range(self.fsdp)])  48.4 us
    ppermute x37, starting transfers between devices, flip(): lax.ppermute(value, 'fsdp', [(i, i ^ mask) for i in range(self.fsdp)])  46.3 us
    ppermute x21, waiting for transfers between devices, turn(): lax.ppermute(value, 'fsdp', [(i, (i + 4 * step) % self.fsdp) for i in ran...  32.3 us
    pallas_call x10, Pallas kernels, call(): pl.pallas_call(kernel, cost_estimate=pl.CostEstimate(flops=0, bytes_acces...  24.3 us
    ppermute x21, starting transfers between devices, turn(): lax.ppermute(value, 'fsdp', [(i, (i + 4 * step) % self.fsdp) for i in ran...  23.6 us
    ppermute x14, waiting for transfers between devices, swap(): return lax.ppermute(value, 'dp', [(0, 1), (1, 0)])  8.2 us
    select_n x23, other arithmetic, pair(): jnp.where(bit == 0, jnp.concatenate([own, other], 1), jnp.concatenate([ot...  4.17 us
  transfers between devices with their start and end apart: 72, of which 37 were waited for; matrix products, arithmetic and copies ran while one was open for 2% of the time, Pallas kernels for 6%

profile of v4, /device:TPU:0, one launch (start us, length us, event | category | flops | bytes accessed | tf_op | source)
XLA Modules:
  0.0 193.1 jit_solution(3904217474358821853)
XLA Ops:
  2.0 2.2 %wire.1 = (bf16[24,3200]{1,0:T(8,128)(2,1)}, bf16[24,3072]{1,0:T(8,128)(2,1)}, bf16[96,768]{1,0:T(8,128)(2,1)}, bf16[16,128]{1,0:T(8,128)(2,1)}, f32[16,128]{1,0...) custom-call(f32[24,2304]{1,0:T(8,128)} %refs_3_.1, f32[24,768]{1,0:T(8,128)} %refs_7_.1, ...), custom_call_target="tpu_custom_call" | custom-call | bytes 6291456 | tf_op jit(solution)/shard_map/wire/pallas_call | solution.py:710
  4.2 3.0 %collective-permute-start.18 = (bf16[24,3072]{1,0:T(8,128)(2,1)}, bf16[24,3072]{1,0:T(8,128)(2,1)S(1)}, u32[]{:S(2)}, u32[]{:S(2)}) collective-permute-start(bf16[24,3072]{1,0:T(8,128)(2,1)} %get-tuple-element.145), channel_id=1, source_target_pairs={{0,2},{1,3},{2,0},{3,1},{4,6},{5,7},{6,4},{7,5},{8,10},{9,11},{10,... | collective-permute-start | bytes 442376 | tf_op jit(solution)/shard_map/ppermute | solution.py:40
  21.9 3.1 %collective-permute-done.33 = bf16[96,768]{1,0:T(8,128)(2,1)S(1)} collective-permute-done((bf16[96,768]{1,0:T(8,128)(2,1)S(1)}, bf16[96,768]{1,0:T(8,128)(2,1)S(1)}, u32[]{:S(2)}, u32[]{:S(2)}) %collective-permute-start.33) | collective-permute-done | bytes 147488 | tf_op jit(solution)/shard_map/ppermute | solution.py:40
  29.4 6.8 %collective-permute-done.36 = bf16[96,768]{1,0:T(8,128)(2,1)S(1)} collective-permute-done((bf16[96,768]{1,0:T(8,128)(2,1)S(1)}, bf16[96,768]{1,0:T(8,128)(2,1)S(1)}, u32[]{:S(2)}, u32[]{:S(2)}) %collective-permute-start.36) | collective-permute-done | bytes 147488 | tf_op jit(solution)/shard_map/ppermute | solution.py:40
  38.6 4.5 %collective-permute-done.38 = bf16[96,768]{1,0:T(8,128)(2,1)S(1)} collective-permute-done((bf16[96,768]{1,0:T(8,128)(2,1)S(1)}, bf16[96,768]{1,0:T(8,128)(2,1)S(1)}, u32[]{:S(2)}, u32[]{:S(2)}) %collective-permute-start.38) | collective-permute-done | bytes 147488 | tf_op jit(solution)/shard_map/ppermute | solution.py:43
  47.6 2.2 %collective-permute-done.39 = bf16[96,768]{1,0:T(8,128)(2,1)S(1)} collective-permute-done((bf16[96,768]{1,0:T(8,128)(2,1)S(1)}, bf16[96,768]{1,0:T(8,128)(2,1)S(1)}, u32[]{:S(2)}, u32[]{:S(2)}) %collective-permute-start.39) | collective-permute-done | bytes 147488 | tf_op jit(solution)/shard_map/ppermute | solution.py:40
  54.7 2.4 %collective-permute-done.22 = bf16[48,3072]{1,0:T(8,128)(2,1)S(1)} collective-permute-done((bf16[48,3072]{1,0:T(8,128)(2,1)S(1)}, bf16[48,3072]{1,0:T(8,128)(2,1)S(1)}, u32[]{:S(2)}, u32[]{:S(2)}) %collective-permute-start.22) | collective-permute-done | bytes 294944 | tf_op jit(solution)/shard_map/ppermute | solution.py:43
  57.3 2.5 %collective-permute-done.21 = bf16[48,3072]{1,0:T(8,128)(2,1)S(1)} collective-permute-done((bf16[48,3072]{1,0:T(8,128)(2,1)S(1)}, bf16[48,3072]{1,0:T(8,128)(2,1)S(1)}, u32[]{:S(2)}, u32[]{:S(2)}) %collective-permute-start.21) | collective-permute-done | bytes 294944 | tf_op jit(solution)/shard_map/ppermute | solution.py:40
  61.0 2.6 %collective-permute-done.4 = bf16[48,3200]{1,0:T(8,128)(2,1)S(1)} collective-permute-done((bf16[48,3200]{1,0:T(8,128)(2,1)S(1)}, bf16[48,3200]{1,0:T(8,128)(2,1)S(1)}, u32[]{:S(2)}, u32[]{:S(2)}) %collective-permute-start.4) | collective-permute-done | bytes 307232 | tf_op jit(solution)/shard_map/ppermute | solution.py:43
  65.1 7.1 %collective-permute-done.6 = bf16[48,3200]{1,0:T(8,128)(2,1)S(1)} collective-permute-done((bf16[48,3200]{1,0:T(8,128)(2,1)S(1)}, bf16[48,3200]{1,0:T(8,128)(2,1)S(1)}, u32[]{:S(2)}, u32[]{:S(2)}) %collective-permute-start.6) | collective-permute-done | bytes 307232 | tf_op jit(solution)/shard_map/ppermute | solution.py:43
  74.4 4.7 %collective-permute-done.7 = bf16[48,3200]{1,0:T(8,128)(2,1)S(1)} collective-permute-done((bf16[48,3200]{1,0:T(8,128)(2,1)S(1)}, bf16[48,3200]{1,0:T(8,128)(2,1)S(1)}, u32[]{:S(2)}, u32[]{:S(2)}) %collective-permute-start.7) | collective-permute-done | bytes 307232 | tf_op jit(solution)/shard_map/ppermute | solution.py:40
  88.3 3.4 %attend.1 = (bf16[16,896]{1,0:T(8,128)(2,1)S(1)}, bf16[192,768]{1,0:T(8,128)(2,1)S(1)}, f32[192,864]{1,0:T(8,128)S(1)}, bf16[192,768]{1,0:T(8,128)(2,1)}, bf16[1...) custom-call(bf16[864,768]{1,0:T(8,128)(2,1)S(1)} %get-tuple-element., ...), custom_call_target="tpu_custom_call" | custom-call | bytes 11534336 | tf_op jit(solution)/shard_map/attend/pallas_call | solution.py:710
  91.7 4.8 %feed.1 = (bf16[16,16,256]{2,1,0:T(8,128)(2,1)S(1)}, bf16[16,3072]{1,0:T(8,128)(2,1)S(1)}, bf16[16,896]{1,0:T(8,128)(2,1)S(1)}, bf16[16,768]{1,0:T(8,128)(2,1)S(...) custom-call(f32[16,768]{1,0:T(8,128)S(1)} %get-tuple-element.140.y_ref, ...), custom_call_target="tpu_custom_call" | custom-call | bytes 17825792 | tf_op jit(solution)/shard_map/feed/pallas_call | solution.py:710
  104.4 5.6 %back.1 = (bf16[16,4096]{1,0:T(8,128)(2,1)S(1)}, bf16[4,16,1024]{2,1,0:T(8,128)(2,1)S(1)}, bf16[4,16,1024]{2,1,0:T(8,128)(2,1)S(1)}, bf16[4,16,1024]{2,1,0:T(8,128)(2,1)S(1)}, bf16[4,16,1024]{2,1,0:T(8,128)(2,1)S(1)}) custom-call(bf16[864,768]{1,0:T(8,128)(2,1)S(1)} %get-tuple-element.124.a_ref, f32[864,768]{1,0:T(8,128)S(1)} %get-tuple-element.137.unit_ref, ...), custom_call_target="tpu_custom_call" | custom-call | bytes 19922944 | tf_op jit(solution)/shard_map/back/pallas_call | solution.py:710
  118.0 6.4 %collective-permute-done.15.refs_1_ = bf16[4,16,768]{2,1,0:T(8,128)(2,1)S(1)} collective-permute-done((bf16[4,16,768]{2,1,0:T(8,128)(2,1)S(1)}, bf16[4,16,768]{2,1,0:T(8,128)(2,1)S(1)}, u32[]{:S(2)}, u32[]{:S(2)}) %collective-permute-start.15) | collective-permute-done | bytes 98336 | tf_op jit(solution)/shard_map/ppermute | solution.py:40
  126.6 5.6 %collective-permute-done.17.refs_3_ = bf16[4,16,768]{2,1,0:T(8,128)(2,1)S(1)} collective-permute-done((bf16[4,16,768]{2,1,0:T(8,128)(2,1)S(1)}, bf16[4,16,768]{2,1,0:T(8,128)(2,1)S(1)}, u32[]{:S(2)}, u32[]{:S(2)}) %collective-permute-start.17) | collective-permute-done | bytes 98336 | tf_op jit(solution)/shard_map/ppermute | solution.py:40
  132.2 2.7 %collective-permute-start.47 = (bf16[4,16,1024]{2,1,0:T(8,128)(2,1)S(1)}, bf16[4,16,1024]{2,1,0:T(8,128)(2,1)S(1)}, u32[]{:S(2)}, u32[]{:S(2)}) collective-permute-start(bf16[4,16,1024]{2,1,0:T(8,128)(2,1)S(1)} %get-tuple-element.170), channel_id=1, source_target_pairs={{0,12},{1,13},{2,14},{3,15},{4,0},{5,1},{6,2},{7,3},{8,4},{9,5},{1... | collective-permute-start | bytes 393224 | tf_op jit(solution)/shard_map/ppermute | solution.py:43
  134.9 4.3 %collective-permute-done.46.refs_2_ = bf16[4,16,1024]{2,1,0:T(8,128)(2,1)S(1)} collective-permute-done((bf16[4,16,1024]{2,1,0:T(8,128)(2,1)S(1)}, bf16[4,16,1024]{2,1,0:T(8,128)(2,1)S(1)}, u32[]{:S(2)}, u32[]{:S(2)}) %collective-permute-start.46) | collective-permute-done | bytes 131104 | tf_op jit(solution)/shard_map/ppermute | solution.py:43
  145.7 4.0 %collective-permute-done.60.refs_14_ = bf16[32,4096]{1,0:T(8,128)(2,1)S(1)} collective-permute-done((bf16[32,4096]{1,0:T(8,128)(2,1)S(1)}, bf16[32,4096]{1,0:T(8,128)(2,1)S(1)}, u32[]{:S(2)}, u32[]{:S(2)}) %collective-permute-start.60) | collective-permute-done | bytes 262176 | tf_op jit(solution)/shard_map/ppermute | solution.py:43
  153.7 4.2 %collective-permute-done.62.refs_16_ = bf16[32,4096]{1,0:T(8,128)(2,1)S(1)} collective-permute-done((bf16[32,4096]{1,0:T(8,128)(2,1)S(1)}, bf16[32,4096]{1,0:T(8,128)(2,1)S(1)}, u32[]{:S(2)}, u32[]{:S(2)}) %collective-permute-start.62) | collective-permute-done | bytes 262176 | tf_op jit(solution)/shard_map/ppermute | solution.py:43
  163.5 3.6 %collective-permute-done.50.refs_7_ = bf16[4,16,1024]{2,1,0:T(8,128)(2,1)S(1)} collective-permute-done((bf16[4,16,1024]{2,1,0:T(8,128)(2,1)S(1)}, bf16[4,16,1024]{2,1,0:T(8,128)(2,1)S(1)}, u32[]{:S(2)}, u32[]{:S(2)}) %collective-permute-start.50) | collective-permute-done | bytes 131104 | tf_op jit(solution)/shard_map/ppermute | solution.py:40
  169.0 2.5 %collective-permute-done.64.got_ref = f32[312,768]{1,0:T(8,128)S(1)} collective-permute-done((f32[312,768]{1,0:T(8,128)S(1)}, f32[312,768]{1,0:T(8,128)S(1)}, u32[]{:S(2)}, u32[]{:S(2)}) %collective-permute-start.64) | collective-permute-done | bytes 958496 | tf_op jit(solution)/shard_map/ppermute | solution.py:48
  183.6 2.5 %collective-permute-start.69 = (f32[16,896]{1,0:T(8,128)S(1)}, f32[16,896]{1,0:T(8,128)S(1)}, u32[]{:S(2)}, u32[]{:S(2)}) collective-permute-start(f32[16,896]{1,0:T(8,128)S(1)} %add_add_fusion.1), channel_id=1, source_target_pairs={{0,4},{1,5},{2,6},{3,7},{4,0},{5,1},{6,2},{7,3},{8,12},{9,13},{10,... | collective-permute-start | bytes 172040 | tf_op jit(solution)/shard_map/ppermute | solution.py:40
  190.1 2.9 %renew.1 = (f32[18,128]{1,0:T(8,128)}, f32[24,2304]{1,0:T(8,128)}, f32[6,128]{1,0:T(8,128)}, f32[24,768]{1,0:T(8,128)}, f32[24,128]{1,0:T(8,128)}, /*index=5*/f3...) custom-call(f32[16,896]{1,0:T(8,128)} %add_add_fusion.stat_ref, ...), custom_call_target="tpu_custom_call" | custom-call | bytes 10485760 | tf_op jit(solution)/shard_map/renew/pallas_call | solution.py:710
  (195 shorter events, 96.7 us)
Async XLA Ops:
  12.8 31.8 %collective-permute-start.20 = (bf16[48,3072]{1,0:T(8,128)(2,1)S(1)}, bf16[48,3072]{1,0:T(8,128)(2,1)S(1)}, u32[]{:S(2)}, u32[]{:S(2)}) collective-permute-start(bf16[48,3072]{1,0:T(8,128)(2,1)S(1)} %maximum_select_fusion.14), channel_id=1, source_target_pairs={{0,4},{1,5},{2,6},{3,7},{4,8},{5,9},{6,10},{7,11},{8,12},{9,13},{1... | collective-permute-start | bytes 884744 | tf_op jit(solution)/shard_map/ppermute | solution.py:43
  14.7 14.0 %collective-permute-start.19 = (bf16[48,3072]{1,0:T(8,128)(2,1)S(1)}, bf16[48,3072]{1,0:T(8,128)(2,1)S(1)}, u32[]{:S(2)}, u32[]{:S(2)}) collective-permute-start(bf16[48,3072]{1,0:T(8,128)(2,1)S(1)} %maximum_select_fusion.14), channel_id=1, source_target_pairs={{0,1},{1,0},{2,3},{3,2},{4,5},{5,4},{6,7},{7,6},{8,9},{9,8},{10,11... | collective-permute-start | bytes 884744 | tf_op jit(solution)/shard_map/ppermute | solution.py:40
  17.3 20.0 %collective-permute-start.31 = (bf16[192,768]{1,0:T(8,128)(2,1)S(1)}, bf16[192,768]{1,0:T(8,128)(2,1)S(1)}, u32[]{:S(2)}, u32[]{:S(2)}) collective-permute-start(bf16[192,768]{1,0:T(8,128)(2,1)S(1)} %maximum_select_fusion.16), channel_id=1, source_target_pairs={{0,1},{1,0},{2,3},{3,2},{4,5},{5,4},{6,7},{7,6},{8,9},{9,8},{10,11... | collective-permute-start | bytes 884744 | tf_op jit(solution)/shard_map/ppermute | solution.py:40
  24.9 21.8 %collective-permute-start.2 = (bf16[48,3200]{1,0:T(8,128)(2,1)S(1)}, bf16[48,3200]{1,0:T(8,128)(2,1)S(1)}, u32[]{:S(2)}, u32[]{:S(2)}) collective-permute-start(bf16[48,3200]{1,0:T(8,128)(2,1)S(1)} %maximum_select_fusion.12), channel_id=1, source_target_pairs={{0,4},{1,5},{2,6},{3,7},{4,8},{5,9},{6,10},{7,11},{8,12},{9,13},{1... | collective-permute-start | bytes 921608 | tf_op jit(solution)/shard_map/ppermute | solution.py:43
  27.1 19.5 %collective-permute-start.1 = (bf16[48,3200]{1,0:T(8,128)(2,1)S(1)}, bf16[48,3200]{1,0:T(8,128)(2,1)S(1)}, u32[]{:S(2)}, u32[]{:S(2)}) collective-permute-start(bf16[48,3200]{1,0:T(8,128)(2,1)S(1)} %maximum_select_fusion.12), channel_id=1, source_target_pairs={{0,2},{1,3},{2,0},{3,1},{4,6},{5,7},{6,4},{7,5},{8,10},{9,11},{10,... | collective-permute-start | bytes 921608 | tf_op jit(solution)/shard_map/ppermute | solution.py:40
  37.3 12.8 %collective-permute-start.34 = (bf16[192,768]{1,0:T(8,128)(2,1)S(1)}, bf16[192,768]{1,0:T(8,128)(2,1)S(1)}, u32[]{:S(2)}, u32[]{:S(2)}) collective-permute-start(bf16[192,768]{1,0:T(8,128)(2,1)S(1)} %maximum_select_fusion.18), channel_id=1, source_target_pairs={{0,1},{1,0},{2,3},{3,2},{4,5},{5,4},{6,7},{7,6},{8,9},{9,8},{10,11... | collective-permute-start | bytes 884744 | tf_op jit(solution)/shard_map/ppermute | solution.py:40
  46.8 13.1 %collective-permute-start.21 = (bf16[48,3072]{1,0:T(8,128)(2,1)S(1)}, bf16[48,3072]{1,0:T(8,128)(2,1)S(1)}, u32[]{:S(2)}, u32[]{:S(2)}) collective-permute-start(bf16[48,3072]{1,0:T(8,128)(2,1)S(1)} %collective-permute-done.20), channel_id=1, source_target_pairs={{0,1},{1,0},{2,3},{3,2},{4,5},{5,4},{6,7},{7,6},{8,9},{9,8},{10,11... | collective-permute-start | bytes 884744 | tf_op jit(solution)/shard_map/ppermute | solution.py:40
  49.8 13.8 %collective-permute-start.4 = (bf16[48,3200]{1,0:T(8,128)(2,1)S(1)}, bf16[48,3200]{1,0:T(8,128)(2,1)S(1)}, u32[]{:S(2)}, u32[]{:S(2)}) collective-permute-start(bf16[48,3200]{1,0:T(8,128)(2,1)S(1)} %collective-permute-done.2), channel_id=1, source_target_pairs={{0,4},{1,5},{2,6},{3,7},{4,8},{5,9},{6,10},{7,11},{8,12},{9,13},{1... | collective-permute-start | bytes 921608 | tf_op jit(solution)/shard_map/ppermute | solution.py:43
  50.1 13.6 %collective-permute-start.3 = (bf16[48,3200]{1,0:T(8,128)(2,1)S(1)}, bf16[48,3200]{1,0:T(8,128)(2,1)S(1)}, u32[]{:S(2)}, u32[]{:S(2)}) collective-permute-start(bf16[48,3200]{1,0:T(8,128)(2,1)S(1)} %collective-permute-done.2), channel_id=1, source_target_pairs={{0,2},{1,3},{2,0},{3,1},{4,6},{5,7},{6,4},{7,5},{8,10},{9,11},{10,... | collective-permute-start | bytes 921608 | tf_op jit(solution)/shard_map/ppermute | solution.py:40
  53.5 20.2 %collective-permute-start.40 = (bf16[192,768]{1,0:T(8,128)(2,1)S(1)}, bf16[192,768]{1,0:T(8,128)(2,1)S(1)}, u32[]{:S(2)}, u32[]{:S(2)}) collective-permute-start(bf16[192,768]{1,0:T(8,128)(2,1)S(1)} %maximum_select_fusion.22), channel_id=1, source_target_pairs={{0,1},{1,0},{2,3},{3,2},{4,5},{5,4},{6,7},{7,6},{8,9},{9,8},{10,11... | collective-permute-start | bytes 884744 | tf_op jit(solution)/shard_map/ppermute | solution.py:40
  57.1 16.8 %collective-permute-start.24 = (bf16[48,3072]{1,0:T(8,128)(2,1)S(1)}, bf16[48,3072]{1,0:T(8,128)(2,1)S(1)}, u32[]{:S(2)}, u32[]{:S(2)}) collective-permute-start(bf16[48,3072]{1,0:T(8,128)(2,1)S(1)} %collective-permute-done.22), channel_id=1, source_target_pairs={{0,4},{1,5},{2,6},{3,7},{4,8},{5,9},{6,10},{7,11},{8,12},{9,13},{1... | collective-permute-start | bytes 884744 | tf_op jit(solution)/shard_map/ppermute | solution.py:43
  59.8 20.1 %collective-permute-start.23 = (bf16[48,3072]{1,0:T(8,128)(2,1)S(1)}, bf16[48,3072]{1,0:T(8,128)(2,1)S(1)}, u32[]{:S(2)}, u32[]{:S(2)}) collective-permute-start(bf16[48,3072]{1,0:T(8,128)(2,1)S(1)} %collective-permute-done.22), channel_id=1, source_target_pairs={{0,1},{1,0},{2,3},{3,2},{4,5},{5,4},{6,7},{7,6},{8,9},{9,8},{10,11... | collective-permute-start | bytes 884744 | tf_op jit(solution)/shard_map/ppermute | solution.py:40
  63.7 15.9 %collective-permute-start.5 = (bf16[48,3200]{1,0:T(8,128)(2,1)S(1)}, bf16[48,3200]{1,0:T(8,128)(2,1)S(1)}, u32[]{:S(2)}, u32[]{:S(2)}) collective-permute-start(bf16[48,3200]{1,0:T(8,128)(2,1)S(1)} %collective-permute-done.4), channel_id=1, source_target_pairs={{0,2},{1,3},{2,0},{3,1},{4,6},{5,7},{6,4},{7,5},{8,10},{9,11},{10,... | collective-permute-start | bytes 921608 | tf_op jit(solution)/shard_map/ppermute | solution.py:40
  96.5 15.1 %collective-permute-start.52 = (bf16[16,3072]{1,0:T(8,128)(2,1)S(1)}, bf16[16,3072]{1,0:T(8,128)(2,1)S(1)}, u32[]{:S(2)}, u32[]{:S(2)}) collective-permute-start(bf16[16,3072]{1,0:T(8,128)(2,1)S(1)} %get-tuple-element.156.du_ref.refs_0_), channel_id=1, source_target_pairs={{0,8},{1,9},{2,10},{3,11},{4,12},{5,13},{6,14},{7,15},{8,0},{9,1},... | collective-permute-start | bytes 294920 | tf_op jit(solution)/shard_map/ppermute | solution.py:43
  96.5 16.4 %collective-permute-start.51 = (bf16[16,3072]{1,0:T(8,128)(2,1)S(1)}, bf16[16,3072]{1,0:T(8,128)(2,1)S(1)}, u32[]{:S(2)}, u32[]{:S(2)}) collective-permute-start(bf16[16,3072]{1,0:T(8,128)(2,1)S(1)} %get-tuple-element.156.du_ref.refs_0_), channel_id=1, source_target_pairs={{0,4},{1,5},{2,6},{3,7},{4,8},{5,9},{6,10},{7,11},{8,12},{9,13},{1... | collective-permute-start | bytes 294920 | tf_op jit(solution)/shard_map/ppermute | solution.py:43
  98.5 14.9 %collective-permute-start.12 = (bf16[4,16,768]{2,1,0:T(8,128)(2,1)S(1)}, bf16[4,16,768]{2,1,0:T(8,128)(2,1)S(1)}, u32[]{:S(2)}, u32[]{:S(2)}) collective-permute-start(bf16[4,16,768]{2,1,0:T(8,128)(2,1)S(1)} %get-tuple-element.130), channel_id=1, source_target_pairs={{0,4},{1,5},{2,6},{3,7},{4,8},{5,9},{6,10},{7,11},{8,12},{9,13},{1... | collective-permute-start | bytes 294920 | tf_op jit(solution)/shard_map/ppermute | solution.py:43
  100.0 13.6 %collective-permute-start.13 = (bf16[4,16,768]{2,1,0:T(8,128)(2,1)S(1)}, bf16[4,16,768]{2,1,0:T(8,128)(2,1)S(1)}, u32[]{:S(2)}, u32[]{:S(2)}) collective-permute-start(bf16[4,16,768]{2,1,0:T(8,128)(2,1)S(1)} %get-tuple-element.131), channel_id=1, source_target_pairs={{0,8},{1,9},{2,10},{3,11},{4,12},{5,13},{6,14},{7,15},{8,0},{9,1},... | collective-permute-start | bytes 294920 | tf_op jit(solution)/shard_map/ppermute | solution.py:43
  102.8 10.9 %collective-permute-start.14 = (bf16[4,16,768]{2,1,0:T(8,128)(2,1)S(1)}, bf16[4,16,768]{2,1,0:T(8,128)(2,1)S(1)}, u32[]{:S(2)}, u32[]{:S(2)}) collective-permute-start(bf16[4,16,768]{2,1,0:T(8,128)(2,1)S(1)} %get-tuple-element.132), channel_id=1, source_target_pairs={{0,12},{1,13},{2,14},{3,15},{4,0},{5,1},{6,2},{7,3},{8,4},{9,5},{1... | collective-permute-start | bytes 294920 | tf_op jit(solution)/shard_map/ppermute | solution.py:43
  112.9 30.1 %collective-permute-start.54 = (bf16[64,3072]{1,0:T(8,128)(2,1)S(1)}, bf16[64,3072]{1,0:T(8,128)(2,1)S(1)}, u32[]{:S(2)}, u32[]{:S(2)}) collective-permute-start(bf16[64,3072]{1,0:T(8,128)(2,1)S(1)} %joined.3.refs_0_), channel_id=1, source_target_pairs={{0,1},{1,0},{2,3},{3,2},{4,5},{5,4},{6,7},{7,6},{8,9},{9,8},{10,11... | collective-permute-start | bytes 1179656 | tf_op jit(solution)/shard_map/ppermute | solution.py:40
  115.9 16.4 %collective-permute-start.45 = (bf16[4,16,1024]{2,1,0:T(8,128)(2,1)S(1)}, bf16[4,16,1024]{2,1,0:T(8,128)(2,1)S(1)}, u32[]{:S(2)}, u32[]{:S(2)}) collective-permute-start(bf16[4,16,1024]{2,1,0:T(8,128)(2,1)S(1)} %get-tuple-element.166), channel_id=1, source_target_pairs={{0,4},{1,5},{2,6},{3,7},{4,8},{5,9},{6,10},{7,11},{8,12},{9,13},{1... | collective-permute-start | bytes 393224 | tf_op jit(solution)/shard_map/ppermute | solution.py:43
  117.7 21.6 %collective-permute-start.58 = (bf16[32,4096]{1,0:T(8,128)(2,1)S(1)}, bf16[32,4096]{1,0:T(8,128)(2,1)S(1)}, u32[]{:S(2)}, u32[]{:S(2)}) collective-permute-start(bf16[32,4096]{1,0:T(8,128)(2,1)S(1)} %joined.5.refs_10_), channel_id=1, source_target_pairs={{0,4},{1,5},{2,6},{3,7},{4,8},{5,9},{6,10},{7,11},{8,12},{9,13},{1... | collective-permute-start | bytes 786440 | tf_op jit(solution)/shard_map/ppermute | solution.py:43
  124.4 14.9 %collective-permute-start.57 = (bf16[32,4096]{1,0:T(8,128)(2,1)S(1)}, bf16[32,4096]{1,0:T(8,128)(2,1)S(1)}, u32[]{:S(2)}, u32[]{:S(2)}) collective-permute-start(bf16[32,4096]{1,0:T(8,128)(2,1)S(1)} %joined.5.refs_10_), channel_id=1, source_target_pairs={{0,1},{1,0},{2,3},{3,2},{4,5},{5,4},{6,7},{7,6},{8,9},{9,8},{10,11... | collective-permute-start | bytes 786440 | tf_op jit(solution)/shard_map/ppermute | solution.py:40
  143.0 24.1 %collective-permute-start.55 = (bf16[128,3072]{1,0:T(8,128)(2,1)S(1)}, bf16[128,3072]{1,0:T(8,128)(2,1)S(1)}, u32[]{:S(2)}, u32[]{:S(2)}) collective-permute-start(bf16[128,3072]{1,0:T(8,128)(2,1)S(1)} %joined.4.refs_8_), channel_id=1, source_target_pairs={{0,2},{1,3},{2,0},{3,1},{4,6},{5,7},{6,4},{7,5},{8,10},{9,11},{10,... | collective-permute-start | bytes 2359304 | tf_op jit(solution)/shard_map/ppermute | solution.py:40
  151.7 15.5 %collective-permute-start.61 = (bf16[32,4096]{1,0:T(8,128)(2,1)S(1)}, bf16[32,4096]{1,0:T(8,128)(2,1)S(1)}, u32[]{:S(2)}, u32[]{:S(2)}) collective-permute-start(bf16[32,4096]{1,0:T(8,128)(2,1)S(1)} %collective-permute-done.60.refs_14_), channel_id=1, source_target_pairs={{0,1},{1,0},{2,3},{3,2},{4,5},{5,4},{6,7},{7,6},{8,9},{9,8},{10,11... | collective-permute-start | bytes 786440 | tf_op jit(solution)/shard_map/ppermute | solution.py:40
  (66 other events, 411.4 us)
